TPU v7x, 32 devices: a whole 2x2x4 slice. The times are simulated.
32 devices in a mesh: section: 2 (over x), shard: 4 (over z), seq: 4 (over y, core).
Axes of the slice: x: 2, y: 2, z: 4, core: 2. Of those that a mesh axis runs over, the one named last changes fastest.
Arguments:
- inputs: bfloat16 [2, 1024, 2048], P(None, ('shard', 'seq')), may hold values from -6 to 6
- cotangent: bfloat16 [2, 1024, 2048], P(None, ('shard', 'seq')), may hold values from -6 to 6
- positions: int32 [2, 1024], replicated, may hold values from 0 to 1023, as said below
- gain_attn: bfloat16 [2, 2048], P('section', ('shard', 'seq')), may hold values from 0.5 to 1.5
- w_query: bfloat16 [2, 2048, 2048], P('section', ('shard', 'seq')), may hold values from -0.125 to 0.125
- w_key: bfloat16 [2, 256, 2048], P('section', ('shard', 'seq')), may hold values from -0.125 to 0.125
- w_value: bfloat16 [2, 256, 2048], P('section', ('shard', 'seq')), may hold values from -0.125 to 0.125
- w_out: bfloat16 [2, 2048, 2048], P('section', ('shard', 'seq')), may hold values from -1.75 to 1.75
- gain_ffn: bfloat16 [2, 2048], P('section', ('shard', 'seq')), may hold values from 0.5 to 1.5
- w_gate: bfloat16 [2, 5632, 2048], P('section', ('shard', 'seq')), may hold values from -0.125 to 0.125
- w_up: bfloat16 [2, 5632, 2048], P('section', ('shard', 'seq')), may hold values from -0.125 to 0.125
- w_down: bfloat16 [2, 5632, 2048], P('section', ('shard', 'seq')), may hold values from -0.078125 to 0.078125
Outputs:
- outputs: bfloat16 [2, 2, 1024, 2048], P('section', None, ('shard', 'seq'))
- input_grads: bfloat16 [2, 2, 1024, 2048], P('section', None, ('shard', 'seq'))
- grad_gain_attn: float32 [2, 2048], P('section', ('shard', 'seq'))
- grad_w_query: float32 [2, 2048, 2048], P('section', ('shard', 'seq'))
- grad_w_key: float32 [2, 256, 2048], P('section', ('shard', 'seq'))
- grad_w_value: float32 [2, 256, 2048], P('section', ('shard', 'seq'))
- grad_w_out: float32 [2, 2048, 2048], P('section', ('shard', 'seq'))
- grad_gain_ffn: float32 [2, 2048], P('section', ('shard', 'seq'))
- grad_w_gate: float32 [2, 5632, 2048], P('section', ('shard', 'seq'))
- grad_w_up: float32 [2, 5632, 2048], P('section', ('shard', 'seq'))
- grad_w_down: float32 [2, 5632, 2048], P('section', ('shard', 'seq'))
Inputs may be any that keep to these rules, and one draw needn't show every extreme that they name: Each row is a permutation of the positions of a sequence made of blocks of 128 consecutive positions in rising order; the order of the blocks is drawn.
All inputs are finite; a program needn't handle non-finite values.
Results may differ from a plain program's by a relative error of at most 0.03.
Values may be sent and summed in bfloat16 or wider, within the bound.
A program may use at most 384 MiB of HBM per device.

v0:
```python
import math

import jax
import jax.numpy as jnp
from jax import lax
from jax.sharding import PartitionSpec as P

HEADS = 32
KV_HEADS = 4
HEAD_DIM = 64


EPSILON = 1e-05
THETA_BASE = 10000.0
NEG_LARGE = -1e30


def shifted(value, axis, by):
    count = lax.axis_size(axis)
    pairs = [(i, i + by) for i in range(count) if 0 <= i + by < count]
    return lax.ppermute(value, axis, pairs)


def times_trans(left, right):
    return lax.dot_general(
        left, right, (((1,), (1,)), ((), ())), preferred_element_type=jnp.float32
    )


def outer_sum(left, right):
    return lax.dot_general(
        left, right, (((0,), (0,)), ((), ())), preferred_element_type=jnp.float32
    )


def plain_dot(left, right):
    return jnp.dot(left, right, preferred_element_type=jnp.float32)


def rotate(values, places, direction):
    half_dim = values.shape[-1] // 2
    inv_freq = THETA_BASE ** (-jnp.arange(half_dim, dtype=jnp.float32) * (2.0 / values.shape[-1]))
    angles = places.astype(jnp.float32)[:, None] * inv_freq[None, :]
    cosine = jnp.cos(angles)[:, None, :]
    sine_val = direction * jnp.sin(angles)[:, None, :]
    first = values[..., :half_dim]
    second = values[..., half_dim:]
    return jnp.concatenate(
        [first * cosine - second * sine_val, second * cosine + first * sine_val], -1
    )


def scaled(values, gain_vec):
    factor = lax.rsqrt(jnp.mean(values * values, -1, keepdims=True) + EPSILON)
    return values * factor * gain_vec


def norm_back(values, gain_vec, grad_in):
    factor = lax.rsqrt(jnp.mean(values * values, -1, keepdims=True) + EPSILON)
    gain_grad = jnp.sum(grad_in * values * factor, 0)
    mean_term = jnp.mean(grad_in * gain_vec * values, -1, keepdims=True)
    return (
        gain_grad,
        factor * gain_vec * grad_in - values * (factor * factor * factor) * mean_term,
    )


def ffn_back(grad_rows, kept_rows, gate_pre, up_pre, wg_part, wu_part, wd_part):
    sigmoid_val = jax.nn.sigmoid(gate_pre)
    silu_val = gate_pre * sigmoid_val
    hidden_act = (silu_val * up_pre).astype(jnp.bfloat16)
    grad_down = outer_sum(hidden_act, grad_rows)
    d_act = times_trans(grad_rows, wd_part)
    d_gate = (d_act * up_pre * sigmoid_val * (1.0 + gate_pre * (1.0 - sigmoid_val))).astype(
        jnp.bfloat16
    )
    d_up = (d_act * silu_val).astype(jnp.bfloat16)
    grad_gate = outer_sum(d_gate, kept_rows)
    grad_up = outer_sum(d_up, kept_rows)
    d_normed = plain_dot(d_gate, wg_part) + plain_dot(d_up, wu_part)
    return ((grad_gate, grad_up, grad_down), d_normed)


def body(
    inputs,
    cotangent,
    positions,
    gain_attn,
    w_query,
    w_key,
    w_value,
    w_out,
    gain_ffn,
    w_gate,
    w_up,
    w_down,
):
    n_micro, per_device, model_width = inputs.shape
    n_seq = lax.axis_size("seq")
    n_shard = lax.axis_size("shard")
    section_idx = lax.axis_index("section")
    shard_pos = lax.axis_index("shard")
    member = shard_pos * n_seq + lax.axis_index("seq")
    span_rows = per_device * n_seq
    total_len = span_rows * n_shard
    local_heads = HEADS // n_seq
    kv_repeat = n_seq // KV_HEADS
    q_width = local_heads * HEAD_DIM
    attn_scale = 1.0 / math.sqrt(HEAD_DIM)
    gain_one, gain_two, wq_full, wk_full, wv_full, wo_full = (
        lax.all_gather(gain_attn[0], ("shard", "seq"), axis=0, tiled=True),
        lax.all_gather(gain_ffn[0], ("shard", "seq"), axis=0, tiled=True),
        lax.all_gather(w_query[0], ("shard", "seq"), axis=0, tiled=True),
        lax.all_gather(w_key[0], ("shard", "seq"), axis=0, tiled=True),
        lax.all_gather(w_value[0], ("shard", "seq"), axis=0, tiled=True),
        lax.all_gather(w_out[0], ("shard", "seq"), axis=0, tiled=True),
    )
    gain_a = gain_one.astype(jnp.float32)
    gain_f = gain_two.astype(jnp.float32)
    wg_use, wu_use, wd_use = (w_gate[0], w_up[0], w_down[0])

    def spread_rows(block_in):
        return lax.all_gather(block_in, ("shard", "seq"), axis=0, tiled=True)

    def fold_rows(block_in):
        return lax.psum_scatter(block_in, ("shard", "seq"), scatter_dimension=0, tiled=True)

    def to_heads(block_in):
        return lax.all_to_all(block_in, "seq", split_axis=1, concat_axis=0, tiled=True)

    def to_tokens(block_in):
        return lax.all_to_all(block_in, "seq", split_axis=0, concat_axis=1, tiled=True)

    def over_keys(head_keys, head_values, step_fn, init_state):
        return step_fn(
            init_state,
            (
                lax.all_gather(head_keys, "shard", axis=0, tiled=True),
                lax.all_gather(head_values, "shard", axis=0, tiled=True),
            ),
            jnp.int32(0),
        )

    def place_sets(batch_index):
        place_row = lax.dynamic_index_in_dim(positions, batch_index, 0, keepdims=False)
        token_places = lax.dynamic_slice_in_dim(place_row, member * per_device, per_device)
        span_places = lax.dynamic_slice_in_dim(place_row, shard_pos * span_rows, span_rows)
        return (place_row, token_places, span_places)

    zero_rows = jnp.zeros((per_device, model_width), jnp.bfloat16)
    arrived_x = zero_rows
    results = []
    stored = []
    for tick_index in range(n_micro + 1):
        own_rows = inputs[tick_index] if tick_index < n_micro else zero_rows
        input_now = jnp.where(section_idx == 0, own_rows, arrived_x)
        batch_index = jnp.clip(tick_index - section_idx, 0, n_micro - 1)
        forward_place_row, forward_token_places, forward_span_places = place_sets(batch_index)
        forward_values_in = input_now.astype(jnp.float32)
        forward_normed_one = scaled(forward_values_in, gain_a).astype(jnp.bfloat16)
        queries = rotate(
            times_trans(forward_normed_one, wq_full).reshape(per_device, HEADS, HEAD_DIM),
            forward_token_places,
            1.0,
        ).astype(jnp.bfloat16)
        key_rows = rotate(
            times_trans(forward_normed_one, wk_full).reshape(per_device, KV_HEADS, HEAD_DIM),
            forward_token_places,
            1.0,
        ).astype(jnp.bfloat16)
        value_rows = (
            times_trans(forward_normed_one, wv_full)
            .reshape(per_device, KV_HEADS, HEAD_DIM)
            .astype(jnp.bfloat16)
        )
        key_rows = jnp.repeat(key_rows, kv_repeat, axis=1)
        value_rows = jnp.repeat(value_rows, kv_repeat, axis=1)
        packed = jnp.concatenate(
            [queries.reshape(per_device, n_seq, q_width), key_rows, value_rows], -1
        )
        arrived = to_heads(packed)[:, 0]
        forward_head_query = arrived[:, :q_width].reshape(span_rows, local_heads, HEAD_DIM)
        forward_head_keys = arrived[:, q_width : q_width + HEAD_DIM]
        forward_head_values = arrived[:, q_width + HEAD_DIM :]

        def absorb(state_in, key_piece, start_row):
            run_max, run_total, run_acc = state_in
            piece_keys, piece_values = key_piece
            visible = forward_place_row[None, None, :] <= forward_span_places[None, :, None]
            scores = (
                jnp.einsum(
                    "qhd,kd->hqk",
                    forward_head_query,
                    piece_keys,
                    preferred_element_type=jnp.float32,
                )
                * attn_scale
            )
            scores = jnp.where(visible, scores, NEG_LARGE)
            new_max = jnp.maximum(run_max, jnp.max(scores, -1))
            weight = jnp.where(visible, jnp.exp(scores - new_max[..., None]), 0.0)
            rescale = jnp.exp(run_max - new_max)
            run_total = jnp.sum(weight, -1)
            run_acc = run_acc * rescale.T[..., None] + jnp.einsum(
                "hqk,kd->qhd",
                weight.astype(jnp.bfloat16),
                piece_values,
                preferred_element_type=jnp.float32,
            )
            return (new_max, run_total, run_acc)

        forward_start_state = (
            jnp.full((local_heads, span_rows), NEG_LARGE, jnp.float32),
            jnp.zeros((local_heads, span_rows), jnp.float32),
            jnp.zeros((span_rows, local_heads, HEAD_DIM), jnp.float32),
        )
        run_max, run_total, run_acc = over_keys(
            forward_head_keys, forward_head_values, absorb, forward_start_state
        )
        forward_attended = run_acc / run_total.T[..., None]
        forward_spread = run_max + jnp.log(run_total)
        forward_mixed_tok = to_tokens(
            forward_attended.astype(jnp.bfloat16).reshape(span_rows, 1, q_width)
        ).reshape(per_device, HEADS * HEAD_DIM)
        forward_hidden_in = forward_values_in + plain_dot(forward_mixed_tok, wo_full)
        normed_two = scaled(forward_hidden_in, gain_f).astype(jnp.bfloat16)
        forward_kept_rows = spread_rows(normed_two)
        forward_gate_pre = times_trans(forward_kept_rows, wg_use)
        forward_up_pre = times_trans(forward_kept_rows, wu_use)
        hidden_act = (jax.nn.silu(forward_gate_pre) * forward_up_pre).astype(jnp.bfloat16)
        branch = fold_rows(plain_dot(hidden_act, wd_use))
        result = (forward_hidden_in + branch).astype(jnp.bfloat16)
        forward_saved = (
            input_now,
            forward_head_query,
            forward_head_keys,
            forward_head_values,
            forward_attended,
            forward_spread,
            forward_mixed_tok,
            forward_hidden_in,
            forward_kept_rows,
            forward_gate_pre,
            forward_up_pre,
        )
        result, saved = (result, forward_saved)
        results.append(result)
        stored.append(saved)
        if tick_index < n_micro:
            arrived_x = shifted(result, "section", 1)
    returned = zero_rows
    grads_back = []
    row_lists = []
    gain_total = None
    ffn_total = None
    for tick_index in range(n_micro + 1):
        own_rows = cotangent[tick_index] if tick_index < n_micro else zero_rows
        grad_now = jnp.where(section_idx == 1, own_rows, returned)
        batch_index = jnp.clip(tick_index - 1 + section_idx, 0, n_micro - 1)
        early_saved = stored[max(tick_index - 1, 0)]
        late_saved = stored[min(tick_index + 1, n_micro)]
        saved = jax.tree.map(
            lambda early_val, late_val: jnp.where(section_idx == 0, early_val, late_val),
            early_saved,
            late_saved,
        )
        (
            input_bf,
            head_query,
            backward_head_keys,
            backward_head_values,
            attended,
            spread,
            mixed_tok,
            hidden_in,
            kept_rows,
            gate_pre,
            up_pre,
        ) = saved
        backward_place_row, backward_token_places, backward_span_places = place_sets(batch_index)
        values_in = input_bf.astype(jnp.float32)
        normed_one = scaled(values_in, gain_a).astype(jnp.bfloat16)
        grad_all = spread_rows(grad_now)
        ffn_terms, d_partial = ffn_back(
            grad_all, kept_rows, gate_pre, up_pre, wg_use, wu_use, wd_use
        )
        d_normed_two = fold_rows(d_partial)
        grad_gf, d_hidden = norm_back(hidden_in, gain_f, d_normed_two)
        d_hidden = d_hidden + grad_now.astype(jnp.float32)
        d_branch = d_hidden.astype(jnp.bfloat16)
        d_mixed = times_trans(d_branch, wo_full).astype(jnp.bfloat16)
        d_att = to_heads(d_mixed.reshape(per_device, n_seq, q_width))[:, 0].reshape(
            span_rows, local_heads, HEAD_DIM
        )
        offset = jnp.sum(d_att.astype(jnp.float32) * attended, -1).T

        def collect(state_in, key_piece, start_row):
            piece_keys, piece_values = key_piece
            visible = backward_place_row[None, None, :] <= backward_span_places[None, :, None]
            scores = (
                jnp.einsum(
                    "qhd,kd->hqk", head_query, piece_keys, preferred_element_type=jnp.float32
                )
                * attn_scale
            )
            probs = jnp.where(visible, jnp.exp(scores - spread[..., None]), 0.0)
            d_probs = jnp.einsum(
                "qhd,kd->hqk", d_att, piece_values, preferred_element_type=jnp.float32
            )
            d_score = (probs * (d_probs - offset[..., None]) * attn_scale).astype(jnp.bfloat16)
            d_query_acc = jnp.einsum(
                "hqk,kd->qhd", d_score, piece_keys, preferred_element_type=jnp.float32
            )
            key_part = jnp.einsum(
                "hqk,qhd->kd", d_score, head_query, preferred_element_type=jnp.float32
            )
            value_part = jnp.einsum(
                "hqk,qhd->kd", probs.astype(jnp.bfloat16), d_att, preferred_element_type=jnp.float32
            )
            return (d_query_acc, key_part, value_part)

        start_state = (
            jnp.zeros((span_rows, local_heads, HEAD_DIM), jnp.float32),
            jnp.zeros((total_len, HEAD_DIM), jnp.float32),
            jnp.zeros((total_len, HEAD_DIM), jnp.float32),
        )
        d_query_acc, d_keys_all, d_values_all = over_keys(
            backward_head_keys, backward_head_values, collect, start_state
        )
        own_keys = lax.psum_scatter(
            d_keys_all.astype(jnp.bfloat16), "shard", scatter_dimension=0, tiled=True
        ).astype(jnp.float32)
        own_values = lax.psum_scatter(
            d_values_all.astype(jnp.bfloat16), "shard", scatter_dimension=0, tiled=True
        ).astype(jnp.float32)
        d_query_head = rotate(d_query_acc, backward_span_places, -1.0).astype(jnp.bfloat16)
        d_query = to_tokens(d_query_head.reshape(span_rows, 1, q_width)).reshape(
            per_device, HEADS * HEAD_DIM
        )
        own_keys = rotate(own_keys[:, None, :], backward_span_places, -1.0)[:, 0]
        back_kv = lax.all_to_all(
            jnp.concatenate([own_keys, own_values], -1)[:, None, :].astype(jnp.bfloat16),
            "seq",
            split_axis=0,
            concat_axis=1,
            tiled=True,
        ).astype(jnp.float32)
        back_kv = jnp.sum(back_kv.reshape(per_device, KV_HEADS, kv_repeat, 2 * HEAD_DIM), 2)
        d_key = (
            back_kv[..., :HEAD_DIM].reshape(per_device, KV_HEADS * HEAD_DIM).astype(jnp.bfloat16)
        )
        d_value = (
            back_kv[..., HEAD_DIM:].reshape(per_device, KV_HEADS * HEAD_DIM).astype(jnp.bfloat16)
        )
        d_normed_one = (
            plain_dot(d_query, wq_full) + plain_dot(d_key, wk_full) + plain_dot(d_value, wv_full)
        )
        grad_ga, d_input = norm_back(values_in, gain_a, d_normed_one)
        d_input = d_input + d_hidden
        gain_terms = (grad_ga, grad_gf)
        row_terms = (d_query, d_key, d_value, normed_one, mixed_tok, d_branch)
        d_input, gain_terms, row_terms, ffn_terms = (
            d_input.astype(jnp.bfloat16),
            gain_terms,
            row_terms,
            ffn_terms,
        )
        grads_back.append(d_input)
        row_lists.append(row_terms)
        if tick_index < n_micro:
            returned = shifted(d_input, "section", -1)
        if gain_total is None:
            gain_total = gain_terms
            ffn_total = ffn_terms
        else:
            gain_total = jax.tree.map(jnp.add, gain_total, gain_terms)
            ffn_total = jax.tree.map(jnp.add, ffn_total, ffn_terms)
    joined = [
        jnp.concatenate([row_set[index_val] for row_set in row_lists], 0) for index_val in range(6)
    ]
    grad_wq = outer_sum(joined[0], joined[3])
    grad_wk = outer_sum(joined[1], joined[3])
    grad_wv = outer_sum(joined[2], joined[3])
    grad_wo = outer_sum(joined[4], joined[5])
    attn_owned = (
        lax.psum_scatter(gain_total[0], ("shard", "seq"), scatter_dimension=0, tiled=True),
        lax.psum_scatter(gain_total[1], ("shard", "seq"), scatter_dimension=0, tiled=True),
        lax.psum_scatter(grad_wq, ("shard", "seq"), scatter_dimension=0, tiled=True),
        lax.psum_scatter(grad_wk, ("shard", "seq"), scatter_dimension=0, tiled=True),
        lax.psum_scatter(grad_wv, ("shard", "seq"), scatter_dimension=0, tiled=True),
        lax.psum_scatter(grad_wo, ("shard", "seq"), scatter_dimension=0, tiled=True),
    )
    outputs = lax.dynamic_slice_in_dim(jnp.stack(results), section_idx, n_micro, 0)[None]
    input_grads = lax.dynamic_slice_in_dim(jnp.stack(grads_back), 1 - section_idx, n_micro, 0)[None]
    return (
        outputs,
        input_grads,
        attn_owned[0][None],
        attn_owned[2][None],
        attn_owned[3][None],
        attn_owned[4][None],
        attn_owned[5][None],
        attn_owned[1][None],
        ffn_total[0][None],
        ffn_total[1][None],
        ffn_total[2][None],
    )


def solution(mesh):
    in_specs = (
        P(None, ("shard", "seq"), None),
        P(None, ("shard", "seq"), None),
        P(),
        P("section", ("shard", "seq")),
        P("section", ("shard", "seq"), None),
        P("section", ("shard", "seq"), None),
        P("section", ("shard", "seq"), None),
        P("section", ("shard", "seq"), None),
        P("section", ("shard", "seq")),
        P("section", ("shard", "seq"), None),
        P("section", ("shard", "seq"), None),
        P("section", ("shard", "seq"), None),
    )
    out_specs = (
        P("section", None, ("shard", "seq"), None),
        P("section", None, ("shard", "seq"), None),
        P("section", ("shard", "seq")),
        P("section", ("shard", "seq"), None),
        P("section", ("shard", "seq"), None),
        P("section", ("shard", "seq"), None),
        P("section", ("shard", "seq"), None),
        P("section", ("shard", "seq")),
        P("section", ("shard", "seq"), None),
        P("section", ("shard", "seq"), None),
        P("section", ("shard", "seq"), None),
    )
    return jax.shard_map(body, mesh=mesh, in_specs=in_specs, out_specs=out_specs, check_vma=False)
```

profile of v0, /device:TPU:0, one launch (start us, length us, event | category | flops | bytes accessed | tf_op | source)
XLA Modules:
  0.0 2377.6 jit_solution(4613267725506911186)
XLA Ops:
  10.0 23.2 all-gather
  37.7 13.2 all-gather.30.cloned.1.call-done
  52.9 37.0 %all-gather.32.cloned.1.call-done = bf16[1,256,2048]{2,1,0:T(8,128)(2,1)} async-done(((bf16[1,16,2048]{2,1,0:T(8,128)(2,1)}), bf16[1,256,2048]{2,1,0:T(8,128)(2,1)}) %all-gather.32.cloned.1.call-update) | async-done | bytes 1048592 | tf_op jit(solution)/shard_map/all_gather | solution.py:115
  91.9 74.1 %all-gather.28.cloned.1.call-done = bf16[1,2048,2048]{2,1,0:T(8,128)(2,1)} async-done(((bf16[1,128,2048]{2,1,0:T(8,128)(2,1)}), bf16[1,2048,2048]{2,1,0:T(8,128)(2,1)}) %all-gather.28.cloned.1.call-update) | async-done | bytes 8388624 | tf_op jit(solution)/shard_map/all_gather | solution.py:113
  177.5 8.6 all-to-all-done
  186.6 13.9 all_gather.76
  200.5 14.2 all_gather.77
  227.1 21.8 all-gather.5
  256.4 47.8 %all-gather.18.cloned.1.call-done = bf16[1024,2048]{1,0:T(8,128)(2,1)} async-done(((bf16[64,2048]{1,0:T(8,128)(2,1)}), bf16[1024,2048]{1,0:T(8,128)(2,1)}) %all-gather.18.cloned.1.call-update) | async-done | bytes 4194320 | tf_op jit(solution)/shard_map/all_gather | solution.py:123
  317.0 103.3 %reduce-scatter.17.cloned.1.call-done = f32[64,2048]{1,0:T(8,128)} async-done(((f32[1024,2048]{1,0:T(8,128)}), f32[64,2048]{1,0:T(8,128)}) %reduce-scatter.17.cloned.1.call-update) | async-done | bytes 524304 | tf_op jit(solution)/shard_map/reduce_scatter | solution.py:126
  473.7 13.6 all_gather.81
  495.8 13.5 all_gather.82
  524.4 10.4 all_to_all.207
  544.9 51.1 %all-gather.20.cloned.1.call-done = bf16[1024,2048]{1,0:T(8,128)(2,1)} async-done(((bf16[64,2048]{1,0:T(8,128)(2,1)}), bf16[1024,2048]{1,0:T(8,128)(2,1)}) %all-gather.20.cloned.1.call-update) | async-done | bytes 4194320 | tf_op jit(solution)/shard_map/all_gather | solution.py:123
  609.1 103.2 %reduce-scatter.19.cloned.1.call-done = f32[64,2048]{1,0:T(8,128)} async-done(((f32[1024,2048]{1,0:T(8,128)}), f32[64,2048]{1,0:T(8,128)}) %reduce-scatter.19.cloned.1.call-update) | async-done | bytes 524304 | tf_op jit(solution)/shard_map/reduce_scatter | solution.py:126
  726.8 6.9 fusion.19
  769.3 13.6 all_gather.84
  790.9 13.5 all_gather.85
  804.4 6.5 fusion.366
  817.0 10.6 all_to_all.208
  839.5 50.1 %all-gather.22.cloned.1.call-done = bf16[1024,2048]{1,0:T(8,128)(2,1)} async-done(((bf16[64,2048]{1,0:T(8,128)(2,1)}), bf16[1024,2048]{1,0:T(8,128)(2,1)}) %all-gather.22.cloned.1.call-update) | async-done | bytes 4194320 | tf_op jit(solution)/shard_map/all_gather | solution.py:123
  902.9 37.8 %all-gather.36.cloned.1.call-done = bf16[1,1024,2048]{2,1,0:T(8,128)(2,1)} async-done(((bf16[1,64,2048]{2,1,0:T(8,128)(2,1)}), bf16[1,1024,2048]{2,1,0:T(8,128)(2,1)}) %all-gather.36.cloned.1.call-update) | async-done | bytes 4194320 | tf_op jit(solution)/shard_map/all_gather | solution.py:123
  948.4 6.3 convolution_add_fusion.2
  963.3 13.3 all_gather.87
  982.9 65.0 %reduce-scatter.21.cloned.1.call-done = f32[64,2048]{1,0:T(8,128)} async-done(((f32[1024,2048]{1,0:T(8,128)}), f32[64,2048]{1,0:T(8,128)}) %reduce-scatter.21.cloned.1.call-update) | async-done | bytes 524304 | tf_op jit(solution)/shard_map/reduce_scatter | solution.py:126
  1052.0 104.2 %reduce-scatter.23.cloned.1.call-done = f32[64,2048]{1,0:T(8,128)} async-done(((f32[1024,2048]{1,0:T(8,128)}), f32[64,2048]{1,0:T(8,128)}) %reduce-scatter.23.cloned.1.call-update) | async-done | bytes 524304 | tf_op jit(solution)/shard_map/reduce_scatter | solution.py:126
  1172.8 14.3 all_gather.88
  1192.4 6.4 fusion.12
  1231.1 15.6 reduce-scatter.27.cloned.1.call-done
  1278.0 9.2 collective-permute-done.2
  1288.5 47.7 %all-gather.24.cloned.1.call-done = bf16[1024,2048]{1,0:T(8,128)(2,1)} async-done(((bf16[64,2048]{1,0:T(8,128)(2,1)}), bf16[1024,2048]{1,0:T(8,128)(2,1)}) %all-gather.24.cloned.1.call-update) | async-done | bytes 4194320 | tf_op jit(solution)/shard_map/all_gather | solution.py:123
  1352.7 14.3 all_gather.90
  1368.2 84.9 %reduce-scatter.29.cloned.1.call-done = f32[64,2048]{1,0:T(8,128)} async-done(((f32[1024,2048]{1,0:T(8,128)}), f32[64,2048]{1,0:T(8,128)}) %reduce-scatter.29.cloned.1.call-update) | async-done | bytes 524304 | tf_op jit(solution)/shard_map/reduce_scatter | solution.py:126
  1474.0 14.2 all_gather.91
  1493.6 6.4 fusion.7
  1532.1 15.6 reduce-scatter.33.cloned.1.call-done
  1579.0 9.2 collective-permute-done.3
  1589.9 47.9 %all-gather.26.cloned.1.call-done = bf16[1024,2048]{1,0:T(8,128)(2,1)} async-done(((bf16[64,2048]{1,0:T(8,128)(2,1)}), bf16[1024,2048]{1,0:T(8,128)(2,1)}) %all-gather.26.cloned.1.call-update) | async-done | bytes 4194320 | tf_op jit(solution)/shard_map/all_gather | solution.py:123
  1654.4 14.3 all_gather.93
  1669.9 85.0 %reduce-scatter.35.cloned.1.call-done = f32[64,2048]{1,0:T(8,128)} async-done(((f32[1024,2048]{1,0:T(8,128)}), f32[64,2048]{1,0:T(8,128)}) %reduce-scatter.35.cloned.1.call-update) | async-done | bytes 524304 | tf_op jit(solution)/shard_map/reduce_scatter | solution.py:126
  1775.7 14.5 all_gather.94
  1795.5 6.4 fusion.2
  1833.5 16.3 reduce-scatter.39.cloned.1.call-done
  1883.7 9.4 fusion.194
  1894.3 8.1 fusion.188
  1940.3 59.2 %all-reduce.2 = (f32[2048]{0:T(1024)S(1)}, f32[2048]{0:T(1024)S(1)}) all-reduce(f32[2048]{0:T(1024)S(1)} %add_add_fusion.1, f32[2048]{0:T(1024)S(1)} %add_add_fusion), channel_id=21, replica_groups=mesh['section'=2,'shard'=4,'seq'=4] {'shard','seq'}, use_global_device_ids=true, to_apply=%region_42.43.clone | all-reduce | flops 4096 | bytes 32768
  2006.4 182.3 %reduce-scatter.47.cloned.1.call-done = f32[128,2048]{1,0:T(8,128)} async-done(((f32[2048,2048]{1,0:T(8,128)}), f32[128,2048]{1,0:T(8,128)}) %reduce-scatter.47.cloned.1.call-update) | async-done | bytes 1048592 | tf_op jit(solution)/shard_map/reduce_scatter | solution.py:391
  2188.7 182.1 %reduce-scatter.41.cloned.1.call-done = f32[128,2048]{1,0:T(8,128)} async-done(((f32[2048,2048]{1,0:T(8,128)}), f32[128,2048]{1,0:T(8,128)}) %reduce-scatter.41.cloned.1.call-update) | async-done | bytes 1048592 | tf_op jit(solution)/shard_map/reduce_scatter | solution.py:388
  (654 shorter events, 620.3 us)
Async XLA Ops:
  7.2 304.0 %copy-start = (bf16[1,352,2048]{2,1,0:T(8,128)(2,1)S(1)}, bf16[1,352,2048]{2,1,0:T(8,128)(2,1)}, u32[]{:S(2)}) copy-start(bf16[1,352,2048]{2,1,0:T(8,128)(2,1)} %param.23) | copy-start | bytes 4325380
  7.2 158.7 %copy-start.42 = (bf16[2,64,2048]{2,1,0:T(8,128)(2,1)S(1)}, bf16[2,64,2048]{2,1,0:T(8,128)(2,1)}, u32[]{:S(2)}) copy-start(bf16[2,64,2048]{2,1,0:T(8,128)(2,1)} %param.12) | copy-start | bytes 1572868
  7.2 43.7 %all-gather.30.cloned.1.call-start = ((), (), s32[]{:S(2)}) async-start(), calls=%async_computation.53 | async-start | bytes 1114112 | tf_op jit(solution)/shard_map/all_gather | solution.py:114
  7.9 82.0 %all-gather.32.cloned.1.call-start = ((), (), s32[]{:S(2)}) async-start(), calls=%async_computation.54 | async-start | bytes 1114112 | tf_op jit(solution)/shard_map/all_gather | solution.py:115
  8.7 157.2 %all-gather.28.cloned.1.call-start = ((), (), s32[]{:S(2)}) async-start(), calls=%async_computation.52 | async-start | bytes 8912896 | tf_op jit(solution)/shard_map/all_gather | solution.py:113
  9.4 240.8 %all-gather.34.cloned.1.call-start = ((), (), s32[]{:S(2)}) async-start(), calls=%async_computation.55 | async-start | bytes 8912896 | tf_op jit(solution)/shard_map/all_gather | solution.py:116
  33.2 138.5 %copy-start.120 = (f32[32]{0:T(128)}, f32[32]{0:T(128)S(1)}, u32[]{:S(2)}) copy-start(f32[32]{0:T(128)S(1)} %multiply_power_fusion) | copy-start | bytes 388
  173.1 13.0 all-to-all-start
  223.6 25.3 %all-to-all-start.1 = ((bf16[4,2,16384]{2,1,0:T(2,128)(2,1)}), bf16[4,2,16384]{2,1,0:T(2,128)(2,1)S(1)}, u32[]{:S(2)}, u32[]{:S(2)}) async-start(bf16[4,2,16384]{2,1,0:T(2,128)(2,1)} %reshape.1315), calls=%async_computation.1 | async-start | bytes 524288 | tf_op jit(solution)/shard_map/all_to_all | solution.py:132
  227.0 77.2 %all-gather.18.cloned.1.call-start = ((), (), s32[]{:S(2)}) async-start(), calls=%async_computation.31 | async-start | bytes 4456448 | tf_op jit(solution)/shard_map/all_gather | solution.py:123
  255.5 164.7 %copy-start.38 = (f32[64,2048]{1,0:T(8,128)}, f32[64,2048]{1,0:T(8,128)S(1)}, u32[]{:S(2)}) copy-start(f32[64,2048]{1,0:T(8,128)S(1)} %get-tuple-element.166) | copy-start | bytes 1572868
  256.4 163.8 %reduce-scatter.17.cloned.1.call-start = ((), (), s32[]{:S(2)}) async-start(), calls=%async_computation.32 | async-start | bytes 8912896 | tf_op jit(solution)/shard_map/reduce_scatter | solution.py:126
  316.9 113.3 %copy-start.43 = (bf16[2,64,2048]{2,1,0:T(8,128)(2,1)S(1)}, bf16[2,64,2048]{2,1,0:T(8,128)(2,1)}, u32[]{:S(2)}) copy-start(bf16[2,64,2048]{2,1,0:T(8,128)(2,1)} %param.12) | copy-start | bytes 1572868
  421.3 9.0 collective-permute-start
  456.2 10.9 all-to-all-start.2
  460.3 135.7 %all-gather.20.cloned.1.call-start = ((), (), s32[]{:S(2)}) async-start(), calls=%async_computation.33 | async-start | bytes 4456448 | tf_op jit(solution)/shard_map/all_gather | solution.py:123
  544.9 167.5 %reduce-scatter.19.cloned.1.call-start = ((), (), s32[]{:S(2)}) async-start(), calls=%async_computation.34 | async-start | bytes 8912896 | tf_op jit(solution)/shard_map/reduce_scatter | solution.py:126
  714.3 9.3 collective-permute-start.1
  751.7 10.9 all-to-all-start.4
  755.8 133.8 %all-gather.22.cloned.1.call-start = ((), (), s32[]{:S(2)}) async-start(), calls=%async_computation.35 | async-start | bytes 4456448 | tf_op jit(solution)/shard_map/all_gather | solution.py:123
  837.7 103.0 %all-gather.36.cloned.1.call-start = ((), (), s32[]{:S(2)}) async-start(), calls=%async_computation.56 | async-start | bytes 4456448 | tf_op jit(solution)/shard_map/all_gather | solution.py:123
  839.4 208.4 %reduce-scatter.21.cloned.1.call-start = ((), (), s32[]{:S(2)}) async-start(), calls=%async_computation.36 | async-start | bytes 8912896 | tf_op jit(solution)/shard_map/reduce_scatter | solution.py:126
  902.7 253.5 %reduce-scatter.23.cloned.1.call-start = ((), (), s32[]{:S(2)}) async-start(), calls=%async_computation.37 | async-start | bytes 8912896 | tf_op jit(solution)/shard_map/reduce_scatter | solution.py:126
  1167.3 19.8 all-to-all-start.6
  1171.3 57.5 %reduce-scatter.25.cloned.1.call-start = ((), (), s32[]{:S(2)}) async-start(), calls=%async_computation.38 | async-start | bytes 163840 | tf_op jit(solution)/shard_map/reduce_scatter | solution.py:330
  1214.8 10.1 all-to-all-start.7
  1218.8 27.9 %reduce-scatter.27.cloned.1.call-start = ((), (), s32[]{:S(2)}) async-start(), calls=%async_computation.39 | async-start | bytes 163840 | tf_op jit(solution)/shard_map/reduce_scatter | solution.py:333
  1253.3 9.8 all-to-all-start.8
  1257.2 78.9 %all-gather.24.cloned.1.call-start = ((), (), s32[]{:S(2)}) async-start(), calls=%async_computation.40 | async-start | bytes 4456448 | tf_op jit(solution)/shard_map/all_gather | solution.py:123
  1276.7 10.5 collective-permute-start.2
  1288.0 165.1 %reduce-scatter.29.cloned.1.call-start = ((), (), s32[]{:S(2)}) async-start(), calls=%async_computation.41 | async-start | bytes 8912896 | tf_op jit(solution)/shard_map/reduce_scatter | solution.py:126
  1464.2 24.0 %all-to-all-start.9 = ((bf16[64,4,512]{2,0,1:T(8,128)(2,1)}), bf16[64,4,512]{2,0,1:T(8,128)(2,1)}, u32[]{:S(2)}, u32[]{:S(2)}) async-start(bf16[64,4,512]{2,0,1:T(8,128)(2,1)} %bitcast.681), calls=%async_computation.16 | async-start | bytes 524288 | tf_op jit(solution)/shard_map/all_to_all | solution.py:129
  1468.3 61.6 %reduce-scatter.31.cloned.1.call-start = ((), (), s32[]{:S(2)}) async-start(), calls=%async_computation.42 | async-start | bytes 163840 | tf_op jit(solution)/shard_map/reduce_scatter | solution.py:330
  1515.8 10.1 all-to-all-start.10
  1519.9 27.8 %reduce-scatter.33.cloned.1.call-start = ((), (), s32[]{:S(2)}) async-start(), calls=%async_computation.43 | async-start | bytes 163840 | tf_op jit(solution)/shard_map/reduce_scatter | solution.py:333
  1554.3 9.8 all-to-all-start.11
  1558.2 79.6 %all-gather.26.cloned.1.call-start = ((), (), s32[]{:S(2)}) async-start(), calls=%async_computation.44 | async-start | bytes 4456448 | tf_op jit(solution)/shard_map/all_gather | solution.py:123
  1577.7 10.5 collective-permute-start.3
  1589.7 165.2 %reduce-scatter.35.cloned.1.call-start = ((), (), s32[]{:S(2)}) async-start(), calls=%async_computation.45 | async-start | bytes 8912896 | tf_op jit(solution)/shard_map/reduce_scatter | solution.py:126
  1766.0 24.2 %all-to-all-start.12 = ((bf16[64,4,512]{2,0,1:T(8,128)(2,1)}), bf16[64,4,512]{2,0,1:T(8,128)(2,1)}, u32[]{:S(2)}, u32[]{:S(2)}) async-start(bf16[64,4,512]{2,0,1:T(8,128)(2,1)} %bitcast.680), calls=%async_computation.22 | async-start | bytes 524288 | tf_op jit(solution)/shard_map/all_to_all | solution.py:129
  1770.0 61.9 %reduce-scatter.37.cloned.1.call-start = ((), (), s32[]{:S(2)}) async-start(), calls=%async_computation.46 | async-start | bytes 163840 | tf_op jit(solution)/shard_map/reduce_scatter | solution.py:330
  1817.9 10.2 all-to-all-start.13
  1821.9 27.9 %reduce-scatter.39.cloned.1.call-start = ((), (), s32[]{:S(2)}) async-start(), calls=%async_computation.47 | async-start | bytes 163840 | tf_op jit(solution)/shard_map/reduce_scatter | solution.py:333
  1856.4 9.8 all-to-all-start.14
  1860.3 141.9 %reduce-scatter.45.cloned.1.call-start = ((), (), s32[]{:S(2)}) async-start(), calls=%async_computation.50 | async-start | bytes 2228224 | tf_op jit(solution)/shard_map/reduce_scatter | solution.py:390
  1880.8 125.7 %reduce-scatter.43.cloned.1.call-start = ((), (), s32[]{:S(2)}) async-start(), calls=%async_computation.49 | async-start | bytes 2228224 | tf_op jit(solution)/shard_map/reduce_scatter | solution.py:389
  1883.5 305.2 %reduce-scatter.47.cloned.1.call-start = ((), (), s32[]{:S(2)}) async-start(), calls=%async_computation.51 | async-start | bytes 17825792 | tf_op jit(solution)/shard_map/reduce_scatter | solution.py:391
  1893.1 477.7 %reduce-scatter.41.cloned.1.call-start = ((), (), s32[]{:S(2)}) async-start(), calls=%async_computation.48 | async-start | bytes 17825792 | tf_op jit(solution)/shard_map/reduce_scatter | solution.py:388
  (135 other events, 1042.8 us)
Sparse Core Ops, SparseCore 0:
  10.2 40.6 all-gather.29
  53.0 36.8 all-gather.31
  92.1 73.7 all-gather.27
  168.0 75.9 all-gather.33
  256.5 47.6 all-gather.17
  317.1 103.0 reduce-scatter.16
  545.0 50.9 all-gather.19
  609.2 103.0 reduce-scatter.18
  837.8 51.7 all-gather.21
  891.6 49.0 all-gather.35
  944.7 103.0 reduce-scatter.20
  1051.8 104.3 reduce-scatter.22
  1207.0 19.4 reduce-scatter.24
  1229.3 17.3 reduce-scatter.26
  1288.1 47.9 all-gather.23
  1350.0 103.0 reduce-scatter.28
  1508.0 19.4 reduce-scatter.30
  1530.3 17.3 reduce-scatter.32
  1589.8 48.0 all-gather.25
  1651.7 103.1 reduce-scatter.34
  1810.1 19.3 reduce-scatter.36
  1832.4 17.3 reduce-scatter.38
  1880.9 60.1 reduce-scatter.44
  1945.7 60.6 reduce-scatter.42
  2011.1 177.5 reduce-scatter.46
  2193.3 177.5 reduce-scatter.40
where the time goes:
time: 2390 us; the launch traced here: 2380 us
  waiting for transfers between devices  1420 us (59%)
  matrix products  316 us (13%)
  blocking collectives  293 us (12%)
  local copies, waits for them, and re-layouts  153 us (6%)
  other arithmetic  120 us (5%)
  starting transfers between devices  63.4 us (3%)
    reduce_scatter x6, waiting for transfers between devices, fold_rows(): lax.psum_scatter(block_in, ('shard', 'seq'), scatter_dimension=0, tiled=T...  546 us
    all_gather x6, waiting for transfers between devices, spread_rows(): return lax.all_gather(block_in, ('shard', 'seq'), axis=0, tiled=True)  282 us
    reduce_scatter x1, waiting for transfers between devices, body(): lax.psum_scatter(grad_wo, ('shard', 'seq'), scatter_dimension=0, tiled=True)  182 us
    reduce_scatter x1, waiting for transfers between devices, body(): lax.psum_scatter(grad_wq, ('shard', 'seq'), scatter_dimension=0, tiled=True)  182 us
    dot_general x21, matrix products, plain_dot(): return jnp.dot(left, right, preferred_element_type=jnp.float32)  88 us
    unnamed x329, local copies, waits for them, and re-layouts  84.7 us
    all_gather x6, blocking collectives, over_keys(): lax.all_gather(head_values, 'shard', axis=0, tiled=True)  84.3 us
    all_gather x6, blocking collectives, over_keys(): lax.all_gather(head_keys, 'shard', axis=0, tiled=True)  83 us
  transfers between devices with their start and end apart: 43, of which 31 were waited for; matrix products, arithmetic and copies ran while one was open for 10% of the time, Pallas kernels for 0%

commit v1 on v0

--- a/solution.py
+++ b/solution.py
@@ -1,8 +1,12 @@
+import functools
 import math
+import types
 
 import jax
 import jax.numpy as jnp
 from jax import lax
+from jax.experimental import pallas as pl
+from jax.experimental.pallas import tpu as pltpu
 from jax.sharding import PartitionSpec as P
 
 HEADS = 32
@@ -407,6 +411,1045 @@
     )
 
 
+LOW = jnp.bfloat16
+FULL = jnp.float32
+MESH = pl.DeviceIdType.MESH
+RING = 4
+CHIPS = 2 * RING
+SPLIT = 2
+PLACE = 128
+ORDER = ((2, 1), (1, 1), (3, 1), (0, 1), (2, 0), (1, 0), (3, 0), (0, 0))
+IN_VMEM = pl.BlockSpec(memory_space=pltpu.VMEM)
+ANYWHERE = pl.BlockSpec(memory_space=pl.ANY)
+
+
+class Site:
+    def __init__(self):
+        self.section = lax.axis_index("section")
+        self.z = lax.axis_index("shard")
+        member = lax.axis_index("seq")
+        self.y = lax.div(member, 2)
+        self.core = lax.rem(member, 2)
+        self.up = (self.section, lax.rem(self.z + 1, RING), member)
+        self.down = (self.section, lax.rem(self.z + RING - 1, RING), member)
+        self.across = (self.section, self.z, (1 - self.y) * 2 + self.core)
+        self.sibling = (self.section, self.z, self.y * 2 + 1 - self.core)
+        self.corner = (self.section, self.z, (1 - self.y) * 2 + 1 - self.core)
+        self.partner = (1 - self.section, self.z, member)
+        self.member = member
+
+    def chip(self, along_z, along_y):
+        return lax.rem(self.z + along_z, RING) * 2 + lax.rem(self.y + along_y, 2)
+
+
+class Links:
+    def __init__(self, send, recv, site):
+        self.send, self.recv, self.site = send, recv, site
+        self.sent = []
+
+    def copy(self, index, src, dst, device):
+        return pltpu.make_async_remote_copy(
+            src_ref=src,
+            dst_ref=dst,
+            send_sem=self.send.at[index],
+            recv_sem=self.recv.at[index],
+            device_id=device,
+            device_id_type=MESH,
+        )
+
+    def go(self, index, src, dst, device):
+        copy = self.copy(index, src, dst, device)
+        copy.start()
+        self.sent.append(copy)
+
+    def got(self, index, where):
+        self.copy(index, where, where, self.site.sibling).wait_recv()
+        return where
+
+    def close(self):
+        for copy in self.sent:
+            copy.wait_send()
+
+
+def greet(site, corner, partner):
+    barrier = pltpu.get_barrier_semaphore()
+    devices = [site.up, site.down, site.across, site.sibling]
+    devices += [site.corner] * corner + [site.partner] * partner
+    for device in devices:
+        pl.semaphore_signal(barrier, inc=1, device_id=device, device_id_type=MESH)
+    pl.semaphore_wait(barrier, len(devices))
+
+
+SPREAD_SEMS = 7 * SPLIT + CHIPS
+SMALL_SEMS = 7 + CHIPS
+FOLD_SEMS = 7 * SPLIT + CHIPS
+
+
+def spread_steps(site, held, links, use, parts=SPLIT):
+    size = held.shape[2] // parts
+    other = 1 - site.core
+    up, down, across, relay, y_below, y_above, y_far = (k * parts for k in range(7))
+    shared = 7 * parts
+
+    def piece(along, part):
+        return held.at[site.chip(*along), site.core, pl.ds(part * size, size)]
+
+    def block(along, core):
+        return held.at[site.chip(*along), core]
+
+    def go(index, where, device):
+        links.go(index, where, where, device)
+
+    def share(slot, along):
+        go(shared + slot, block(along, site.core), site.sibling)
+
+    def consume(slot, along):
+        links.got(shared + slot, block(along, other))
+        use(site.chip(*along))
+
+    own, below, above, far = (0, 0), (3, 0), (1, 0), (2, 0)
+    y_own, yb, ya, yf = (0, 1), (3, 1), (1, 1), (2, 1)
+    for part in range(parts):
+        go(up + part, piece(own, part), site.up)
+        go(down + part, piece(own, part), site.down)
+        go(across + part, piece(own, part), site.across)
+    share(0, own)
+    yield
+    for part in range(parts):
+        came = links.got(up + part, piece(below, part))
+        if part % 2 == 0:
+            go(relay + part, came, site.up)
+        go(y_below + part, came, site.across)
+        came = links.got(down + part, piece(above, part))
+        if part % 2 == 1:
+            go(relay + part, came, site.down)
+        go(y_above + part, came, site.across)
+    share(1, below)
+    share(2, above)
+    yield
+    for part in range(parts):
+        links.got(across + part, piece(y_own, part))
+    share(3, y_own)
+    consume(0, own)
+    for part in range(parts):
+        go(y_far + part, links.got(relay + part, piece(far, part)), site.across)
+    share(4, far)
+    consume(1, below)
+    consume(2, above)
+    consume(3, y_own)
+    for part in range(parts):
+        links.got(y_below + part, piece(yb, part))
+        links.got(y_above + part, piece(ya, part))
+    share(5, yb)
+    share(6, ya)
+    consume(4, far)
+    consume(5, yb)
+    consume(6, ya)
+    for part in range(parts):
+        links.got(y_far + part, piece(yf, part))
+    share(7, yf)
+    consume(7, yf)
+
+
+def fold_steps(site, part_of, mine, pass_out, pass_in, stage, land, links):
+    rows = mine.shape[1]
+    size = rows // SPLIT
+    over, relay, up, down = CHIPS, CHIPS + 4 * SPLIT, CHIPS + 5 * SPLIT, CHIPS + 6 * SPLIT
+
+    def came(index, where):
+        return links.got(index, where)[...].astype(FULL)
+
+    def compute(step):
+        both = part_of(site.chip(*ORDER[step]))
+        pass_out[step] = both[:rows].astype(LOW)
+        links.go(step, pass_out.at[step], pass_in.at[step], site.sibling)
+        mine[step] = both[rows:]
+
+    def settle(step):
+        mine[step] += came(step, pass_in.at[step])
+
+    def send_over(step):
+        stage[step] = (mine[step] + came(step, pass_in.at[step])).astype(LOW)
+        for part in range(SPLIT):
+            where = pl.ds(part * size, size)
+            links.go(
+                over + step * SPLIT + part,
+                stage.at[step, where],
+                land.at[step, where],
+                site.across,
+            )
+
+    def pass_on(part):
+        where = pl.ds(part * size, size)
+        value = mine[4, where] + came(over + part, land.at[0, where])
+        stage[4, where] = value.astype(LOW)
+        device = site.up if part % 2 == 0 else site.down
+        links.go(relay + part, stage.at[4, where], land.at[4, where], device)
+
+    compute(0)
+    compute(1)
+    send_over(0)
+    compute(2)
+    send_over(1)
+    compute(3)
+    send_over(2)
+    compute(4)
+    send_over(3)
+    compute(5)
+    settle(4)
+    compute(6)
+    compute(7)
+    for part in range(SPLIT):
+        pass_on(part)
+    for step in (5, 6, 7):
+        settle(step)
+    for part in range(SPLIT):
+        where = pl.ds(part * size, size)
+        for step, base, device in ((5, up, site.up), (6, down, site.down)):
+            from_y = over + (step - 4) * SPLIT + part
+            value = mine[step, where] + came(from_y, land.at[step - 4, where])
+            if part % 2 == step - 5:
+                value = value + came(relay + part, land.at[4, where])
+            stage[step, where] = value.astype(LOW)
+            links.go(base + part, stage.at[step, where], land.at[step, where], device)
+    sums = []
+    for part in range(SPLIT):
+        where = pl.ds(part * size, size)
+        value = mine[7, where] + came(over + 3 * SPLIT + part, land.at[3, where])
+        value = value + came(up + part, land.at[5, where])
+        sums.append(value + came(down + part, land.at[6, where]))
+    return jnp.concatenate(sums, 0)
+
+
+class Cross:
+    def __init__(self, site, groups, src, dst, send, recv):
+        self.links = Links(send, recv, site)
+        self.site, self.groups, self.src, self.dst = site, groups, src, dst
+        self.started = 0
+        self.landed = set()
+        self.start()
+
+    def start(self):
+        if self.started < len(self.groups):
+            for index in self.groups[self.started]:
+                self.links.go(index, self.src[index], self.dst[index], self.site.partner)
+            self.started += 1
+
+    def wait(self, index):
+        if index in self.landed:
+            return
+        self.landed.add(index)
+        self.links.got(index, self.dst[index])
+        if all(other in self.landed for other in self.groups[self.started - 1]):
+            self.start()
+
+    def close(self):
+        for group in self.groups:
+            for index in group:
+                self.wait(index)
+        self.links.close()
+
+
+class Weights:
+    def __init__(self, site, plan, held, own, other, sems, cross):
+        self.site, self.plan, self.cross, self.sems = site, plan, cross, sems
+        self.held, self.own, self.other = held, own, other
+        self.waits = {}
+        for index, (_, _, _, crossed) in enumerate(plan):
+            if crossed is None:
+                self.start(index)
+
+    def start(self, index):
+        _, layer, start, _ = self.plan[index]
+        rows = self.own[index].shape[0]
+        target = self.held[index]
+        target = target if start is None else target.at[pl.ds(start, rows)]
+        from_own = pltpu.make_async_copy(self.own[index], target, self.sems.at[index])
+        from_other = pltpu.make_async_copy(self.other[index], target, self.sems.at[index])
+        pl.when(self.site.section == layer)(from_own.start)
+        pl.when(self.site.section != layer)(from_other.start)
+        self.waits[index] = from_own
+
+    def settle(self, keys):
+        todo = [index for index, item in enumerate(self.plan) if item[0] in keys]
+        for index in todo:
+            crossed = self.plan[index][3]
+            if crossed is not None and index not in self.waits:
+                self.cross.wait(crossed)
+                self.start(index)
+        for index in todo:
+            if self.waits[index] is not None:
+                self.waits[index].wait()
+                self.waits[index] = None
+
+
+def ring_kernel(spec, *refs):
+    refs = list(refs)
+
+    def take(count):
+        taken = refs[:count]
+        del refs[:count]
+        return taken
+
+    plan = spec.plan
+    values = take(spec.n_in)
+    own, other = take(len(plan)), take(len(plan))
+    sources = take(spec.n_cross)
+    take(spec.n_after)
+    named = types.SimpleNamespace(**dict(zip(spec.names, values + refs)))
+    site = Site()
+    named.site = site
+    greet(site, spec.peers, spec.n_cross or spec.peers)
+    cross = weights = None
+    if spec.n_cross:
+        targets = [getattr(named, key) for key in spec.crossed]
+        cross = Cross(
+            site, spec.groups, sources, targets, named.cross_send, named.cross_recv
+        )
+        for index, item in enumerate(plan):
+            if item[3] is not None:
+                own[index], other[index] = sources[item[3]], targets[item[3]]
+    if plan:
+        held = [getattr(named, item[0]) for item in plan]
+        weights = Weights(site, plan, held, own, other, named.weight_sem, cross)
+    total = None
+    if spec.fold is not None:
+        links = Links(named.fold_send, named.fold_recv, site)
+        weights.settle(spec.fold_keys)
+        total = fold_steps(
+            site,
+            functools.partial(spec.fold, named),
+            named.mine,
+            named.pass_out,
+            named.pass_in,
+            named.stage,
+            named.land,
+            links,
+        )
+    rows = spec.local(named, total)
+    if spec.use is not None:
+        held = named.held
+        held[site.chip(0, 0), site.core] = rows
+        kept = []
+
+        def consume(chip):
+            if plan:
+                weights.settle(spec.use_keys)
+            block = held[chip]
+            spec.use(named, chip, block.reshape(block.shape[0] * block.shape[1], block.shape[2]))
+            source = named.normed if spec.normed else held
+            copy = pltpu.make_async_copy(
+                source.at[chip], named.rows_all.at[chip], named.keep_sem.at[len(kept)]
+            )
+            copy.start()
+            kept.append(copy)
+
+        links_on = Links(named.spread_send, named.spread_recv, site)
+        spreading = spread_steps(site, held, links_on, consume)
+        next(spreading)
+        if spec.meanwhile is not None:
+            spec.meanwhile(named, spreading)
+        for _ in spreading:
+            pass
+        for copy in kept:
+            copy.wait()
+        links_on.close()
+    if spec.fold is not None:
+        links.close()
+    if cross is not None:
+        cross.close()
+
+
+def ring_call(
+    name, ident, inputs, fold_weights, use_weights, outputs, local, fold=None, use=None,
+    extra=None, after=(), meanwhile=None, peers=False, normed=False, cross=(),
+):
+    per_device, width = inputs.pop("like").shape
+    out_shape = [jax.ShapeDtypeStruct(*value) for value in outputs.values()]
+    out_specs = [IN_VMEM] * len(out_shape)
+    names = list(inputs) + list(outputs)
+    scratch, plan, own_set, other_set = {}, [], [], []
+    crossed = [key for group in cross for key in group]
+    cross_set = [value for group in cross for value in group.values()]
+    for key, parts in {**fold_weights, **use_weights}.items():
+        start = 0
+        for part in parts:
+            place = start if len(parts) > 1 else None
+            if len(part) == 2:
+                index = crossed.index(part[0])
+                own = other = cross_set[index]
+            else:
+                index = None
+                own, other = part[:2]
+            plan.append((key, part[-1], place, index))
+            own_set.append(own)
+            other_set.append(other)
+            start += own.shape[0]
+        scratch[key] = pltpu.VMEM((start, width), LOW)
+    full = (per_device, width)
+    more = dict(extra or {})
+    for key, value in zip(crossed, cross_set):
+        names.append(key)
+        out_shape.append(jax.ShapeDtypeStruct(value.shape, value.dtype))
+        out_specs.append(ANYWHERE)
+    if cross:
+        more.update(
+            cross_send=pltpu.SemaphoreType.DMA((len(crossed),)),
+            cross_recv=pltpu.SemaphoreType.DMA((len(crossed),)),
+        )
+    if plan:
+        more.update(weight_sem=pltpu.SemaphoreType.DMA((len(plan),)))
+    if fold is not None:
+        more.update(
+            mine=pltpu.VMEM((CHIPS, *full), FULL),
+            pass_out=pltpu.VMEM((CHIPS, *full), LOW),
+            pass_in=pltpu.VMEM((CHIPS, *full), LOW),
+            stage=pltpu.VMEM((CHIPS - 1, *full), LOW),
+            land=pltpu.VMEM((CHIPS - 1, *full), LOW),
+            fold_send=pltpu.SemaphoreType.DMA((FOLD_SEMS,)),
+            fold_recv=pltpu.SemaphoreType.DMA((FOLD_SEMS,)),
+        )
+    if use is not None:
+        names.append("rows_all")
+        out_shape.append(jax.ShapeDtypeStruct((CHIPS, 2, *full), LOW))
+        out_specs.append(ANYWHERE)
+        more.update(
+            held=pltpu.VMEM((CHIPS, 2, *full), LOW),
+            keep_sem=pltpu.SemaphoreType.DMA((CHIPS,)),
+            spread_send=pltpu.SemaphoreType.DMA((SPREAD_SEMS,)),
+            spread_recv=pltpu.SemaphoreType.DMA((SPREAD_SEMS,)),
+        )
+        if normed:
+            more.update(normed=pltpu.VMEM((CHIPS, 2, *full), LOW))
+    scratch.update(more)
+    names += list(scratch)
+    groups, at = [], 0
+    for group in cross:
+        groups.append(list(range(at, at + len(group))))
+        at += len(group)
+    spec = types.SimpleNamespace(
+        names=names, plan=plan, n_in=len(inputs), n_cross=len(crossed), n_after=len(after),
+        crossed=crossed, groups=groups, fold=fold, local=local, use=use, meanwhile=meanwhile,
+        peers=peers, normed=normed, fold_keys=list(fold_weights), use_keys=list(use_weights),
+    )
+    return pl.pallas_call(
+        functools.partial(ring_kernel, spec),
+        out_shape=out_shape,
+        in_specs=[IN_VMEM] * len(inputs)
+        + [ANYWHERE] * (2 * len(plan) + len(crossed) + len(after)),
+        out_specs=out_specs,
+        scratch_shapes=list(scratch.values()),
+        compiler_params=pltpu.CompilerParams(
+            collective_id=ident, has_side_effects=True, vmem_limit_bytes=56 * 2**20
+        ),
+        cost_estimate=pl.CostEstimate(
+            flops=2**35 * ((fold is not None) + (use is not None)),
+            bytes_accessed=2**23,
+            transcendentals=0,
+        ),
+        name=name,
+    )(*inputs.values(), *own_set, *other_set, *cross_set, *after)
+
+
+def rows_of(ref, chip, site):
+    return jnp.concatenate([ref[chip, 1 - site.core], ref[chip, site.core]], 0)
+
+
+def fold_mixed(named, chip):
+    return plain_dot(rows_of(named.mixed, chip, named.site), named.w_out[...])
+
+
+def fold_act(named, chip):
+    return plain_dot(rows_of(named.act, chip, named.site), named.w_down[...])
+
+
+def fold_d_qkv(named, chip):
+    return plain_dot(rows_of(named.d_qkv, chip, named.site), named.w_in[...])
+
+
+def fold_d_act(named, chip):
+    site = named.site
+    return plain_dot(rows_of(named.d_gate, chip, site), named.w_gate[...]) + plain_dot(
+        rows_of(named.d_up, chip, site), named.w_up[...]
+    )
+
+
+def use_qkv(named, chip, rows):
+    named.qkv[chip] = times_trans(rows, named.w_in[...])
+
+
+def put(ref, chip, value):
+    ref[chip] = value.astype(LOW).reshape(ref.shape[1:])
+
+
+def use_gate_up(named, chip, rows):
+    gate_pre = times_trans(rows, named.w_gate[...])
+    up_pre = times_trans(rows, named.w_up[...])
+    sig = jax.nn.sigmoid(gate_pre)
+    silu_val = gate_pre * sig
+    put(named.act, chip, silu_val * up_pre)
+    put(named.gate_slope, chip, up_pre * sig * (1.0 + gate_pre * (1.0 - sig)))
+    put(named.up_slope, chip, silu_val)
+
+
+def use_d_act(named, chip, rows):
+    d_act = times_trans(rows, named.w_down[...])
+    for out, slope in ((named.d_gate, named.gate_slope), (named.d_up, named.up_slope)):
+        put(out, chip, d_act * slope[chip].astype(FULL).reshape(d_act.shape))
+
+
+def use_d_mixed(named, chip, rows):
+    named.d_mixed[chip] = times_trans(rows, named.w_out[...]).astype(LOW)
+
+
+def local_start(named, total):
+    return named.x_rows[...]
+
+
+def gather_small(named, rows_spreading):
+    site = named.site
+    links_x = Links(named.small_x_send, named.small_x_recv, site)
+    links_x.go(0, named.gains_own, named.gains_x, site.partner)
+    links_x.go(1, named.kv_own, named.kv_x, site.partner)
+    links_x.got(0, named.gains_x)
+    own, came = named.gains_own[...], named.gains_x[...]
+    first = site.section == 0
+    named.gains_all[site.chip(0, 0), site.core] = jnp.concatenate(
+        [
+            jnp.where(first, own, came)[:2],
+            jnp.where(first, came, own)[:2],
+            jnp.zeros((4, own.shape[1]), FULL),
+        ],
+        0,
+    )
+    links = Links(named.small_send, named.small_recv, site)
+    spreading = spread_steps(site, named.gains_all, links, lambda chip: None, 1)
+    next(spreading)
+    links_x.got(1, named.kv_x)
+    named.kv_all[site.member, site.section] = named.kv_own[...]
+    named.kv_all[site.member, 1 - site.section] = named.kv_x[...]
+    links_kv = Links(named.kv_send, named.kv_recv, site)
+    mine = named.kv_all.at[site.member]
+    peers = (site.sibling, site.across, site.corner)
+    for index, device in enumerate(peers):
+        links_kv.go(index, mine, mine, device)
+    next(rows_spreading)
+    for _ in spreading:
+        pass
+    for index, device in enumerate(peers):
+        links_kv.got(index, named.kv_all.at[device[2]])
+    links.close()
+    links_kv.close()
+    links_x.close()
+    named.gain_row[...] = jnp.concatenate(
+        [named.gains_all[chip, core, :1] for chip in range(CHIPS) for core in range(2)], 1
+    )
+
+
+def use_first(named, chip, rows):
+    normed = scaled(rows.astype(FULL), named.gain_row[...]).astype(LOW)
+    named.normed[chip] = normed.reshape(named.normed.shape[1:])
+    query = times_trans(normed, named.w_query[...])
+    pair = [
+        times_trans(normed, named.kv_all[:, 0, index].reshape(HEAD_DIM, normed.shape[1]))
+        for index in range(2)
+    ]
+    named.qkv[chip] = jnp.concatenate([query, *pair], 1)
+
+
+def local_middle(named, total):
+    hidden_in = named.x_rows[...].astype(FULL) + total
+    named.hidden_in[...] = hidden_in
+    return scaled(hidden_in, named.gain[...]).astype(LOW)
+
+
+def local_next(named, total):
+    result = (named.hidden_in[...] + total).astype(LOW)
+    named.result[...] = result
+    return scaled(result.astype(FULL), named.gain[...]).astype(LOW)
+
+
+def local_last(named, total):
+    named.result[...] = (named.hidden_in[...] + total).astype(LOW)
+
+
+def local_top(named, total):
+    return named.top_rows[...]
+
+
+def norm_back_rows(values, gain_vec, grad_in):
+    factor = lax.rsqrt(jnp.mean(values * values, -1, keepdims=True) + EPSILON)
+    gain_grad = jnp.sum(grad_in * values * factor, 0, keepdims=True)
+    mean_term = jnp.mean(grad_in * gain_vec * values, -1, keepdims=True)
+    return (
+        gain_grad,
+        factor * gain_vec * grad_in - values * (factor * factor * factor) * mean_term,
+    )
+
+
+def local_branch(named, total):
+    gain_grad, d_hidden = norm_back_rows(named.hidden_in[...], named.gain[...], total)
+    d_hidden = d_hidden + named.top_rows[...].astype(FULL)
+    named.gain_grad[...] = gain_grad
+    named.d_hidden[...] = d_hidden
+    return d_hidden.astype(LOW)
+
+
+def local_input(named, total):
+    gain_grad, d_input = norm_back_rows(
+        named.x_rows[...].astype(FULL), named.gain[...], total
+    )
+    d_input = (d_input + named.d_hidden[...]).astype(LOW)
+    named.gain_grad[...] = gain_grad
+    named.d_input[...] = d_input
+    return d_input
+
+
+def swap_halves(value):
+    width = value.shape[1]
+    half = HEAD_DIM // 2
+    lane = lax.broadcasted_iota(jnp.int32, value.shape, 1)
+    return jnp.where(
+        lax.rem(lane, HEAD_DIM) < half,
+        pltpu.roll(value, width - half, 1),
+        pltpu.roll(value, half, 1),
+    )
+
+
+def stacked(pair):
+    return jnp.concatenate([pair[:, :HEAD_DIM], pair[:, HEAD_DIM:]], 0)
+
+
+def side_by_side(turned):
+    return jnp.concatenate([turned[:, :PLACE], turned[:, PLACE:]], 0).T
+
+
+def hide_later(scores, fill):
+    last = scores[-PLACE:]
+    key = lax.broadcasted_iota(jnp.int32, last.shape, 0)
+    query = lax.rem(lax.broadcasted_iota(jnp.int32, last.shape, 1), PLACE)
+    last = jnp.where(key <= query, last, fill)
+    if scores.shape[0] == PLACE:
+        return last
+    return jnp.concatenate([scores[:-PLACE], last], 0)
+
+
+def turn_of(turns, place):
+    near, far = pl.ds(0, PLACE), pl.ds(PLACE + place, 1)
+    cos_near, sin_near = turns[0, near], turns[1, near]
+    cos_far, sin_far = turns[0, far], turns[1, far]
+    cosine = cos_near * cos_far - sin_near * sin_far
+    sine = sin_near * cos_far + cos_near * sin_far
+    lane = lax.broadcasted_iota(jnp.int32, cosine.shape, 1)
+    sine = jnp.where(lax.rem(lane, HEAD_DIM) < HEAD_DIM // 2, -sine, sine)
+    keyed = lane < HEAD_DIM
+    return (
+        jnp.concatenate([cosine, jnp.where(keyed, cosine, 1.0)], 1),
+        jnp.concatenate([sine, jnp.where(keyed, sine, 0.0)], 1),
+    )
+
+
+def attend_kernel(block_at, qkv, turns, mixed, turned, attended, spread, values_t):
+    q_width = 2 * HEAD_DIM
+    for place in range(CHIPS):
+        at = pl.ds(place * PLACE, PLACE)
+        value = qkv[block_at[place]]
+        cosine, sine = turn_of(turns, place)
+        value = value * cosine + swap_halves(value) * sine
+        value = value.astype(LOW)
+        scale = jnp.asarray(1.0 / math.sqrt(HEAD_DIM), LOW)
+        turned[at, :q_width] = value[:, :q_width] * scale
+        turned[at, q_width:] = value[:, q_width:]
+        values_t[:, at] = value[:, q_width:].astype(FULL).T[HEAD_DIM:].astype(LOW)
+    for place in range(CHIPS):
+        at = pl.ds(place * PLACE, PLACE)
+        keys = pl.ds(0, (place + 1) * PLACE)
+        query = stacked(turned[at, :q_width])
+        scores = times_trans(turned[keys, q_width : q_width + HEAD_DIM], query)
+        scores = hide_later(scores, NEG_LARGE)
+        top = jnp.max(scores, 0, keepdims=True)
+        weight = jnp.exp(scores - top)
+        total = jnp.sum(weight, 0, keepdims=True)
+        out = plain_dot(values_t[:, keys], weight.astype(LOW)) / total
+        out = side_by_side(out)
+        attended[at] = out
+        mixed[block_at[place]] = out.astype(LOW).reshape(mixed.shape[1:])
+        spread[pl.ds(place, 1)] = top + jnp.log(total)
+
+
+def attend_back_kernel(
+    block_at, d_mixed, turns, turned, attended, spread, d_qkv, keys_t, d_query, d_key, d_value
+):
+    q_width = 2 * HEAD_DIM
+    d_key[...] = jnp.zeros_like(d_key)
+    d_value[...] = jnp.zeros_like(d_value)
+    for place in range(CHIPS):
+        at = pl.ds(place * PLACE, PLACE)
+        keys_t[:, at] = turned[at, q_width:].astype(FULL).T[:HEAD_DIM].astype(LOW)
+    for place in range(CHIPS):
+        at = pl.ds(place * PLACE, PLACE)
+        keys = pl.ds(0, (place + 1) * PLACE)
+        d_out = d_mixed[block_at[place]]
+        product = (d_out.astype(FULL) * attended[at]).T
+        offset = jnp.concatenate(
+            [
+                jnp.sum(product[:HEAD_DIM], 0, keepdims=True),
+                jnp.sum(product[HEAD_DIM:], 0, keepdims=True),
+            ],
+            1,
+        )
+        d_out = stacked(d_out)
+        query = stacked(turned[at, :q_width])
+        scores = times_trans(turned[keys, q_width : q_width + HEAD_DIM], query)
+        scores = hide_later(scores, NEG_LARGE)
+        probs = jnp.exp(scores - spread[pl.ds(place, 1)])
+        d_probs = times_trans(turned[keys, q_width + HEAD_DIM :], d_out)
+        d_scores = (probs * (d_probs - offset)).astype(LOW)
+        d_key[keys] += plain_dot(d_scores, query)
+        d_value[keys] += plain_dot(probs.astype(LOW), d_out)
+        d_query[at] = side_by_side(plain_dot(keys_t[:, keys], d_scores)) * (
+            1.0 / math.sqrt(HEAD_DIM)
+        )
+    for place in range(CHIPS):
+        at = pl.ds(place * PLACE, PLACE)
+        value = jnp.concatenate([d_query[at], d_key[at], d_value[at]], 1)
+        cosine, sine = turn_of(turns, place)
+        value = value * cosine - swap_halves(value) * sine
+        d_qkv[block_at[place]] = value.astype(LOW).reshape(d_qkv.shape[1:])
+
+
+def plain_call(kernel, name, count, out_shape, scratch):
+    return pl.pallas_call(
+        kernel,
+        out_shape=out_shape,
+        in_specs=[pl.BlockSpec(memory_space=pltpu.SMEM)] + [IN_VMEM] * (count - 1),
+        out_specs=[IN_VMEM] * len(out_shape),
+        scratch_shapes=scratch,
+        compiler_params=pltpu.CompilerParams(vmem_limit_bytes=48 * 2**20),
+        cost_estimate=pl.CostEstimate(flops=2**33, bytes_accessed=2**23, transcendentals=2**21),
+        name=name,
+    )
+
+
+def relay_body(
+    inputs,
+    cotangent,
+    positions,
+    gain_attn,
+    w_query,
+    w_key,
+    w_value,
+    w_out,
+    gain_ffn,
+    w_gate,
+    w_up,
+    w_down,
+):
+    n_micro, per_device, model_width = inputs.shape
+    n_seq = lax.axis_size("seq")
+    n_shard = lax.axis_size("shard")
+    members = n_seq * n_shard
+    total_len = members * per_device
+    section_idx = lax.axis_index("section")
+    q_width = HEADS // members * HEAD_DIM
+    in_width = q_width + 2 * HEAD_DIM
+    hidden = w_down.shape[1]
+    shape = jax.ShapeDtypeStruct
+
+    def swap(value):
+        return lax.ppermute(value, "section", [(0, 1), (1, 0)])
+
+    def pick(first, second):
+        return jnp.where(section_idx == 0, first, second)
+
+    rows_in = pick(inputs[0], inputs[1])
+    top_in = pick(cotangent[0], cotangent[1])
+    places = pick(positions[0], positions[1])
+
+    small = jnp.concatenate([gain_attn, gain_ffn], 0).astype(FULL)
+    small = jnp.concatenate([small, jnp.zeros((6, small.shape[1]), FULL)], 0)
+    kv_pair = jnp.stack([w_key[0], w_value[0]])
+
+    def w_in_of(layer):
+        return [(w_query[0], x_query, layer), (kv_all[layer], kv_all[layer], layer)]
+
+    order = places.reshape(CHIPS, PLACE)[:, 0] // PLACE
+    block_at = jnp.sum(
+        jnp.where(
+            order[None, :] == jnp.arange(CHIPS)[:, None], jnp.arange(CHIPS)[None, :], 0
+        ),
+        1,
+    ).astype(jnp.int32)
+    half_dim = HEAD_DIM // 2
+    inv_freq = THETA_BASE ** (-jnp.arange(half_dim, dtype=FULL) * (2.0 / HEAD_DIM))
+    steps = jnp.concatenate([jnp.arange(PLACE), PLACE * jnp.arange(CHIPS)]).astype(FULL)
+    angles = steps[:, None] * jnp.tile(inv_freq, 2 * q_width // HEAD_DIM)[None, :]
+    turns = jnp.stack([jnp.cos(angles), jnp.sin(angles)])
+
+    narrow = (CHIPS, 2, per_device, hidden)
+    chip_rows = 2 * per_device
+    act_outs = dict(act=(narrow, LOW), gate_slope=(narrow, LOW), up_slope=(narrow, LOW))
+    back_outs = dict(d_gate=(narrow, LOW), d_up=(narrow, LOW))
+    qkv_out = dict(qkv=((CHIPS, chip_rows, in_width), FULL))
+    row_low = ((per_device, model_width), LOW)
+    row_full = ((per_device, model_width), FULL)
+    gain_out = ((1, model_width), FULL)
+
+    def flat(value):
+        return value.reshape(total_len, value.shape[-1])
+
+    def attend(qkv):
+        mixed, *saved = plain_call(
+            attend_kernel,
+            "attend",
+            3,
+            [
+                shape((CHIPS, 2, per_device, q_width), LOW),
+                shape((total_len, in_width), LOW),
+                shape((total_len, q_width), FULL),
+                shape((CHIPS, 2 * PLACE), FULL),
+            ],
+            [pltpu.VMEM((HEAD_DIM, total_len), LOW)],
+        )(block_at, qkv, turns)
+        return mixed, saved
+
+    def attend_back(saved, d_mixed):
+        (d_qkv,) = plain_call(
+            attend_back_kernel,
+            "attend_back",
+            6,
+            [shape((CHIPS, 2, per_device, in_width), LOW)],
+            [
+                pltpu.VMEM((HEAD_DIM, total_len), LOW),
+                pltpu.VMEM((total_len, q_width), FULL),
+                pltpu.VMEM((total_len, HEAD_DIM), FULL),
+                pltpu.VMEM((total_len, HEAD_DIM), FULL),
+            ],
+        )(block_at, d_mixed, turns, *saved)
+        return d_qkv
+
+    def middle(layer, mixed, x_rows, w_gate_set, w_up_set, cross=()):
+        return ring_call(
+            "attn_out_to_ffn",
+            1 + 7 * layer,
+            dict(like=x_rows, x_rows=x_rows, mixed=mixed, gain=gains[layer, 1]),
+            dict(w_out=[(w_out[0], x_out, layer)]),
+            dict(w_gate=[(*w_gate_set, layer)], w_up=[(*w_up_set, layer)]),
+            dict(hidden_in=row_full, **act_outs),
+            local_middle,
+            fold=fold_mixed,
+            use=use_gate_up,
+            cross=cross,
+        )
+
+    def middle_back(layer, d_gate, d_up, hidden_in, top_rows, after=()):
+        return ring_call(
+            "ffn_back_to_attn",
+            2 + 7 * layer,
+            dict(
+                like=top_rows,
+                d_gate=d_gate,
+                d_up=d_up,
+                hidden_in=hidden_in,
+                top_rows=top_rows,
+                gain=gains[layer, 1],
+            ),
+            dict(w_gate=[(w_gate[0], x_gate, layer)], w_up=[(w_up[0], x_up, layer)]),
+            dict(w_out=[(w_out[0], x_out, layer)]),
+            dict(
+                gain_grad=gain_out,
+                d_hidden=row_full,
+                d_mixed=((CHIPS, chip_rows, q_width), LOW),
+            ),
+            local_branch,
+            fold=fold_d_act,
+            use=use_d_mixed,
+            after=after,
+        )
+
+    qkv, gains_all, kv_all, x_query, x_out, normed_one_a = ring_call(
+        "first_rows",
+        0,
+        dict(like=rows_in, x_rows=rows_in, gains_own=small, kv_own=kv_pair),
+        {},
+        dict(w_query=[("x_query", 0)]),
+        dict(
+            **qkv_out,
+            gains_all=((CHIPS, 2, *small.shape), FULL),
+            kv_all=((n_seq, 2, *kv_pair.shape), LOW),
+        ),
+        local_start,
+        use=use_first,
+        extra=dict(
+            gain_row=pltpu.VMEM((1, model_width), FULL),
+            small_send=pltpu.SemaphoreType.DMA((SMALL_SEMS,)),
+            small_recv=pltpu.SemaphoreType.DMA((SMALL_SEMS,)),
+            kv_send=pltpu.SemaphoreType.DMA((n_seq - 1,)),
+            kv_recv=pltpu.SemaphoreType.DMA((n_seq - 1,)),
+            gains_x=pltpu.VMEM(small.shape, FULL),
+            kv_x=pltpu.VMEM(kv_pair.shape, LOW),
+            small_x_send=pltpu.SemaphoreType.DMA((2,)),
+            small_x_recv=pltpu.SemaphoreType.DMA((2,)),
+        ),
+        normed=True,
+        cross=[dict(x_query=w_query[0]), dict(x_out=w_out[0])],
+        meanwhile=gather_small,
+        peers=True,
+    )
+    gains = gains_all.reshape(members, -1, gain_attn.shape[1])[:, :4]
+    gains = gains.transpose(1, 0, 2).reshape(2, 2, 1, model_width)
+    kv_all = kv_all.transpose(1, 2, 0, 3, 4).reshape(2, 2 * HEAD_DIM, model_width)
+    mixed_a, saved_a = attend(qkv)
+    hidden_a, act_a, gate_slope_a, up_slope_a, x_gate, x_up, x_down, normed_two_a = middle(
+        0,
+        mixed_a,
+        rows_in,
+        ("x_gate",),
+        ("x_up",),
+        [dict(x_gate=w_gate[0], x_up=w_up[0]), dict(x_down=w_down[0])],
+    )
+    result_a, qkv, normed_one_b = ring_call(
+        "ffn_to_next",
+        3,
+        dict(like=rows_in, act=act_a, hidden_in=hidden_a, gain=gains[1, 0]),
+        dict(w_down=[(w_down[0], x_down, 0)]),
+        dict(w_in=w_in_of(1)),
+        dict(result=row_low, **qkv_out),
+        local_next,
+        fold=fold_act,
+        use=use_qkv,
+    )
+    mixed_b, saved_b = attend(qkv)
+    hidden_b, act_b, gate_slope_b, up_slope_b, normed_two_b = middle(
+        1, mixed_b, result_a, (w_gate[0], x_gate), (w_up[0], x_up)
+    )
+
+    def join_to(layer, own):
+        pairs = [(0, 1)] if layer else [(1, 0)]
+        return own, lax.ppermute(own, "section", pairs)
+
+    def ffn_sums(layer, act, top_all, d_gate, d_up, normed_two):
+        return [
+            join_to(layer, outer_sum(flat(left), flat(right)).astype(LOW))
+            for left, right in ((act, top_all), (d_gate, normed_two), (d_up, normed_two))
+        ]
+
+    def attn_sums(layer, mixed, branch_all, d_qkv, normed_one):
+        g_in = outer_sum(flat(d_qkv), flat(normed_one)).astype(LOW)
+        kv = g_in[q_width:].reshape(2, n_seq, -1, model_width)
+        kv = lax.all_to_all(kv, "seq", split_axis=1, concat_axis=1, tiled=True)
+        kv = jnp.sum(kv.astype(FULL), 1).astype(LOW)
+        g_out = outer_sum(flat(mixed), flat(branch_all)).astype(LOW)
+        return [join_to(layer, value) for value in (g_out, g_in[:q_width], kv)]
+
+    def came_of(sums):
+        return [came for _, came in sums]
+
+    (result_b,) = ring_call(
+        "ffn_last",
+        4,
+        dict(like=rows_in, act=act_b, hidden_in=hidden_b),
+        dict(w_down=[(w_down[0], x_down, 1)]),
+        {},
+        dict(result=row_low),
+        local_last,
+        fold=fold_act,
+    )
+    d_gate_b, d_up_b, top_all_b = ring_call(
+        "top_rows",
+        5,
+        dict(like=top_in, top_rows=top_in, gate_slope=gate_slope_b, up_slope=up_slope_b),
+        {},
+        dict(w_down=[(w_down[0], x_down, 1)]),
+        back_outs,
+        local_top,
+        use=use_d_act,
+    )
+    ffn_b = ffn_sums(1, act_b, top_all_b, d_gate_b, d_up_b, normed_two_b)
+    gain_ffn_b, d_hidden_b, d_mixed, branch_all_b = middle_back(
+        1, d_gate_b, d_up_b, hidden_b, top_in
+    )
+    d_qkv_b = attend_back(saved_b, d_mixed)
+    attn_b = attn_sums(1, mixed_b, branch_all_b, d_qkv_b, normed_one_b)
+    gain_attn_b, back_b, d_gate_a, d_up_a, top_all_a = ring_call(
+        "attn_back_to_prev",
+        6,
+        dict(
+            like=top_in,
+            d_qkv=d_qkv_b,
+            x_rows=result_a,
+            d_hidden=d_hidden_b,
+            gain=gains[1, 0],
+            gate_slope=gate_slope_a,
+            up_slope=up_slope_a,
+        ),
+        dict(w_in=w_in_of(1)),
+        dict(w_down=[(w_down[0], x_down, 0)]),
+        dict(gain_grad=gain_out, d_input=row_low, **back_outs),
+        local_input,
+        fold=fold_d_qkv,
+        use=use_d_act,
+    )
+    ffn_a = ffn_sums(0, act_a, top_all_a, d_gate_a, d_up_a, normed_two_a)
+    gain_ffn_a, d_hidden_a, d_mixed, branch_all_a = middle_back(
+        0, d_gate_a, d_up_a, hidden_a, back_b, after=came_of(ffn_b)
+    )
+    d_qkv_a = attend_back(saved_a, d_mixed)
+    attn_a = attn_sums(0, mixed_a, branch_all_a, d_qkv_a, normed_one_a)
+    gain_attn_a, back_a = ring_call(
+        "attn_back_last",
+        7,
+        dict(like=top_in, d_qkv=d_qkv_a, x_rows=rows_in, d_hidden=d_hidden_a, gain=gains[0, 0]),
+        dict(w_in=w_in_of(0)),
+        {},
+        dict(gain_grad=gain_out, d_input=row_low),
+        local_input,
+        fold=fold_d_qkv,
+        after=came_of(attn_b),
+    )
+
+    def joined(first, second):
+        came = swap(pick(second, first))
+        kept = pick(first, second)
+        return pick(jnp.stack([kept, came]), jnp.stack([came, kept]))[None]
+
+    outputs = joined(result_a, result_b)
+    input_grads = joined(back_a, back_b)
+
+    g_down, g_gate, g_up, g_out, g_query, g_kv = (
+        pick(own_a, own_b).astype(FULL) + pick(came_a, came_b).astype(FULL)
+        for (own_a, came_a), (own_b, came_b) in zip(ffn_a + attn_a, ffn_b + attn_b)
+    )
+    gain_grads = jnp.concatenate([gain_attn_a, gain_ffn_a, gain_attn_b, gain_ffn_b], 0)
+    gain_grads = gain_grads.reshape(2, 2, members, -1).transpose(0, 2, 1, 3)
+    gain_grads = lax.all_to_all(
+        gain_grads.reshape(2 * members, 2, -1),
+        ("section", "shard", "seq"),
+        split_axis=0,
+        concat_axis=0,
+        tiled=True,
+    )
+    gain_grads = jnp.sum(gain_grads, 0, keepdims=True)
+    return (
+        outputs,
+        input_grads,
+        gain_grads[:, 0],
+        g_query[None],
+        g_kv[:1],
+        g_kv[1:],
+        g_out[None],
+        gain_grads[:, 1],
+        g_gate[None],
+        g_up[None],
+        g_down[None],
+    )
+
+
+def fits_relay(mesh):
+    shape = mesh.shape
+    return shape["section"] == 2 and shape["shard"] == KV_HEADS == RING and shape["seq"] == 4
+
+
 def solution(mesh):
     in_specs = (
         P(None, ("shard", "seq"), None),
@@ -435,4 +1478,5 @@
         P("section", ("shard", "seq"), None),
         P("section", ("shard", "seq"), None),
     )
-    return jax.shard_map(body, mesh=mesh, in_specs=in_specs, out_specs=out_specs, check_vma=False)
+    chosen = relay_body if fits_relay(mesh) else body
+    return jax.shard_map(chosen, mesh=mesh, in_specs=in_specs, out_specs=out_specs, check_vma=False)

time: 2390 us -> 740 us (0.31)
  waiting for transfers between devices: 1420 us -> 9.37 us
  Pallas kernels: 0 us -> 595 us
  blocking collectives: 293 us -> 0 us
  matrix products: 316 us -> 29.7 us
  local copies, waits for them, and re-layouts: 153 us -> 16.4 us
  other arithmetic: 120 us -> 33.2 us
    reduce_scatter x16 -> x0, waiting for transfers between devices: 962 us -> none  [the longest x6 546 us: fold_rows(): lax.psum_scatter(block_in, ('shard', 'seq'), scatter_dimension=0, tiled=T...]
    pallas_call x0 -> x14, Pallas kernels: none -> 595 us  [the longest x10 577 us: ring_call(): pl.pallas_call(functools.partial(ring_kernel, spec), out_shape=out_shape,...]
    all_gather x10 -> x0, waiting for transfers between devices: 407 us -> none  [the longest x6 282 us: spread_rows(): return lax.all_gather(block_in, ('shard', 'seq'), axis=0, tiled=True)]
    dot_general x63 -> x0, matrix products: 264 us -> none  [the longest x21 88 us: plain_dot(): return jnp.dot(left, right, preferred_element_type=jnp.float32)]
    all_gather x14 -> x0, blocking collectives: 212 us -> none  [the longest x6 84.3 us: over_keys(): lax.all_gather(head_values, 'shard', axis=0, tiled=True)]
    unnamed x329 -> x91, local copies, waits for them, and re-layouts: 84.7 us -> 5.56 us
    unnamed x1 -> x0, blocking collectives: 59.2 us -> none
    all_to_all x13 -> x3, starting transfers between devices: 51 us -> 15.2 us  [the longest x2 8.07 us: attn_sums(): kv = lax.all_to_all(kv, 'seq', split_axis=1, concat_axis=1, tiled=True)]
  transfers between devices with their start and end apart: 43 -> 17, of which waited for: 31 -> 2; matrix products, arithmetic and copies ran while one was open for 10% -> 8% of each run, Pallas kernels for 0% -> 36%
where the time goes in v1:
time: 740 us; the launch traced here: 730 us
  Pallas kernels  595 us (80%)
  starting transfers between devices  45 us (6%)
  other arithmetic  33.2 us (4%)
  matrix products  29.7 us (4%)
  local copies, waits for them, and re-layouts  16.4 us (2%)
  waiting for transfers between devices  9.37 us (1%)
    pallas_call x10, Pallas kernels, ring_call(): pl.pallas_call(functools.partial(ring_kernel, spec), out_shape=out_shape,...  577 us
    dot_general x10, matrix products, outer_sum(): lax.dot_general(left, right, (((0,), (0,)), ((), ())), preferred_element_...  29.7 us
    ppermute x12, starting transfers between devices, join_to(): return (own, lax.ppermute(own, 'section', pairs))  26.8 us
  transfers between devices with their start and end apart: 17, of which 2 were waited for; matrix products, arithmetic and copies ran while one was open for 8% of the time, Pallas kernels for 36%

profile of v1, /device:TPU:0, one launch (start us, length us, event | category | flops | bytes accessed | tf_op | source)
XLA Modules:
  0.0 730.3 jit_solution(11170858904239181437)
XLA Ops:
  1.8 1.8 select_bitcast_fusion.3.refs_0_.refs_1_
  4.8 1.5 pad_maximum_fusion.1.refs_2_
  6.4 63.6 %first_rows.1 = (f32[8,128,256]{2,1,0:T(8,128)}, f32[8,2,8,128]{3,2,1,0:T(8,128)}, bf16[4,2,2,16,2048]{4,3,2,1,0:T(8,128)(2,1)}, bf16[128,2048]{1,0:T(8,128)(2,1...) custom-call(bf16[64,2048]{1,0:T(8,128)(2,1)} %select_bitcast_fusion.3.refs_0_.refs_1_, ...), custom_call_target="tpu_custom_call" | custom-call | flops 34359738368 | bytes 8388608 | tf_op jit(solution)/shard_map/first_rows/pallas_call | solution.py:835
  71.5 2.1 fusion.16
  74.8 4.7 attend.2
  80.2 100.6 %attn_out_to_ffn.2 = (f32[64,2048]{1,0:T(8,128)}, bf16[8,2,64,352]{3,2,1,0:T(8,128)(2,1)}, bf16[8,2,64,352]{3,2,1,0:T(8,128)(2,1)}, bf16[8,2,64,352]{3,2,1,0:T(8...) custom-call(bf16[64,2048]{1,0:T(8,128)(2,1)} %select_bitcast_fusion., ...), custom_call_target="tpu_custom_call" | custom-call | flops 68719476736 | bytes 8388608 | tf_op jit(solution)/shard_map/attn_out_to_ffn/pallas_call | solution.py:835
  180.8 62.5 %ffn_to_next.1 = (bf16[64,2048]{1,0:T(8,128)(2,1)}, f32[8,128,256]{2,1,0:T(8,128)}, bf16[8,2,64,2048]{3,2,1,0:T(8,128)(2,1)}) custom-call(bf16[8,2,64,352]{3,2,1,0:T(8,128)(2,1)} %get-tuple-element.63.refs_0_, f32[64,2048]{1,0:T(8,128)} %get-tuple-element.64.refs_1_.refs_2_, f32[1,2048]{1,0:T(1,128)} %get-tuple-element.121.refs_2_.refs_3_, ...), custom_call_target="tpu_custom_call" | custom-call | flops 68719476736 | bytes 8388608 | tf_op jit(solution)/shard_map/ffn_to_next/pallas_call | solution.py:835
  244.6 4.7 attend.3
  250.0 62.4 %attn_out_to_ffn.3 = (f32[64,2048]{1,0:T(8,128)}, bf16[8,2,64,352]{3,2,1,0:T(8,128)(2,1)}, bf16[8,2,64,352]{3,2,1,0:T(8,128)(2,1)}, bf16[8,2,64,352]{3,2,1,0:T(8,128)(2,1)}, bf16[8,2,64,2048]{3,2,1,0:T(8,128)(2,1)}) custom-call(bf16[64,2048]{1,0:T(8,128)(2,1)} %get-tuple-element.68.refs_0_.refs_1_, bf16[8,2,64,128]{3,2,1,0:T(8,128)(2,1)} %copy-done.5, ...), custom_call_target="tpu_custom_call" | custom-call | flops 68719476736 | bytes 8388608 | tf_op jit(solution)/shard_map/attn_out_to_ffn/pallas_call | solution.py:835
  312.4 33.6 %ffn_last.1 = bf16[64,2048]{1,0:T(8,128)(2,1)} custom-call(bf16[8,2,64,352]{3,2,1,0:T(8,128)(2,1)} %get-tuple-element.73.refs_0_, f32[64,2048]{1,0:T(8,128)} %get-tuple-element.74.refs_1_.refs_2_, bf16[352,2048]{1,0:T(8,128)(2,1)} %bitcast.161, bf16[352,2048]{1,0:T(8,128)(2,1)} %get-tuple-element.66.refs_6_.refs_3_.refs_4_.refs_11_), custom_call_target="tpu_custom_call" | custom-call | flops 34359738368 | bytes 8388608 | tf_op jit(solution)/shard_map/ffn_last/pallas_call | solution.py:835
  346.0 1.8 select_bitcast_fusion.2
  349.8 32.5 %top_rows.1 = (bf16[8,2,64,352]{3,2,1,0:T(8,128)(2,1)}, bf16[8,2,64,352]{3,2,1,0:T(8,128)(2,1)}, bf16[8,2,64,2048]{3,2,1,0:T(8,128)(2,1)}) custom-call(bf16[64,2048]{1,0:T(8,128)(2,1)} %select_bitcast_fusion.1.refs_0_.refs_3_, bf16[8,2,64,352]{3,2,1,0:T(8,128)(2,1)} %get-tuple-element.75.refs_1_, bf16[8,2,64,352]{3,2,1,0:T(8,128)(2,1)} %get-tuple-element.76.refs_2_, ...), custom_call_target="tpu_custom_call" | custom-call | flops 34359738368 | bytes 8388608 | tf_op jit(solution)/shard_map/top_rows/pallas_call | solution.py:835
  382.4 4.1 fusion.2
  386.5 3.0 collective-permute-start.3
  389.5 2.8 fusion.1
  392.3 2.6 collective-permute-start.2
  395.0 2.9 fusion
  397.9 2.5 collective-permute-start.1
  400.4 61.9 %ffn_back_to_attn.2 = (f32[1,2048]{1,0:T(1,128)}, f32[64,2048]{1,0:T(8,128)}, bf16[8,128,128]{2,1,0:T(8,128)(2,1)}, bf16[8,2,64,2048]{3,2,1,0:T(8,128)(2,1)}) custom-call(bf16[8,2,64,352]{3,2,1,0:T(8,128)(2,1)} %get-tuple-element.77.refs_0_, bf16[8,2,64,352]{3,2,1,0:T(8,128)(2,1)} %get-tuple-element.78.refs_1_, ...), custom_call_target="tpu_custom_call" | custom-call | flops 68719476736 | bytes 8388608 | tf_op jit(solution)/shard_map/ffn_back_to_attn/pallas_call | solution.py:835
  462.3 3.8 fusion.8
  466.1 2.1 collective-permute-start.4
  468.2 4.5 attend_back.2.refs_0_
  476.0 4.5 all-to-all-start
  480.5 62.2 %attn_back_to_prev.1 = (f32[1,2048]{1,0:T(1,128)}, bf16[64,2048]{1,0:T(8,128)(2,1)}, bf16[8,2,64,352]{3,2,1,0:T(8,128)(2,1)}, bf16[8,2,64,352]{3,2,1,0:T(8,128)(2,1)}, bf16[8,2,64,2048]{3,2,1,0:T(8,128)(2,1)}) custom-call(bf16[8,2,64,256]{3,2,1,0:T(8,128)(2,1)} %copy-done.2, bf16[64,2048]{1,0:T(8,128)(2,1)} %get-tuple-element.68.refs_0_.refs_1_, ...), custom_call_target="tpu_custom_call" | custom-call | flops 68719476736 | bytes 8388608 | tf_op jit(solution)/shard_map/attn_back_to_prev/pallas_call | solution.py:835
  542.7 4.0 fusion.5
  546.8 2.9 fusion.4
  549.7 2.8 fusion.3
  554.7 1.9 maximum_select_fusion
  559.9 7.0 collective-permute-start.6
  566.9 63.4 %ffn_back_to_attn.3 = (f32[1,2048]{1,0:T(1,128)}, f32[64,2048]{1,0:T(8,128)}, bf16[8,128,128]{2,1,0:T(8,128)(2,1)}, bf16[8,2,64,2048]{3,2,1,0:T(8,128)(2,1)}) custom-call(bf16[8,2,64,352]{3,2,1,0:T(8,128)(2,1)} %get-tuple-element.86.refs_0_, bf16[8,2,64,352]{3,2,1,0:T(8,128)(2,1)} %get-tuple-element.87.refs_1_, ...), custom_call_target="tpu_custom_call" | custom-call | flops 68719476736 | bytes 8388608 | tf_op jit(solution)/shard_map/ffn_back_to_attn/pallas_call | solution.py:835
  631.3 4.4 attend_back.3.refs_0_
  636.5 1.5 collective-permute-start.13
  638.9 34.0 %attn_back_last.1 = (f32[1,2048]{1,0:T(1,128)}, bf16[64,2048]{1,0:T(8,128)(2,1)}) custom-call(bf16[8,2,64,256]{3,2,1,0:T(8,128)(2,1)} %copy-done, bf16[64,2048]{1,0:T(8,128)(2,1)} %select_bitcast_fusion.3.refs_0_.refs_1_, f32[64,2048]{1,0:T(8,128)} %get-tuple-element.95.refs_2_, f32[1,2048]{1,0:T(1,128)} %get-tuple-element.119.refs_3_, ...), custom_call_target="tpu_custom_call" | custom-call | flops 34359738368 | bytes 8388608 | tf_op jit(solution)/shard_map/attn_back_last/pallas_call | solution.py:835
  672.9 1.8 select_bitcast_fusion
  676.1 7.1 all-to-all-start.1
  683.2 1.8 collective-permute-start.7
  685.0 3.6 fusion.7
  688.6 1.6 fusion.9
  694.7 3.9 add_bitcast_fusion.2
  698.7 3.9 add_bitcast_fusion.1
  702.6 3.9 add_bitcast_fusion
  706.5 3.6 all-to-all-start.2
  711.4 2.1 maximum_select_fusion.1
  713.5 5.4 all-to-all-done.2
  719.0 1.4 collective-permute-start.9
  720.5 2.5 add_bitcast_fusion.3
  723.0 2.3 add_bitcast_fusion.4
  725.4 3.9 collective-permute-done.9
  (144 shorter events, 29.3 us)
Async XLA Ops:
  1.8 241.6 %copy-start.10 = (s32[8]{0:T(128)}, s32[8]{0:T(128)S(1)}, u32[]{:S(2)}) copy-start(s32[8]{0:T(128)S(1)} %select_reduce_fusion.block_at) | copy-start | bytes 100
  69.9 4.9 copy-start.13
  74.8 168.6 %copy-start.7 = (f32[2,136,128]{2,1,0:T(8,128)}, f32[2,136,128]{2,1,0:T(8,128)S(1)}, u32[]{:S(2)}) copy-start(f32[2,136,128]{2,1,0:T(8,128)S(1)} %pad_maximum_fusion.turns) | copy-start | bytes 417796
  312.4 33.6 %copy-start.38 = (bf16[64,2048]{1,0:T(8,128)(2,1)S(1)}, bf16[64,2048]{1,0:T(8,128)(2,1)}, u32[]{:S(2)}) copy-start(bf16[64,2048]{1,0:T(8,128)(2,1)} %get-tuple-element.68.refs_0_.refs_1_) | copy-start | bytes 786436
  312.4 36.7 %copy-start.33 = (bf16[2,64,2048]{2,1,0:T(8,128)(2,1)S(1)}, bf16[2,64,2048]{2,1,0:T(8,128)(2,1)}, u32[]{:S(2)}) copy-start(bf16[2,64,2048]{2,1,0:T(8,128)(2,1)} %param.13) | copy-start | bytes 1572868
  347.8 205.5 %collective-permute-start = (bf16[64,2048]{1,0:T(8,128)(2,1)}, bf16[64,2048]{1,0:T(8,128)(2,1)}, u32[]{:S(2)}, u32[]{:S(2)}) collective-permute-start(bf16[64,2048]{1,0:T(8,128)(2,1)} %get-tuple-element.116), channel_id=1, source_target_pairs={{0,16},{16,0},{1,17},{17,1},{2,18},{18,2},{3,19},{19,3},{4,20},{20... | collective-permute-start | bytes 786440 | tf_op jit(solution)/shard_map/ppermute | solution.py:1160
  349.8 32.6 %copy-start.18 = (bf16[8,2,64,2048]{3,2,1,0:T(8,128)(2,1)S(1)}, bf16[8,2,64,2048]{3,2,1,0:T(8,128)(2,1)}, u32[]{:S(2)}) copy-start(bf16[8,2,64,2048]{3,2,1,0:T(8,128)(2,1)} %get-tuple-element.90) | copy-start | bytes 12582916
  382.4 7.1 copy-start.32
  386.5 170.8 %collective-permute-start.3 = (bf16[352,2048]{1,0:T(8,128)(2,1)}, bf16[352,2048]{1,0:T(8,128)(2,1)}, u32[]{:S(2)}, u32[]{:S(2)}) collective-permute-start(bf16[352,2048]{1,0:T(8,128)(2,1)} %fusion.2), channel_id=1, source_target_pairs={{0,16},{1,17},{2,18},{3,19},{4,20},{5,21},{6,22},{7,23},{8,24},{9,... | collective-permute-start | bytes 4325384 | tf_op jit(solution)/shard_map/ppermute | solution.py:1329
  389.5 5.5 copy-start.25
  389.5 5.5 copy-start.31
  392.3 166.3 %collective-permute-start.2 = (bf16[352,2048]{1,0:T(8,128)(2,1)}, bf16[352,2048]{1,0:T(8,128)(2,1)}, u32[]{:S(2)}, u32[]{:S(2)}) collective-permute-start(bf16[352,2048]{1,0:T(8,128)(2,1)} %fusion.1), channel_id=1, source_target_pairs={{0,16},{1,17},{2,18},{3,19},{4,20},{5,21},{6,22},{7,23},{8,24},{9,... | collective-permute-start | bytes 4325384 | tf_op jit(solution)/shard_map/ppermute | solution.py:1329
  397.8 64.4 %copy-start.6 = (bf16[8,2,64,128]{3,2,1,0:T(8,128)(2,1)S(1)}, bf16[8,2,64,128]{3,2,1,0:T(8,128)(2,1)}, u32[]{:S(2)}) copy-start(bf16[8,2,64,128]{3,2,1,0:T(8,128)(2,1)} %copy-done.5) | copy-start | bytes 786436
  397.9 162.1 %collective-permute-start.1 = (bf16[352,2048]{1,0:T(8,128)(2,1)}, bf16[352,2048]{1,0:T(8,128)(2,1)}, u32[]{:S(2)}, u32[]{:S(2)}) collective-permute-start(bf16[352,2048]{1,0:T(8,128)(2,1)} %fusion), channel_id=1, source_target_pairs={{0,16},{1,17},{2,18},{3,19},{4,20},{5,21},{6,22},{7,23},{8,24},{9,... | collective-permute-start | bytes 4325384 | tf_op jit(solution)/shard_map/ppermute | solution.py:1329
  462.3 5.9 copy-start.8
  462.3 5.9 copy-start.11
  462.3 5.9 copy-start.15
  466.1 170.4 %collective-permute-start.4 = (bf16[128,2048]{1,0:T(8,128)(2,1)}, bf16[128,2048]{1,0:T(8,128)(2,1)}, u32[]{:S(2)}, u32[]{:S(2)}) collective-permute-start(bf16[128,2048]{1,0:T(8,128)(2,1)} %fusion.8), channel_id=1, source_target_pairs={{0,16},{1,17},{2,18},{3,19},{4,20},{5,21},{6,22},{7,23},{8,24},{9,... | collective-permute-start | bytes 1572872 | tf_op jit(solution)/shard_map/ppermute | solution.py:1329
  468.2 4.5 copy-start.24
  476.0 80.6 %all-to-all-start = ((bf16[2,4,16,2048]{3,2,0,1:T(8,128)(2,1)}), bf16[2,4,16,2048]{3,2,0,1:T(8,128)(2,1)S(1)}, u32[]{:S(2)}, u32[]{:S(2)}) async-start(bf16[2,4,16,2048]{3,2,0,1:T(8,128)(2,1)} %copy.43), calls=%async_computation | async-start | bytes 1048576 | tf_op jit(solution)/shard_map/all_to_all | solution.py:1340
  480.4 62.3 %copy-start.28 = (bf16[8,2,64,352]{3,2,1,0:T(8,128)(2,1)S(1)}, bf16[8,2,64,352]{3,2,1,0:T(8,128)(2,1)}, u32[]{:S(2)}) copy-start(bf16[8,2,64,352]{3,2,1,0:T(8,128)(2,1)} %get-tuple-element.63.refs_0_) | copy-start | bytes 2162692
  542.7 4.0 copy-start.17
  542.7 4.0 copy-start.30
  549.7 5.0 copy-start.27
  553.3 84.7 %collective-permute-start.5 = (bf16[128,2048]{1,0:T(8,128)(2,1)}, bf16[128,2048]{1,0:T(8,128)(2,1)S(1)}, u32[]{:S(2)}, u32[]{:S(2)}) collective-permute-start(bf16[128,2048]{1,0:T(8,128)(2,1)} %get-tuple-element.110), channel_id=1, source_target_pairs={{0,16},{1,17},{2,18},{3,19},{4,20},{5,21},{6,22},{7,23},{8,24},{9,... | collective-permute-start | bytes 1572872 | tf_op jit(solution)/shard_map/ppermute | solution.py:1329
  557.3 136.0 %collective-permute-start.11 = (bf16[352,2048]{1,0:T(8,128)(2,1)}, bf16[352,2048]{1,0:T(8,128)(2,1)}, u32[]{:S(2)}, u32[]{:S(2)}) collective-permute-start(bf16[352,2048]{1,0:T(8,128)(2,1)} %fusion.3), channel_id=1, source_target_pairs={{16,0},{17,1},{18,2},{19,3},{20,4},{21,5},{22,6},{23,7},{24,8},{25... | collective-permute-start | bytes 4325384 | tf_op jit(solution)/shard_map/ppermute | solution.py:1329
  558.6 140.1 %collective-permute-start.12 = (bf16[352,2048]{1,0:T(8,128)(2,1)}, bf16[352,2048]{1,0:T(8,128)(2,1)}, u32[]{:S(2)}, u32[]{:S(2)}) collective-permute-start(bf16[352,2048]{1,0:T(8,128)(2,1)} %fusion.4), channel_id=1, source_target_pairs={{16,0},{17,1},{18,2},{19,3},{20,4},{21,5},{22,6},{23,7},{24,8},{25... | collective-permute-start | bytes 4325384 | tf_op jit(solution)/shard_map/ppermute | solution.py:1329
  559.9 78.1 %collective-permute-start.6 = (bf16[2,16,2048]{2,1,0:T(8,128)(2,1)}, bf16[2,16,2048]{2,1,0:T(8,128)(2,1)S(1)}, u32[]{:S(2)}, u32[]{:S(2)}) collective-permute-start(bf16[2,16,2048]{2,1,0:T(8,128)(2,1)} %reduce_sum.43), channel_id=1, source_target_pairs={{0,16},{1,17},{2,18},{3,19},{4,20},{5,21},{6,22},{7,23},{8,24},{9,... | collective-permute-start | bytes 393224 | tf_op jit(solution)/shard_map/ppermute | solution.py:1329
  566.9 63.4 %copy-start.9 = (f32[2,136,128]{2,1,0:T(8,128)S(1)}, f32[2,136,128]{2,1,0:T(8,128)}, u32[]{:S(2)}) copy-start(f32[2,136,128]{2,1,0:T(8,128)} %copy-done.7) | copy-start | bytes 417796
  566.9 63.4 %copy-start.12 = (s32[8]{0:T(128)S(1)}, s32[8]{0:T(128)}, u32[]{:S(2)}) copy-start(s32[8]{0:T(128)} %copy-done.10) | copy-start | bytes 100
  636.5 66.1 %collective-permute-start.13 = (bf16[352,2048]{1,0:T(8,128)(2,1)S(1)}, bf16[352,2048]{1,0:T(8,128)(2,1)}, u32[]{:S(2)}, u32[]{:S(2)}) collective-permute-start(bf16[352,2048]{1,0:T(8,128)(2,1)S(1)} %fusion.5), channel_id=1, source_target_pairs={{16,0},{17,1},{18,2},{19,3},{20,4},{21,5},{22,6},{23,7},{24,8},{25... | collective-permute-start | bytes 4325384 | tf_op jit(solution)/shard_map/ppermute | solution.py:1329
  638.8 34.0 %copy-start.37 = (bf16[64,2048]{1,0:T(8,128)(2,1)S(1)}, bf16[64,2048]{1,0:T(8,128)(2,1)}, u32[]{:S(2)}) copy-start(bf16[64,2048]{1,0:T(8,128)(2,1)} %get-tuple-element.88.refs_3_) | copy-start | bytes 786436
  638.8 35.9 %copy-start.41 = (f32[1,2048]{1,0:T(1,128)S(1)}, f32[1,2048]{1,0:T(1,128)}, u32[]{:S(2)}) copy-start(f32[1,2048]{1,0:T(1,128)} %get-tuple-element.102) | copy-start | bytes 24580
  638.9 35.9 %copy-start.42 = (f32[1,2048]{1,0:T(1,128)S(1)}, f32[1,2048]{1,0:T(1,128)}, u32[]{:S(2)}) copy-start(f32[1,2048]{1,0:T(1,128)} %get-tuple-element.101) | copy-start | bytes 24580
  638.9 35.9 %copy-start.43 = (f32[1,2048]{1,0:T(1,128)S(1)}, f32[1,2048]{1,0:T(1,128)}, u32[]{:S(2)}) copy-start(f32[1,2048]{1,0:T(1,128)} %get-tuple-element.100) | copy-start | bytes 24580
  638.9 46.1 %copy-start.1 = (bf16[8,2,64,256]{3,2,1,0:T(8,128)(2,1)S(1)}, bf16[8,2,64,256]{3,2,1,0:T(8,128)(2,1)}, u32[]{:S(2)}) copy-start(bf16[8,2,64,256]{3,2,1,0:T(8,128)(2,1)} %copy-done) | copy-start | bytes 1572868
  676.1 30.4 %all-to-all-start.1 = ((f32[32,2,128]{2,1,0:T(2,128)}), f32[32,2,128]{2,1,0:T(2,128)}, u32[]{:S(2)}, u32[]{:S(2)}) async-start(f32[32,2,128]{2,1,0:T(2,128)} %copy.45), calls=%async_computation.1 | async-start | bytes 65536 | tf_op jit(solution)/shard_map/all_to_all | solution.py:1425
  683.2 28.2 %collective-permute-start.7 = (bf16[64,2048]{1,0:T(8,128)(2,1)}, bf16[64,2048]{1,0:T(8,128)(2,1)}, u32[]{:S(2)}, u32[]{:S(2)}) collective-permute-start(bf16[64,2048]{1,0:T(8,128)(2,1)} %get-tuple-element.114), channel_id=1, source_target_pairs={{0,16},{16,0},{1,17},{17,1},{2,18},{18,2},{3,19},{19,3},{4,20},{20... | collective-permute-start | bytes 786440 | tf_op jit(solution)/shard_map/ppermute | solution.py:1160
  690.2 4.6 copy-start.23
  690.2 30.3 %collective-permute-start.10 = (bf16[128,2048]{1,0:T(8,128)(2,1)}, bf16[128,2048]{1,0:T(8,128)(2,1)}, u32[]{:S(2)}, u32[]{:S(2)}) collective-permute-start(bf16[128,2048]{1,0:T(8,128)(2,1)} %fusion.9), channel_id=1, source_target_pairs={{16,0},{17,1},{18,2},{19,3},{20,4},{21,5},{22,6},{23,7},{24,8},{25... | collective-permute-start | bytes 1572872 | tf_op jit(solution)/shard_map/ppermute | solution.py:1329
  693.3 5.4 copy-start.22
  693.3 29.7 %collective-permute-start.8 = (bf16[128,2048]{1,0:T(8,128)(2,1)}, bf16[128,2048]{1,0:T(8,128)(2,1)}, u32[]{:S(2)}, u32[]{:S(2)}) collective-permute-start(bf16[128,2048]{1,0:T(8,128)(2,1)} %get-tuple-element.108), channel_id=1, source_target_pairs={{16,0},{17,1},{18,2},{19,3},{20,4},{21,5},{22,6},{23,7},{24,8},{25... | collective-permute-start | bytes 1572872 | tf_op jit(solution)/shard_map/ppermute | solution.py:1329
  706.5 16.5 %copy-start.21 = (bf16[256,2048]{1,0:T(8,128)(2,1)S(1)}, bf16[256,2048]{1,0:T(8,128)(2,1)}, u32[]{:S(2)}) copy-start(bf16[256,2048]{1,0:T(8,128)(2,1)} %copy-done.20) | copy-start | bytes 3145732
  706.5 16.5 %copy-start.35 = (bf16[128,2048]{1,0:T(8,128)(2,1)S(1)}, bf16[128,2048]{1,0:T(8,128)(2,1)}, u32[]{:S(2)}) copy-start(bf16[128,2048]{1,0:T(8,128)(2,1)} %copy-done.34) | copy-start | bytes 1572868
  706.5 12.4 %all-to-all-start.2 = ((bf16[2,4,16,2048]{3,2,0,1:T(8,128)(2,1)}), bf16[2,4,16,2048]{3,2,0,1:T(8,128)(2,1)S(1)}, u32[]{:S(2)}, u32[]{:S(2)}) async-start(bf16[2,4,16,2048]{3,2,0,1:T(8,128)(2,1)} %copy.46), calls=%async_computation.2 | async-start | bytes 1048576 | tf_op jit(solution)/shard_map/all_to_all | solution.py:1340
  719.0 10.3 %copy-start.36 = (bf16[2,16,2048]{2,1,0:T(8,128)(2,1)S(1)}, bf16[2,16,2048]{2,1,0:T(8,128)(2,1)}, u32[]{:S(2)}) copy-start(bf16[2,16,2048]{2,1,0:T(8,128)(2,1)} %reduce_sum.43) | copy-start | bytes 393220
  719.0 10.3 %copy-start.40 = (bf16[2,16,2048]{2,1,0:T(8,128)(2,1)S(1)}, bf16[2,16,2048]{2,1,0:T(8,128)(2,1)}, u32[]{:S(2)}) copy-start(bf16[2,16,2048]{2,1,0:T(8,128)(2,1)} %copy-done.39) | copy-start | bytes 393220
  719.0 10.2 %collective-permute-start.9 = (bf16[2,16,2048]{2,1,0:T(8,128)(2,1)S(1)}, bf16[2,16,2048]{2,1,0:T(8,128)(2,1)S(1)}, u32[]{:S(2)}, u32[]{:S(2)}) collective-permute-start(bf16[2,16,2048]{2,1,0:T(8,128)(2,1)S(1)} %reduce_sum.45), channel_id=1, source_target_pairs={{16,0},{17,1},{18,2},{19,3},{20,4},{21,5},{22,6},{23,7},{24,8},{25... | collective-permute-start | bytes 393224 | tf_op jit(solution)/shard_map/ppermute | solution.py:1329
  (13 other events, 21.2 us)

commit v2 on v1

--- a/solution.py
+++ b/solution.py
@@ -420,7 +420,7 @@
 PLACE = 128
 ORDER = ((2, 1), (1, 1), (3, 1), (0, 1), (2, 0), (1, 0), (3, 0), (0, 0))
 IN_VMEM = pl.BlockSpec(memory_space=pltpu.VMEM)
-ANYWHERE = pl.BlockSpec(memory_space=pl.ANY)
+IN_HBM = pl.BlockSpec(memory_space=pltpu.HBM)
 
 
 class Site:
@@ -435,6 +435,7 @@
         self.across = (self.section, self.z, (1 - self.y) * 2 + self.core)
         self.sibling = (self.section, self.z, self.y * 2 + 1 - self.core)
         self.corner = (self.section, self.z, (1 - self.y) * 2 + 1 - self.core)
+        self.opposite = (self.section, lax.rem(self.z + 2, RING), member)
         self.partner = (1 - self.section, self.z, member)
         self.member = member
 
@@ -474,14 +475,15 @@
 def greet(site, corner, partner):
     barrier = pltpu.get_barrier_semaphore()
     devices = [site.up, site.down, site.across, site.sibling]
-    devices += [site.corner] * corner + [site.partner] * partner
+    devices += [site.corner] * (corner > 0) + [site.partner] * partner
+    devices += [site.opposite] * (corner > 1)
     for device in devices:
         pl.semaphore_signal(barrier, inc=1, device_id=device, device_id_type=MESH)
     pl.semaphore_wait(barrier, len(devices))
 
 
 SPREAD_SEMS = 7 * SPLIT + CHIPS
-SMALL_SEMS = 7 + CHIPS
+SMALL_SEMS = 11
 FOLD_SEMS = 7 * SPLIT + CHIPS
 
 
@@ -530,28 +532,29 @@
     for part in range(parts):
         links.got(across + part, piece(y_own, part))
     share(3, y_own)
-    consume(0, own)
     for part in range(parts):
         go(y_far + part, links.got(relay + part, piece(far, part)), site.across)
     share(4, far)
+    yield
+    consume(0, own)
     consume(1, below)
-    consume(2, above)
-    consume(3, y_own)
     for part in range(parts):
         links.got(y_below + part, piece(yb, part))
         links.got(y_above + part, piece(ya, part))
     share(5, yb)
     share(6, ya)
+    consume(2, above)
+    consume(3, y_own)
     consume(4, far)
-    consume(5, yb)
-    consume(6, ya)
     for part in range(parts):
         links.got(y_far + part, piece(yf, part))
     share(7, yf)
+    consume(5, yb)
+    consume(6, ya)
     consume(7, yf)
 
 
-def fold_steps(site, part_of, mine, pass_out, pass_in, stage, land, links):
+def fold_steps(site, part_of, mine, pass_out, pass_in, stage, land, links, idle):
     rows = mine.shape[1]
     size = rows // SPLIT
     over, relay, up, down = CHIPS, CHIPS + 4 * SPLIT, CHIPS + 5 * SPLIT, CHIPS + 6 * SPLIT
@@ -599,10 +602,12 @@
     settle(4)
     compute(6)
     compute(7)
+    idle(4)
     for part in range(SPLIT):
         pass_on(part)
     for step in (5, 6, 7):
         settle(step)
+    idle(5)
     for part in range(SPLIT):
         where = pl.ds(part * size, size)
         for step, base, device in ((5, up, site.up), (6, down, site.down)):
@@ -612,6 +617,7 @@
                 value = value + came(relay + part, land.at[4, where])
             stage[step, where] = value.astype(LOW)
             links.go(base + part, stage.at[step, where], land.at[step, where], device)
+    idle(6)
     sums = []
     for part in range(SPLIT):
         where = pl.ds(part * size, size)
@@ -622,32 +628,90 @@
 
 
 class Cross:
-    def __init__(self, site, groups, src, dst, send, recv):
+    def __init__(self, site, groups, src, dst, ways, send, recv):
         self.links = Links(send, recv, site)
-        self.site, self.groups, self.src, self.dst = site, groups, src, dst
+        self.site, self.groups, self.src, self.dst, self.ways = site, groups, src, dst, ways
         self.started = 0
         self.landed = set()
-        self.start()
+
+    def where(self, index, receives, action):
+        layer = self.ways[index]
+        if layer is None:
+            action()
+        else:
+            pl.when((self.site.section == layer) == receives)(action)
+
+    def copy(self, index):
+        return self.links.copy(index, self.src[index], self.dst[index], self.site.partner)
+
+    def send(self, index):
+        self.where(index, False, self.copy(index).start)
 
     def start(self):
         if self.started < len(self.groups):
             for index in self.groups[self.started]:
-                self.links.go(index, self.src[index], self.dst[index], self.site.partner)
+                self.send(index)
             self.started += 1
 
     def wait(self, index):
         if index in self.landed:
             return
         self.landed.add(index)
-        self.links.got(index, self.dst[index])
-        if all(other in self.landed for other in self.groups[self.started - 1]):
+        self.where(index, True, self.copy(index).wait_recv)
+        if self.started and all(
+            other in self.landed for other in self.groups[self.started - 1]
+        ):
             self.start()
 
     def close(self):
-        for group in self.groups:
-            for index in group:
-                self.wait(index)
-        self.links.close()
+        for index in range(len(self.dst)):
+            self.wait(index)
+        for index in range(len(self.dst)):
+            self.where(index, False, self.copy(index).wait_send)
+
+
+def side_steps(named, side, loads, made):
+    tile = 512
+    while loads:
+        loads.pop().wait()
+    for left_key, right_key, out_key in side:
+        left = getattr(named, left_key)
+        right = getattr(named, right_key)
+        count = math.prod(left.shape[:-1])
+        for start in range(0, right.shape[-1], tile):
+            where = pl.ds(start, tile)
+            value = outer_sum(
+                left[...].reshape(count, left.shape[-1]),
+                right[:, :, :, where].reshape(count, tile),
+            ).astype(LOW)
+            if out_key is None:
+                query = named.g_query.shape[0]
+                named.g_query[:, where] = value[:query]
+                named.kv_mine[:, :, :, where] = value[query:].reshape(
+                    *named.kv_mine.shape[:3], tile
+                )
+            else:
+                getattr(named, out_key)[:, where] = value
+            yield
+        if out_key is None:
+            made("g_query")
+            site = named.site
+            peers = (site.sibling, site.across, site.corner)
+            links = Links(named.kv_send, named.kv_recv, site)
+            for index, device in enumerate(peers):
+                links.go(
+                    index, named.kv_mine.at[:, device[2]], named.kv_came.at[index], device
+                )
+            yield
+            yield
+            total = named.kv_mine[:, site.member].astype(FULL)
+            for index in range(len(peers)):
+                total = total + links.got(index, named.kv_came.at[index])[...].astype(FULL)
+            named.g_kv[...] = total.astype(LOW)
+            made("g_kv")
+            links.close()
+        else:
+            made(out_key)
 
 
 class Weights:
@@ -694,17 +758,27 @@
     plan = spec.plan
     values = take(spec.n_in)
     own, other = take(len(plan)), take(len(plan))
-    sources = take(spec.n_cross)
+    sources = take(spec.n_cross - len(spec.late_cross))
+    load_from = take(spec.n_loads)
     take(spec.n_after)
-    named = types.SimpleNamespace(**dict(zip(spec.names, values + refs)))
+    by_name = dict(zip(spec.names, values + refs))
+    places = {key: by_name.pop((key,)) for key in spec.stored}
+    named = types.SimpleNamespace(**by_name)
     site = Site()
     named.site = site
-    greet(site, spec.peers, spec.n_cross or spec.peers)
+    greet(site, spec.peers, spec.n_cross > 0)
     cross = weights = None
     if spec.n_cross:
         targets = [getattr(named, key) for key in spec.crossed]
+        sources += [getattr(named, key) for key in spec.late_cross]
         cross = Cross(
-            site, spec.groups, sources, targets, named.cross_send, named.cross_recv
+            site,
+            spec.groups,
+            sources,
+            targets,
+            spec.ways,
+            named.cross_send,
+            named.cross_recv,
         )
         for index, item in enumerate(plan):
             if item[3] is not None:
@@ -712,6 +786,37 @@
     if plan:
         held = [getattr(named, item[0]) for item in plan]
         weights = Weights(site, plan, held, own, other, named.weight_sem, cross)
+    loads = [
+        pltpu.make_async_copy(source, getattr(named, key), named.load_sem.at[index])
+        for index, (key, source) in enumerate(zip(spec.load_keys, load_from))
+    ]
+    for copy in loads:
+        copy.start()
+    if spec.before is not None:
+        spec.before(named)
+    if cross is not None:
+        cross.start()
+
+    storing = []
+
+    def made(key):
+        if key in places:
+            copy = pltpu.make_async_copy(
+                getattr(named, key),
+                places.pop(key),
+                named.stored_sem.at[spec.stored.index(key)],
+            )
+            copy.start()
+            storing.append(copy)
+        if key in spec.late_cross:
+            cross.send(len(sources) - len(spec.late_cross) + spec.late_cross.index(key))
+
+    working = side_steps(named, spec.side, loads, made)
+
+    def idle(count):
+        for _ in range(count if spec.side else 0):
+            next(working, None)
+
     total = None
     if spec.fold is not None:
         links = Links(named.fold_send, named.fold_recv, site)
@@ -725,16 +830,52 @@
             named.stage,
             named.land,
             links,
+            idle,
         )
     rows = spec.local(named, total)
+    for key in spec.local_made:
+        made(key)
+    folding = None
+    if spec.middle is not None:
+        folding = spec.middle(named)
+        next(folding)
+    if spec.second is not None:
+        for _ in working:
+            pass
+        links_second = Links(named.second_send, named.second_recv, site)
+        total = fold_steps(
+            site,
+            functools.partial(spec.second[0], named),
+            named.mine_b,
+            named.pass_out_b,
+            named.pass_in_b,
+            named.stage_b,
+            named.land_b,
+            links_second,
+            lambda count: next(folding, None),
+        )
+        spec.second[1](named, total)
+        links_second.close()
+        made("result_swap")
+        for _ in folding:
+            pass
+    if spec.side:
+        for _ in working:
+            pass
     if spec.use is not None:
         held = named.held
         held[site.chip(0, 0), site.core] = rows
-        kept = []
+        kept, waiting = [], []
+        named.ready = False
 
         def consume(chip):
+            if spec.late and not named.ready:
+                waiting.append(chip)
+                return
             if plan:
                 weights.settle(spec.use_keys)
+            while loads:
+                loads.pop().wait()
             block = held[chip]
             spec.use(named, chip, block.reshape(block.shape[0] * block.shape[1], block.shape[2]))
             source = named.normed if spec.normed else held
@@ -751,18 +892,43 @@
             spec.meanwhile(named, spreading)
         for _ in spreading:
             pass
+        if spec.top:
+            for index in spec.groups[0]:
+                cross.wait(index)
+            place = named.top_all.at[site.chip(0, 0), site.core]
+            copy = pltpu.make_async_copy(named.top_rows, place, named.top_sem)
+            copy.start()
+            copy.wait()
+            named.ready = True
+            links_top = Links(named.top_send, named.top_recv, site)
+            for _ in spread_steps(site, named.top_all, links_top, lambda chip: None):
+                for _ in range(3):
+                    if waiting:
+                        consume(waiting.pop(0))
+            links_top.close()
+        named.ready = True
+        for chip in waiting:
+            consume(chip)
         for copy in kept:
             copy.wait()
         links_on.close()
+    for key in list(places):
+        made(key)
+    if spec.after_all is not None:
+        spec.after_all(named)
     if spec.fold is not None:
         links.close()
     if cross is not None:
         cross.close()
+    for copy in storing:
+        copy.wait()
 
 
 def ring_call(
     name, ident, inputs, fold_weights, use_weights, outputs, local, fold=None, use=None,
-    extra=None, after=(), meanwhile=None, peers=False, normed=False, cross=(),
+    extra=None, after=(), before=None, meanwhile=None, peers=False, normed=False, cross=(),
+    late=False, top=None, loads=None, side=(), late_cross=None, second=None, local_made=(), layer=None, two_way=(),
+    to_second=(), stored=None, middle=None, after_all=None,
 ):
     per_device, width = inputs.pop("like").shape
     out_shape = [jax.ShapeDtypeStruct(*value) for value in outputs.values()]
@@ -787,15 +953,36 @@
             start += own.shape[0]
         scratch[key] = pltpu.VMEM((start, width), LOW)
     full = (per_device, width)
-    more = dict(extra or {})
-    for key, value in zip(crossed, cross_set):
+    late_cross = late_cross or {}
+    stored = stored or {}
+    extra = dict(extra or {})
+    for key, value in stored.items():
+        extra[key] = pltpu.VMEM(*value)
+    known = dict(zip(names[len(inputs) :], out_shape), **extra)
+    more = dict(extra)
+    cross_shapes = cross_set + [known[key] for key in late_cross.values()]
+    crossed += list(late_cross)
+    for key, value in zip(crossed, cross_shapes):
         names.append(key)
         out_shape.append(jax.ShapeDtypeStruct(value.shape, value.dtype))
-        out_specs.append(ANYWHERE)
-    if cross:
+        out_specs.append(IN_HBM)
+    if crossed:
         more.update(
             cross_send=pltpu.SemaphoreType.DMA((len(crossed),)),
             cross_recv=pltpu.SemaphoreType.DMA((len(crossed),)),
+        )
+    if loads:
+        more.update(load_sem=pltpu.SemaphoreType.DMA((len(loads),)))
+        for key, value in loads.items():
+            scratch[key] = pltpu.VMEM(value.shape, value.dtype)
+    if top is not None:
+        names.append("top_all")
+        out_shape.append(jax.ShapeDtypeStruct((CHIPS, 2, *full), LOW))
+        out_specs.append(IN_HBM)
+        more.update(
+            top_sem=pltpu.SemaphoreType.DMA,
+            top_send=pltpu.SemaphoreType.DMA((SPREAD_SEMS,)),
+            top_recv=pltpu.SemaphoreType.DMA((SPREAD_SEMS,)),
         )
     if plan:
         more.update(weight_sem=pltpu.SemaphoreType.DMA((len(plan),)))
@@ -809,10 +996,25 @@
             fold_send=pltpu.SemaphoreType.DMA((FOLD_SEMS,)),
             fold_recv=pltpu.SemaphoreType.DMA((FOLD_SEMS,)),
         )
+    if second is not None:
+        more.update(
+            mine_b=pltpu.VMEM((CHIPS, *full), FULL),
+            pass_out_b=pltpu.VMEM((CHIPS, *full), LOW),
+            pass_in_b=pltpu.VMEM((CHIPS, *full), LOW),
+            stage_b=pltpu.VMEM((CHIPS - 1, *full), LOW),
+            land_b=pltpu.VMEM((CHIPS - 1, *full), LOW),
+            second_send=pltpu.SemaphoreType.DMA((FOLD_SEMS,)),
+            second_recv=pltpu.SemaphoreType.DMA((FOLD_SEMS,)),
+        )
+    if stored:
+        names += [(key,) for key in stored]
+        out_shape += [jax.ShapeDtypeStruct(*value) for value in stored.values()]
+        out_specs += [IN_HBM] * len(stored)
+        more.update(stored_sem=pltpu.SemaphoreType.DMA((len(stored),)))
     if use is not None:
         names.append("rows_all")
         out_shape.append(jax.ShapeDtypeStruct((CHIPS, 2, *full), LOW))
-        out_specs.append(ANYWHERE)
+        out_specs.append(IN_HBM)
         more.update(
             held=pltpu.VMEM((CHIPS, 2, *full), LOW),
             keep_sem=pltpu.SemaphoreType.DMA((CHIPS,)),
@@ -827,20 +1029,35 @@
     for group in cross:
         groups.append(list(range(at, at + len(group))))
         at += len(group)
+    sizes = [math.prod(value.shape) * value.dtype.itemsize for value in inputs.values()]
+    sizes += [
+        math.prod(value.shape) * jnp.dtype(value.dtype).itemsize
+        for value, place in zip(out_shape, out_specs)
+        if place is IN_VMEM
+    ]
+    sizes += [
+        math.prod(value.shape) * jnp.dtype(value.dtype).itemsize
+        for value in scratch.values()
+        if isinstance(value, type(pltpu.VMEM((1,), LOW))) and len(value.shape) > 1
+    ]
     spec = types.SimpleNamespace(
         names=names, plan=plan, n_in=len(inputs), n_cross=len(crossed), n_after=len(after),
         crossed=crossed, groups=groups, fold=fold, local=local, use=use, meanwhile=meanwhile,
-        peers=peers, normed=normed, fold_keys=list(fold_weights), use_keys=list(use_weights),
+        peers=peers, normed=normed, before=before, late=late, top=top is not None,
+        stored=list(stored), middle=middle, after_all=after_all, side=side, ways=[None if key in two_way else 1 if key in to_second else layer for key in crossed], late_cross=list(late_cross.values()), second=second, local_made=local_made,
+        n_loads=len(loads or {}), load_keys=list(loads or {}), fold_keys=list(fold_weights), use_keys=list(use_weights),
     )
     return pl.pallas_call(
         functools.partial(ring_kernel, spec),
         out_shape=out_shape,
         in_specs=[IN_VMEM] * len(inputs)
-        + [ANYWHERE] * (2 * len(plan) + len(crossed) + len(after)),
+        + [IN_HBM] * (2 * len(plan) + len(cross_set) + len(loads or {}) + len(after)),
         out_specs=out_specs,
         scratch_shapes=list(scratch.values()),
         compiler_params=pltpu.CompilerParams(
-            collective_id=ident, has_side_effects=True, vmem_limit_bytes=56 * 2**20
+            collective_id=ident,
+            has_side_effects=True,
+            vmem_limit_bytes=int(sum(sizes) * 1.1) + 5 * 2**20,
         ),
         cost_estimate=pl.CostEstimate(
             flops=2**35 * ((fold is not None) + (use is not None)),
@@ -848,7 +1065,7 @@
             transcendentals=0,
         ),
         name=name,
-    )(*inputs.values(), *own_set, *other_set, *cross_set, *after)
+    )(*inputs.values(), *own_set, *other_set, *cross_set, *(loads or {}).values(), *after)
 
 
 def rows_of(ref, chip, site):
@@ -892,6 +1109,18 @@
     put(named.up_slope, chip, silu_val)
 
 
+def use_gate_up_back(named, chip, rows):
+    gate_pre = times_trans(rows, named.w_gate[...])
+    up_pre = times_trans(rows, named.w_up[...])
+    sig = jax.nn.sigmoid(gate_pre)
+    silu_val = gate_pre * sig
+    put(named.act, chip, silu_val * up_pre)
+    top = named.top_held[chip].reshape(rows.shape)
+    d_act = times_trans(top, named.w_down[...])
+    put(named.d_gate, chip, d_act * up_pre * sig * (1.0 + gate_pre * (1.0 - sig)))
+    put(named.d_up, chip, d_act * silu_val)
+
+
 def use_d_act(named, chip, rows):
     d_act = times_trans(rows, named.w_down[...])
     for out, slope in ((named.d_gate, named.gate_slope), (named.d_up, named.up_slope)):
@@ -906,15 +1135,15 @@
     return named.x_rows[...]
 
 
-def gather_small(named, rows_spreading):
+def gather_small(named):
     site = named.site
-    links_x = Links(named.small_x_send, named.small_x_recv, site)
-    links_x.go(0, named.gains_own, named.gains_x, site.partner)
-    links_x.go(1, named.kv_own, named.kv_x, site.partner)
-    links_x.got(0, named.gains_x)
+    links = Links(named.small_send, named.small_recv, site)
+    links.go(0, named.gains_own, named.gains_x, site.partner)
+    links.go(1, named.kv_own, named.kv_x, site.partner)
+    links.got(0, named.gains_x)
     own, came = named.gains_own[...], named.gains_x[...]
     first = site.section == 0
-    named.gains_all[site.chip(0, 0), site.core] = jnp.concatenate(
+    named.gains_all[site.z, site.member] = jnp.concatenate(
         [
             jnp.where(first, own, came)[:2],
             jnp.where(first, came, own)[:2],
@@ -922,39 +1151,48 @@
         ],
         0,
     )
-    links = Links(named.small_send, named.small_recv, site)
-    spreading = spread_steps(site, named.gains_all, links, lambda chip: None, 1)
-    next(spreading)
-    links_x.got(1, named.kv_x)
+    peers = (site.sibling, site.across, site.corner)
+    mine = named.gains_all.at[site.z, site.member]
+    for index, device in enumerate(peers):
+        links.go(2 + index, mine, mine, device)
+    for index, device in enumerate(peers):
+        links.got(2 + index, named.gains_all.at[site.z, device[2]])
+    shard = named.gains_all.at[site.z]
+    for index, device in enumerate((site.up, site.down, site.opposite)):
+        links.go(5 + index, shard, shard, device)
+    named.links_small = links
+
+
+def gather_small_end(named, rows_spreading):
+    site, links = named.site, named.links_small
+    links.got(1, named.kv_x)
     named.kv_all[site.member, site.section] = named.kv_own[...]
     named.kv_all[site.member, 1 - site.section] = named.kv_x[...]
-    links_kv = Links(named.kv_send, named.kv_recv, site)
     mine = named.kv_all.at[site.member]
     peers = (site.sibling, site.across, site.corner)
     for index, device in enumerate(peers):
-        links_kv.go(index, mine, mine, device)
+        links.go(8 + index, mine, mine, device)
     next(rows_spreading)
-    for _ in spreading:
-        pass
+    for index, along_z in enumerate((RING - 1, 1, 2)):
+        links.got(5 + index, named.gains_all.at[lax.rem(site.z + along_z, RING)])
     for index, device in enumerate(peers):
-        links_kv.got(index, named.kv_all.at[device[2]])
+        links.got(8 + index, named.kv_all.at[device[2]])
     links.close()
-    links_kv.close()
-    links_x.close()
     named.gain_row[...] = jnp.concatenate(
-        [named.gains_all[chip, core, :1] for chip in range(CHIPS) for core in range(2)], 1
+        [named.gains_all[shard, seq, :1] for shard in range(RING) for seq in range(RING)], 1
+    )
+    named.w_kv[...] = jnp.concatenate(
+        [named.kv_all[:, 0, index].reshape(HEAD_DIM, named.w_kv.shape[1]) for index in range(2)],
+        0,
     )
 
 
 def use_first(named, chip, rows):
     normed = scaled(rows.astype(FULL), named.gain_row[...]).astype(LOW)
     named.normed[chip] = normed.reshape(named.normed.shape[1:])
-    query = times_trans(normed, named.w_query[...])
-    pair = [
-        times_trans(normed, named.kv_all[:, 0, index].reshape(HEAD_DIM, normed.shape[1]))
-        for index in range(2)
-    ]
-    named.qkv[chip] = jnp.concatenate([query, *pair], 1)
+    named.qkv[chip] = jnp.concatenate(
+        [times_trans(normed, named.w_query[...]), times_trans(normed, named.w_kv[...])], 1
+    )
 
 
 def local_middle(named, total):
@@ -970,7 +1208,9 @@
 
 
 def local_last(named, total):
-    named.result[...] = (named.hidden_in[...] + total).astype(LOW)
+    result = (named.hidden_in[...] + total).astype(LOW)
+    named.result[...] = result
+    named.result_swap[...] = jnp.where(named.site.section == 0, result, named.result_first[...])
 
 
 def local_top(named, total):
@@ -1003,6 +1243,50 @@
     named.gain_grad[...] = gain_grad
     named.d_input[...] = d_input
     return d_input
+
+
+def local_input_last(named, total):
+    d_input = local_input(named, total)
+    named.input_swap[...] = jnp.where(
+        named.site.section == 0, named.input_second[...], d_input
+    )
+
+
+def fold_gains(named):
+    site = named.site
+    links = Links(named.gain_send, named.gain_recv, site)
+    own = jnp.concatenate(
+        [named.gain_grad[...], named.gain_ffn_a[...], named.gain_attn_b[...],
+         named.gain_ffn_b[...], jnp.zeros((4, named.gain_grad.shape[1]), FULL)],
+        0,
+    )
+    width = named.gain_parts.shape[-1]
+    for shard in range(RING):
+        for seq in range(RING):
+            start = (shard * RING + seq) * width
+            named.gain_parts[seq, shard] = own[:, start : start + width]
+    peers = (site.sibling, site.across, site.corner)
+    for index, device in enumerate(peers):
+        links.go(index, named.gain_parts.at[device[2]], named.gain_came.at[index], device)
+    yield
+    total = named.gain_parts[site.member]
+    for index in range(3):
+        total = total + links.got(index, named.gain_came.at[index])[...]
+    named.gain_shards[...] = total
+    for index, device in enumerate((site.up, site.down, site.opposite)):
+        links.go(
+            3 + index, named.gain_shards.at[device[1]], named.gain_last.at[index], device
+        )
+    yield
+    total = named.gain_shards[site.z]
+    for index in range(3):
+        total = total + links.got(3 + index, named.gain_last.at[index])[...]
+    named.gain_own[...] = total
+    links.go(6, named.gain_own, named.gain_other, site.partner)
+    yield
+    total = named.gain_own[...] + links.got(6, named.gain_other)[...]
+    named.gain_sums[...] = jnp.where(site.section == 0, total[:2], total[2:4])
+    links.close()
 
 
 def swap_halves(value):
@@ -1118,6 +1402,57 @@
         d_qkv[block_at[place]] = value.astype(LOW).reshape(d_qkv.shape[1:])
 
 
+def join_kernel(count, *refs):
+    own, came = (refs[:count], refs[count : 2 * count]), (
+        refs[2 * count : 3 * count],
+        refs[3 * count : 4 * count],
+    )
+    outs, refs = refs[4 * count : 5 * count], refs[5 * count :]
+    own_at, came_at, sums = refs[:count], refs[count : 2 * count], refs[2 * count : 3 * count]
+    sems, out_sem = refs[3 * count :]
+    section = lax.axis_index("section")
+    waits = []
+    for index in range(count):
+        for slot, (pair, target) in enumerate(((own, own_at), (came, came_at))):
+            copies = [
+                pltpu.make_async_copy(
+                    pair[layer][index], target[index], sems.at[2 * index + slot]
+                )
+                for layer in range(2)
+            ]
+            pl.when(section == 0)(copies[0].start)
+            pl.when(section != 0)(copies[1].start)
+            waits.append(copies[0])
+    done = []
+    for index in range(count):
+        waits[2 * index].wait()
+        waits[2 * index + 1].wait()
+        sums[index][...] = own_at[index][...].astype(FULL) + came_at[index][...].astype(FULL)
+        copy = pltpu.make_async_copy(sums[index], outs[index], out_sem.at[index])
+        copy.start()
+        done.append(copy)
+    for copy in done:
+        copy.wait()
+
+
+def join_sums(own_a, own_b, came_a, came_b):
+    count = len(own_a)
+    kept = [pltpu.VMEM(value.shape, LOW) for value in own_a]
+    return pl.pallas_call(
+        functools.partial(join_kernel, count),
+        out_shape=[jax.ShapeDtypeStruct(value.shape, FULL) for value in own_a],
+        in_specs=[IN_HBM] * (4 * count),
+        out_specs=[IN_HBM] * count,
+        scratch_shapes=kept
+        + kept
+        + [pltpu.VMEM(value.shape, FULL) for value in own_a]
+        + [pltpu.SemaphoreType.DMA((2 * count,)), pltpu.SemaphoreType.DMA((count,))],
+        compiler_params=pltpu.CompilerParams(vmem_limit_bytes=40 * 2**20),
+        cost_estimate=pl.CostEstimate(flops=2**32, bytes_accessed=2**24, transcendentals=0),
+        name="join_sums",
+    )(*own_a, *own_b, *came_a, *came_b)
+
+
 def plain_call(kernel, name, count, out_shape, scratch):
     return pl.pallas_call(
         kernel,
@@ -1156,9 +1491,6 @@
     hidden = w_down.shape[1]
     shape = jax.ShapeDtypeStruct
 
-    def swap(value):
-        return lax.ppermute(value, "section", [(0, 1), (1, 0)])
-
     def pick(first, second):
         return jnp.where(section_idx == 0, first, second)
 
@@ -1188,7 +1520,6 @@
 
     narrow = (CHIPS, 2, per_device, hidden)
     chip_rows = 2 * per_device
-    act_outs = dict(act=(narrow, LOW), gate_slope=(narrow, LOW), up_slope=(narrow, LOW))
     back_outs = dict(d_gate=(narrow, LOW), d_up=(narrow, LOW))
     qkv_out = dict(qkv=((CHIPS, chip_rows, in_width), FULL))
     row_low = ((per_device, model_width), LOW)
@@ -1228,21 +1559,24 @@
         )(block_at, d_mixed, turns, *saved)
         return d_qkv
 
-    def middle(layer, mixed, x_rows, w_gate_set, w_up_set, cross=()):
-        return ring_call(
-            "attn_out_to_ffn",
-            1 + 7 * layer,
-            dict(like=x_rows, x_rows=x_rows, mixed=mixed, gain=gains[layer, 1]),
-            dict(w_out=[(w_out[0], x_out, layer)]),
-            dict(w_gate=[(*w_gate_set, layer)], w_up=[(*w_up_set, layer)]),
-            dict(hidden_in=row_full, **act_outs),
-            local_middle,
-            fold=fold_mixed,
-            use=use_gate_up,
-            cross=cross,
-        )
-
-    def middle_back(layer, d_gate, d_up, hidden_in, top_rows, after=()):
+    wide = ((hidden, model_width), LOW)
+    kv_shape = (2, n_seq, w_key.shape[1], model_width)
+    in_outs = dict(
+        g_out=((q_width, model_width), LOW),
+        g_query=((q_width, model_width), LOW),
+        g_kv=((2, *kv_shape[2:]), LOW),
+    )
+    kv_extra = dict(
+        kv_mine=pltpu.VMEM(kv_shape, LOW),
+        kv_came=pltpu.VMEM((n_seq - 1, 2, *kv_shape[2:]), LOW),
+        kv_send=pltpu.SemaphoreType.DMA((n_seq - 1,)),
+        kv_recv=pltpu.SemaphoreType.DMA((n_seq - 1,)),
+    )
+    in_side = (("mixed", "branch_all", "g_out"), ("d_qkv", "normed_one", None))
+
+    def middle_back(
+        layer, d_gate, d_up, hidden_in, top_rows, more_in, loads, late_cross, cross=()
+    ):
         return ring_call(
             "ffn_back_to_attn",
             2 + 7 * layer,
@@ -1253,6 +1587,7 @@
                 hidden_in=hidden_in,
                 top_rows=top_rows,
                 gain=gains[layer, 1],
+                **more_in,
             ),
             dict(w_gate=[(w_gate[0], x_gate, layer)], w_up=[(w_up[0], x_up, layer)]),
             dict(w_out=[(w_out[0], x_out, layer)]),
@@ -1262,9 +1597,19 @@
                 d_mixed=((CHIPS, chip_rows, q_width), LOW),
             ),
             local_branch,
+            stored=dict(g_down=wide, g_gate=wide, g_up=wide),
             fold=fold_d_act,
             use=use_d_mixed,
-            after=after,
+            loads=loads,
+            side=(
+                ("act", "top_all", "g_down"),
+                ("d_gate", "normed_two", "g_gate"),
+                ("d_up", "normed_two", "g_up"),
+            ),
+            late_cross=late_cross,
+            cross=cross,
+            layer=layer,
+            to_second=("came_up_b",),
         )
 
     qkv, gains_all, kv_all, x_query, x_out, normed_one_a = ring_call(
@@ -1275,38 +1620,47 @@
         dict(w_query=[("x_query", 0)]),
         dict(
             **qkv_out,
-            gains_all=((CHIPS, 2, *small.shape), FULL),
+            gains_all=((n_shard, n_seq, *small.shape), FULL),
             kv_all=((n_seq, 2, *kv_pair.shape), LOW),
         ),
         local_start,
         use=use_first,
         extra=dict(
             gain_row=pltpu.VMEM((1, model_width), FULL),
+            w_kv=pltpu.VMEM((2 * HEAD_DIM, model_width), LOW),
             small_send=pltpu.SemaphoreType.DMA((SMALL_SEMS,)),
             small_recv=pltpu.SemaphoreType.DMA((SMALL_SEMS,)),
-            kv_send=pltpu.SemaphoreType.DMA((n_seq - 1,)),
-            kv_recv=pltpu.SemaphoreType.DMA((n_seq - 1,)),
             gains_x=pltpu.VMEM(small.shape, FULL),
             kv_x=pltpu.VMEM(kv_pair.shape, LOW),
-            small_x_send=pltpu.SemaphoreType.DMA((2,)),
-            small_x_recv=pltpu.SemaphoreType.DMA((2,)),
         ),
         normed=True,
-        cross=[dict(x_query=w_query[0]), dict(x_out=w_out[0])],
-        meanwhile=gather_small,
-        peers=True,
+        cross=[dict(x_query=w_query[0], x_out=w_out[0])],
+        before=gather_small,
+        meanwhile=gather_small_end,
+        peers=2,
     )
     gains = gains_all.reshape(members, -1, gain_attn.shape[1])[:, :4]
     gains = gains.transpose(1, 0, 2).reshape(2, 2, 1, model_width)
     kv_all = kv_all.transpose(1, 2, 0, 3, 4).reshape(2, 2 * HEAD_DIM, model_width)
     mixed_a, saved_a = attend(qkv)
-    hidden_a, act_a, gate_slope_a, up_slope_a, x_gate, x_up, x_down, normed_two_a = middle(
-        0,
-        mixed_a,
-        rows_in,
-        ("x_gate",),
-        ("x_up",),
-        [dict(x_gate=w_gate[0], x_up=w_up[0]), dict(x_down=w_down[0])],
+    hidden_a, act_a, x_gate, x_up, x_down, top_all_b, gate_slope_a, up_slope_a, normed_two_a = (
+        ring_call(
+            "attn_out_to_ffn",
+            1,
+            dict(
+                like=rows_in, x_rows=rows_in, mixed=mixed_a, gain=gains[0, 1], top_rows=top_in
+            ),
+            dict(w_out=[(w_out[0], x_out, 0)]),
+            dict(w_gate=[("x_gate", 0)], w_up=[("x_up", 0)]),
+            dict(hidden_in=row_full, act=(narrow, LOW)),
+            local_middle,
+            fold=fold_mixed,
+            use=use_gate_up,
+            stored=dict(gate_slope=(narrow, LOW), up_slope=(narrow, LOW)),
+            cross=[dict(x_gate=w_gate[0], x_up=w_up[0]), dict(x_down=w_down[0])],
+            late=True,
+            top=top_in,
+        )
     )
     result_a, qkv, normed_one_b = ring_call(
         "ffn_to_next",
@@ -1320,58 +1674,36 @@
         use=use_qkv,
     )
     mixed_b, saved_b = attend(qkv)
-    hidden_b, act_b, gate_slope_b, up_slope_b, normed_two_b = middle(
-        1, mixed_b, result_a, (w_gate[0], x_gate), (w_up[0], x_up)
-    )
-
-    def join_to(layer, own):
-        pairs = [(0, 1)] if layer else [(1, 0)]
-        return own, lax.ppermute(own, "section", pairs)
-
-    def ffn_sums(layer, act, top_all, d_gate, d_up, normed_two):
-        return [
-            join_to(layer, outer_sum(flat(left), flat(right)).astype(LOW))
-            for left, right in ((act, top_all), (d_gate, normed_two), (d_up, normed_two))
-        ]
-
-    def attn_sums(layer, mixed, branch_all, d_qkv, normed_one):
-        g_in = outer_sum(flat(d_qkv), flat(normed_one)).astype(LOW)
-        kv = g_in[q_width:].reshape(2, n_seq, -1, model_width)
-        kv = lax.all_to_all(kv, "seq", split_axis=1, concat_axis=1, tiled=True)
-        kv = jnp.sum(kv.astype(FULL), 1).astype(LOW)
-        g_out = outer_sum(flat(mixed), flat(branch_all)).astype(LOW)
-        return [join_to(layer, value) for value in (g_out, g_in[:q_width], kv)]
-
-    def came_of(sums):
-        return [came for _, came in sums]
-
-    (result_b,) = ring_call(
-        "ffn_last",
-        4,
-        dict(like=rows_in, act=act_b, hidden_in=hidden_b),
-        dict(w_down=[(w_down[0], x_down, 1)]),
-        {},
-        dict(result=row_low),
-        local_last,
-        fold=fold_act,
-    )
-    d_gate_b, d_up_b, top_all_b = ring_call(
-        "top_rows",
+    hidden_b, act_b, d_gate_b, d_up_b, normed_two_b = ring_call(
+        "attn_out_to_ffn_and_back",
         5,
-        dict(like=top_in, top_rows=top_in, gate_slope=gate_slope_b, up_slope=up_slope_b),
-        {},
-        dict(w_down=[(w_down[0], x_down, 1)]),
-        back_outs,
-        local_top,
-        use=use_d_act,
-    )
-    ffn_b = ffn_sums(1, act_b, top_all_b, d_gate_b, d_up_b, normed_two_b)
-    gain_ffn_b, d_hidden_b, d_mixed, branch_all_b = middle_back(
-        1, d_gate_b, d_up_b, hidden_b, top_in
+        dict(like=rows_in, x_rows=result_a, mixed=mixed_b, gain=gains[1, 1]),
+        dict(w_out=[(w_out[0], x_out, 1)]),
+        dict(
+            w_gate=[(w_gate[0], x_gate, 1)],
+            w_up=[(w_up[0], x_up, 1)],
+            w_down=[(w_down[0], x_down, 1)],
+        ),
+        dict(hidden_in=row_full, act=(narrow, LOW), **back_outs),
+        local_middle,
+        fold=fold_mixed,
+        use=use_gate_up_back,
+        loads=dict(top_held=top_all_b),
+    )
+
+    (
+        gain_ffn_b, d_hidden_b, d_mixed, came_down_b, own_down_b, own_gate_b, own_up_b,
+        branch_all_b,
+    ) = middle_back(
+        1, d_gate_b, d_up_b, hidden_b, top_in, dict(act=act_b),
+        dict(top_all=top_all_b, normed_two=normed_two_b),
+        dict(came_down="g_down"),
     )
     d_qkv_b = attend_back(saved_b, d_mixed)
-    attn_b = attn_sums(1, mixed_b, branch_all_b, d_qkv_b, normed_one_b)
-    gain_attn_b, back_b, d_gate_a, d_up_a, top_all_a = ring_call(
+    (
+        gain_attn_b, back_b, d_gate_a, d_up_a, came_gate_b, came_out_b, came_query_b,
+        came_kv_b, own_out_b, own_query_b, own_kv_b, top_all_a,
+    ) = ring_call(
         "attn_back_to_prev",
         6,
         dict(
@@ -1380,8 +1712,6 @@
             x_rows=result_a,
             d_hidden=d_hidden_b,
             gain=gains[1, 0],
-            gate_slope=gate_slope_a,
-            up_slope=up_slope_a,
         ),
         dict(w_in=w_in_of(1)),
         dict(w_down=[(w_down[0], x_down, 0)]),
@@ -1389,56 +1719,116 @@
         local_input,
         fold=fold_d_qkv,
         use=use_d_act,
-    )
-    ffn_a = ffn_sums(0, act_a, top_all_a, d_gate_a, d_up_a, normed_two_a)
-    gain_ffn_a, d_hidden_a, d_mixed, branch_all_a = middle_back(
-        0, d_gate_a, d_up_a, hidden_a, back_b, after=came_of(ffn_b)
+        extra=kv_extra,
+        peers=1,
+        stored=in_outs,
+        loads=dict(
+            mixed=mixed_b,
+            branch_all=branch_all_b,
+            normed_one=normed_one_b,
+            gate_slope=gate_slope_a,
+            up_slope=up_slope_a,
+        ),
+        side=in_side,
+        cross=[dict(came_gate=own_gate_b)],
+        layer=1,
+        late_cross=dict(came_out="g_out", came_query="g_query", came_kv="g_kv"),
+    )
+    (
+        gain_ffn_a, d_hidden_a, d_mixed, came_up_b, came_down_a, came_gate_a, own_down_a,
+        own_gate_a, own_up_a, branch_all_a,
+    ) = middle_back(
+        0, d_gate_a, d_up_a, hidden_a, back_b, {},
+        dict(act=act_a, top_all=top_all_a, normed_two=normed_two_a),
+        dict(came_down="g_down", came_gate="g_gate"),
+        [dict(came_up_b=own_up_b)],
     )
     d_qkv_a = attend_back(saved_a, d_mixed)
-    attn_a = attn_sums(0, mixed_a, branch_all_a, d_qkv_a, normed_one_a)
-    gain_attn_a, back_a = ring_call(
+    (
+        _, back_a, result_b, gain_sums, came_up_a, came_out_a, came_query_a, came_kv_a,
+        input_came, result_came, own_out_a, own_query_a, own_kv_a,
+    ) = ring_call(
         "attn_back_last",
         7,
-        dict(like=top_in, d_qkv=d_qkv_a, x_rows=rows_in, d_hidden=d_hidden_a, gain=gains[0, 0]),
-        dict(w_in=w_in_of(0)),
+        dict(
+            like=top_in,
+            d_qkv=d_qkv_a,
+            x_rows=rows_in,
+            d_hidden=d_hidden_a,
+            gain=gains[0, 0],
+            act=act_b,
+            hidden_in=hidden_b,
+            result_first=result_a,
+            input_second=back_b,
+            gain_ffn_a=gain_ffn_a,
+            gain_attn_b=gain_attn_b,
+            gain_ffn_b=gain_ffn_b,
+        ),
+        dict(w_in=w_in_of(0), w_down=[(w_down[0], x_down, 1)]),
         {},
-        dict(gain_grad=gain_out, d_input=row_low),
-        local_input,
+        dict(
+            gain_grad=gain_out,
+            d_input=row_low,
+            result=row_low,
+            gain_sums=((2, gain_attn.shape[1]), FULL),
+        ),
+
+        local_input_last,
         fold=fold_d_qkv,
-        after=came_of(attn_b),
-    )
-
-    def joined(first, second):
-        came = swap(pick(second, first))
+        extra=dict(
+            **kv_extra,
+            input_swap=pltpu.VMEM(*row_low),
+            result_swap=pltpu.VMEM(*row_low),
+            gain_parts=pltpu.VMEM((n_seq, n_shard, *small.shape), FULL),
+            gain_came=pltpu.VMEM((n_seq - 1, n_shard, *small.shape), FULL),
+            gain_shards=pltpu.VMEM((n_shard, *small.shape), FULL),
+            gain_last=pltpu.VMEM((n_shard - 1, *small.shape), FULL),
+            gain_own=pltpu.VMEM(small.shape, FULL),
+            gain_other=pltpu.VMEM(small.shape, FULL),
+            gain_send=pltpu.SemaphoreType.DMA((7,)),
+            gain_recv=pltpu.SemaphoreType.DMA((7,)),
+        ),
+        stored=in_outs,
+        middle=fold_gains,
+        peers=2,
+        loads=dict(mixed=mixed_a, branch_all=branch_all_a, normed_one=normed_one_a),
+        side=in_side,
+        cross=[dict(came_up=own_up_a)],
+        layer=0,
+        two_way=("input_came", "result_came"),
+        late_cross=dict(
+            came_out="g_out",
+            came_query="g_query",
+            came_kv="g_kv",
+            input_came="input_swap",
+            result_came="result_swap",
+        ),
+        second=(fold_act, local_last),
+        local_made=("input_swap",),
+    )
+
+    def joined(first, second, came):
         kept = pick(first, second)
         return pick(jnp.stack([kept, came]), jnp.stack([came, kept]))[None]
 
-    outputs = joined(result_a, result_b)
-    input_grads = joined(back_a, back_b)
-
-    g_down, g_gate, g_up, g_out, g_query, g_kv = (
-        pick(own_a, own_b).astype(FULL) + pick(came_a, came_b).astype(FULL)
-        for (own_a, came_a), (own_b, came_b) in zip(ffn_a + attn_a, ffn_b + attn_b)
-    )
-    gain_grads = jnp.concatenate([gain_attn_a, gain_ffn_a, gain_attn_b, gain_ffn_b], 0)
-    gain_grads = gain_grads.reshape(2, 2, members, -1).transpose(0, 2, 1, 3)
-    gain_grads = lax.all_to_all(
-        gain_grads.reshape(2 * members, 2, -1),
-        ("section", "shard", "seq"),
-        split_axis=0,
-        concat_axis=0,
-        tiled=True,
-    )
-    gain_grads = jnp.sum(gain_grads, 0, keepdims=True)
+    outputs = joined(result_a, result_b, result_came)
+    input_grads = joined(back_a, back_b, input_came)
+
+    g_down, g_gate, g_up, g_out, g_query, g_kv = join_sums(
+        (own_down_a, own_gate_a, own_up_a, own_out_a, own_query_a, own_kv_a),
+        (own_down_b, own_gate_b, own_up_b, own_out_b, own_query_b, own_kv_b),
+        (came_down_a, came_gate_a, came_up_a, came_out_a, came_query_a, came_kv_a),
+        (came_down_b, came_gate_b, came_up_b, came_out_b, came_query_b, came_kv_b),
+    )
     return (
         outputs,
         input_grads,
-        gain_grads[:, 0],
+        gain_sums[:1],
         g_query[None],
         g_kv[:1],
         g_kv[1:],
         g_out[None],
-        gain_grads[:, 1],
+        gain_sums[1:],
         g_gate[None],
         g_up[None],
         g_down[None],

time: 740 us -> 640 us (0.86)
  starting transfers between devices: 45 us -> 0 us
  local copies, waits for them, and re-layouts: 16.4 us -> 49.4 us
  matrix products: 29.7 us -> 0 us
  other arithmetic: 33.2 us -> 6.3 us
  Pallas kernels: 595 us -> 574 us
  waiting for transfers between devices: 9.37 us -> 0 us
    unnamed x91 -> x176, local copies, waits for them, and re-layouts: 5.56 us -> 47.1 us
    ppermute x14 -> x0, starting transfers between devices: 29.8 us -> none  [the longest x12 26.8 us: join_to(): return (own, lax.ppermute(own, 'section', pairs))]
    dot_general x10 -> x0, matrix products: 29.7 us -> none  [outer_sum(): lax.dot_general(left, right, (((0,), (0,)), ((), ())), preferred_element_...]
    pallas_call x10 -> x8, Pallas kernels: 577 us -> 549 us  [ring_call(): pl.pallas_call(functools.partial(ring_kernel, spec), out_shape=out_shape,...]
    broadcast_in_dim x5 -> x0, other arithmetic: 16.6 us -> none  [the longest x1 3.91 us: relay_body(): g_gate[None]]
    all_to_all x3 -> x0, starting transfers between devices: 15.2 us -> none  [the longest x2 8.07 us: attn_sums(): kv = lax.all_to_all(kv, 'seq', split_axis=1, concat_axis=1, tiled=True)]
  transfers between devices with their start and end apart: 17 -> 0, of which waited for: 2 -> 0; matrix products, arithmetic and copies ran while one was open for 8% -> 0% of each run, Pallas kernels for 36% -> 0%
where the time goes in v2:
time: 640 us; the launch traced here: 631 us
  Pallas kernels  574 us (90%)
  local copies, waits for them, and re-layouts  49.4 us (8%)
    pallas_call x8, Pallas kernels, ring_call(): pl.pallas_call(functools.partial(ring_kernel, spec), out_shape=out_shape,...  549 us
    unnamed x176, local copies, waits for them, and re-layouts  47.1 us

profile of v2, /device:TPU:0, one launch (start us, length us, event | category | flops | bytes accessed | tf_op | source)
XLA Modules:
  0.0 630.8 jit_solution(7530467026695179557)
XLA Ops:
  0.8 0.8 broadcast_select_fusion
  2.5 0.9 pad_maximum_fusion.1.refs_2_
  3.8 1.1 select_bitcast_fusion.3.refs_0_.refs_1_
  4.8 1.2 select_bitcast_fusion.2.refs_3_
  6.0 49.2 %first_rows.1 = (f32[8,128,256]{2,1,0:T(8,128)S(1)}, f32[4,4,8,128]{3,2,1,0:T(8,128)S(1)}, bf16[4,2,2,16,2048]{4,3,2,1,0:T(8,128)(2,1)S(1)}, bf16[128,2048]{1,0:...) custom-call(bf16[64,2048]{1,0:T(8,128)(2,1)S(1)} %select_bitcast_fusion.3.refs_0_.refs_1_, ...), custom_call_target="tpu_custom_call" | custom-call | flops 34359738368 | bytes 8388608 | tf_op jit(solution)/shard_map/first_rows/pallas_call | solution.py:1050
  55.2 1.0 copy-done.48
  56.2 2.0 copy-done.54
  59.9 1.2 copy-done.49
  61.1 4.7 attend.2
  65.9 0.9 copy.33
  68.5 98.8 %attn_out_to_ffn.1 = (f32[64,2048]{1,0:T(8,128)S(1)}, bf16[8,2,64,352]{3,2,1,0:T(8,128)(2,1)S(1)}, bf16[352,2048]{1,0:T(8,128)(2,1)S(1)}, bf16[352,2048]{1,0:T(8...) custom-call(bf16[64,2048]{1,0:T(8,128)(2,1)S(1)} %select_bitcast_fus, ...), custom_call_target="tpu_custom_call" | custom-call | flops 68719476736 | bytes 8388608 | tf_op jit(solution)/shard_map/attn_out_to_ffn/pallas_call | solution.py:1050
  167.4 2.0 copy-done.59
  169.4 2.0 copy-done.60
  171.4 0.9 copy-done.79
  172.3 59.7 %ffn_to_next.1 = (bf16[64,2048]{1,0:T(8,128)(2,1)S(1)}, f32[8,128,256]{2,1,0:T(8,128)S(1)}, bf16[8,2,64,2048]{3,2,1,0:T(8,128)(2,1)S(1)}) custom-call(bf16[8,2,64,352]{3,2,1,0:T(8,128)(2,1)S(1)} %get-tuple-element.94.refs_0_.refs_12_, f32[64,2048]{1,0:T(8,128)S(1)} %get-tuple-element.95.refs_1_.refs_2_, f32[1,2048]{1,0:T(1,128)S(1)} %get-tuple-element.175.refs_2_.refs_3_, ...), custom_call_target="tpu_custom_call" | custom-call | flops 68719476736 | bytes 8388608 | tf_op jit(solution)/shard_map/ffn_to_next/pallas_call | solution.py:1050
  232.1 2.1 copy-done.62
  234.2 4.7 attend.3
  238.9 65.0 %attn_out_to_ffn_and_back.1 = (f32[64,2048]{1,0:T(8,128)S(1)}, bf16[8,2,64,352]{3,2,1,0:T(8,128)(2,1)S(1)}, bf16[8,2,64,352]{3,2,1,0:T(8,128)(2,1)S(1)}, bf16[8,...) custom-call(bf16[64,2048]{1,0:T(8,128)(2,1)S(1)} %get-tuple-element.99.refs_0_.refs_1_.refs_6_, ...), custom_call_target="tpu_custom_call" | custom-call | flops 68719476736 | bytes 8388608 | tf_op jit(solution)/shard_map/attn_out_to_ffn_and_back/pallas_call | solution.py:1050
  303.9 2.0 copy-done.61
  305.9 60.0 %ffn_back_to_attn.2 = (f32[1,2048]{1,0:T(1,128)S(1)}, f32[64,2048]{1,0:T(8,128)S(1)}, bf16[8,128,128]{2,1,0:T(8,128)(2,1)S(1)}, bf16[352,2048]{1,0:T(8,128)(2,1)...) custom-call(bf16[8,2,64,352]{3,2,1,0:T(8,128)(2,1)S(1)} %get-tuple-e, ...), custom_call_target="tpu_custom_call" | custom-call | flops 68719476736 | bytes 8388608 | tf_op jit(solution)/shard_map/ffn_back_to_attn/pallas_call | solution.py:1050
  366.0 1.1 copy-done
  367.2 1.2 copy-done.1
  368.3 1.2 copy-done.3
  370.3 4.5 attend_back.2.refs_0_
  374.9 1.1 copy-done.80
  376.0 1.0 copy-done.84
  377.0 63.7 %attn_back_to_prev.1 = (f32[1,2048]{1,0:T(1,128)S(1)}, bf16[64,2048]{1,0:T(8,128)(2,1)S(1)}, bf16[8,2,64,352]{3,2,1,0:T(8,128)(2,1)S(1)}, bf16[8,2,64,352]{3,2,1...) custom-call(bf16[8,2,64,256]{3,2,1,0:T(8,128)(2,1)S(1)} %attend_back, ...), custom_call_target="tpu_custom_call" | custom-call | flops 68719476736 | bytes 8388608 | tf_op jit(solution)/shard_map/attn_back_to_prev/pallas_call | solution.py:1050
  440.8 1.1 copy-done.5
  442.6 79.1 %ffn_back_to_attn.3 = (f32[1,2048]{1,0:T(1,128)S(1)}, f32[64,2048]{1,0:T(8,128)S(1)}, bf16[8,128,128]{2,1,0:T(8,128)(2,1)S(1)}, bf16[352,2048]{1,0:T(8,128)(2,1)...) custom-call(bf16[8,2,64,352]{3,2,1,0:T(8,128)(2,1)S(1)} %get-tuple-e, ...), custom_call_target="tpu_custom_call" | custom-call | flops 68719476736 | bytes 8388608 | tf_op jit(solution)/shard_map/ffn_back_to_attn/pallas_call | solution.py:1050
  521.8 1.2 copy-done.6
  522.9 1.1 copy-done.7
  524.0 1.1 copy-done.8
  526.6 4.5 attend_back.3.refs_0_
  531.1 0.9 copy-done.24
  532.0 0.9 copy-done.26
  533.0 0.9 copy-done.28
  533.9 0.9 copy-done.56
  535.6 73.5 %attn_back_last.1 = (f32[1,2048]{1,0:T(1,128)}, bf16[64,2048]{1,0:T(8,128)(2,1)S(1)}, bf16[64,2048]{1,0:T(8,128)(2,1)S(1)}, f32[2,128]{1,0:T(2,128)S(1)}, bf16[3...) custom-call(bf16[8,2,64,256]{3,2,1,0:T(8,128)(2,1)S(1)} %attend_back, ...), custom_call_target="tpu_custom_call" | custom-call | flops 34359738368 | bytes 8388608 | tf_op jit(solution)/shard_map/attn_back_last/pallas_call | solution.py:1050
  614.3 1.0 copy-done.12
  615.4 1.0 copy-done.14
  616.4 1.0 copy-done.16
  617.4 1.0 copy-done.18
  618.5 0.9 copy-done.32
  619.4 0.9 copy-done.34
  620.3 0.9 copy-done.36
  621.2 6.1 join_sums.1
  627.4 0.9 copy-done.22
  628.3 1.1 maximum_select_fusion
  (167 shorter events, 15.1 us)
Async XLA Ops:
  0.6 5.4 copy-start.44
  0.7 5.4 copy-start.46
  4.8 62.1 %copy-start.23 = (bf16[64,2048]{1,0:T(8,128)(2,1)}, bf16[64,2048]{1,0:T(8,128)(2,1)S(1)}, u32[]{:S(2)}) copy-start(bf16[64,2048]{1,0:T(8,128)(2,1)S(1)} %select_bitcast_fusion.3.refs_0_.refs_1_) | copy-start | bytes 786436
  56.2 2.0 copy-start.54
  59.8 7.1 %copy-start.37 = (f32[1,2048]{1,0:T(1,128)}, f32[1,2048]{1,0:T(1,128)S(1)}, u32[]{:S(2)}) copy-start(f32[1,2048]{1,0:T(1,128)S(1)} %get-tuple-element.176.refs_2_.refs_4_) | copy-start | bytes 24580
  59.8 112.5 %copy-start.39 = (f32[1,2048]{1,0:T(1,128)}, f32[1,2048]{1,0:T(1,128)S(1)}, u32[]{:S(2)}) copy-start(f32[1,2048]{1,0:T(1,128)S(1)} %get-tuple-element.175.refs_2_.refs_3_) | copy-start | bytes 24580
  59.9 1.2 copy-start.49
  61.1 5.9 copy-start.43
  65.8 1.2 copy-start.55
  65.8 2.0 copy-start.42
  65.9 2.5 copy-start.41
  65.9 2.6 copy-start.70
  66.9 105.4 %copy-start.19 = (bf16[1,2,4,16,2048]{4,3,2,1,0:T(8,128)(2,1)}, bf16[1,2,4,16,2048]{4,3,2,1,0:T(8,128)(2,1)S(1)}, u32[]{:S(2)}) copy-start(bf16[1,2,4,16,2048]{4,3,2,1,0:T(8,128)(2,1)S(1)} %copy.32) | copy-start | bytes 1572868
  68.5 103.8 %copy-start.65 = (bf16[128,2048]{1,0:T(8,128)(2,1)S(1)}, bf16[128,2048]{1,0:T(8,128)(2,1)}, u32[]{:S(2)}) copy-start(bf16[128,2048]{1,0:T(8,128)(2,1)} %copy-done.64) | copy-start | bytes 1572868
  167.4 2.0 copy-start.59
  169.4 2.0 copy-start.60
  172.3 59.8 %copy-start.71 = (bf16[352,2048]{1,0:T(8,128)(2,1)}, bf16[352,2048]{1,0:T(8,128)(2,1)S(1)}, u32[]{:S(2)}) copy-start(bf16[352,2048]{1,0:T(8,128)(2,1)S(1)} %get-tuple-element.102.refs_8_.refs_9_) | copy-start | bytes 4325380
  172.3 59.8 %copy-start.73 = (bf16[352,2048]{1,0:T(8,128)(2,1)}, bf16[352,2048]{1,0:T(8,128)(2,1)S(1)}, u32[]{:S(2)}) copy-start(bf16[352,2048]{1,0:T(8,128)(2,1)S(1)} %get-tuple-element.103.refs_9_.refs_10_) | copy-start | bytes 4325380
  172.3 59.8 %copy-start.75 = (bf16[8,2,64,352]{3,2,1,0:T(8,128)(2,1)}, bf16[8,2,64,352]{3,2,1,0:T(8,128)(2,1)S(1)}, u32[]{:S(2)}) copy-start(bf16[8,2,64,352]{3,2,1,0:T(8,128)(2,1)S(1)} %get-tuple-element.94.refs_0_.refs_12_) | copy-start | bytes 2162692
  172.3 59.8 %copy-start.77 = (bf16[8,2,64,352]{3,2,1,0:T(8,128)(2,1)}, bf16[8,2,64,352]{3,2,1,0:T(8,128)(2,1)S(1)}, u32[]{:S(2)}) copy-start(bf16[8,2,64,352]{3,2,1,0:T(8,128)(2,1)S(1)} %get-tuple-element.118.refs_14_) | copy-start | bytes 2162692
  172.3 59.8 %copy-start.81 = (f32[64,2048]{1,0:T(8,128)}, f32[64,2048]{1,0:T(8,128)S(1)}, u32[]{:S(2)}) copy-start(f32[64,2048]{1,0:T(8,128)S(1)} %get-tuple-element.95.refs_1_.refs_2_) | copy-start | bytes 1572868
  172.3 66.6 %copy-start.57 = (bf16[352,2048]{1,0:T(8,128)(2,1)}, bf16[352,2048]{1,0:T(8,128)(2,1)S(1)}, u32[]{:S(2)}) copy-start(bf16[352,2048]{1,0:T(8,128)(2,1)S(1)} %get-tuple-element.97.refs_6_.refs_10_.refs_9_.refs_16_) | copy-start | bytes 4325380
  232.1 2.1 copy-start.62
  234.2 140.6 %copy-start.25 = (bf16[64,2048]{1,0:T(8,128)(2,1)}, bf16[64,2048]{1,0:T(8,128)(2,1)S(1)}, u32[]{:S(2)}) copy-start(bf16[64,2048]{1,0:T(8,128)(2,1)S(1)} %get-tuple-element.99.refs_0_.refs_1_.refs_6_) | copy-start | bytes 786436
  234.2 4.7 copy-start.72
  234.2 4.7 copy-start.74
  303.9 2.0 copy-start.61
  305.9 60.1 %copy-start.63 = (bf16[8,2,64,352]{3,2,1,0:T(8,128)(2,1)}, bf16[8,2,64,352]{3,2,1,0:T(8,128)(2,1)S(1)}, u32[]{:S(2)}) copy-start(bf16[8,2,64,352]{3,2,1,0:T(8,128)(2,1)S(1)} %get-tuple-element.108.refs_5_.refs_4_) | copy-start | bytes 2162692
  305.9 60.1 %copy-start.67 = (f32[64,2048]{1,0:T(8,128)}, f32[64,2048]{1,0:T(8,128)S(1)}, u32[]{:S(2)}) copy-start(f32[64,2048]{1,0:T(8,128)S(1)} %get-tuple-element.107.refs_2_.refs_5_) | copy-start | bytes 1572868
  370.3 4.5 copy-start.20
  370.3 4.5 copy-start.40
  370.3 4.5 copy-start.47
  370.3 4.5 copy-start.58
  370.3 4.5 copy-start.66
  370.3 4.5 copy-start.78
  377.0 65.5 %copy-start.38 = (f32[1,2048]{1,0:T(1,128)S(1)}, f32[1,2048]{1,0:T(1,128)}, u32[]{:S(2)}) copy-start(f32[1,2048]{1,0:T(1,128)} %copy-done.37) | copy-start | bytes 24580
  377.0 65.5 %copy-start.45 = (bf16[1,128,2048]{2,1,0:T(8,128)(2,1)S(1)}, bf16[1,128,2048]{2,1,0:T(8,128)(2,1)}, u32[]{:S(2)}) copy-start(bf16[1,128,2048]{2,1,0:T(8,128)(2,1)} %param.19) | copy-start | bytes 1572868
  377.0 65.5 %copy-start.76 = (bf16[8,2,64,352]{3,2,1,0:T(8,128)(2,1)S(1)}, bf16[8,2,64,352]{3,2,1,0:T(8,128)(2,1)}, u32[]{:S(2)}) copy-start(bf16[8,2,64,352]{3,2,1,0:T(8,128)(2,1)} %copy-done.75) | copy-start | bytes 2162692
  377.0 65.5 %copy-start.82 = (f32[64,2048]{1,0:T(8,128)S(1)}, f32[64,2048]{1,0:T(8,128)}, u32[]{:S(2)}) copy-start(f32[64,2048]{1,0:T(8,128)} %copy-done.81) | copy-start | bytes 1572868
  442.6 79.2 %copy-start.27 = (bf16[64,2048]{1,0:T(8,128)(2,1)}, bf16[64,2048]{1,0:T(8,128)(2,1)S(1)}, u32[]{:S(2)}) copy-start(bf16[64,2048]{1,0:T(8,128)(2,1)S(1)} %get-tuple-element.122.refs_3_.refs_7_) | copy-start | bytes 786436
  442.6 79.2 %copy-start.29 = (bf16[2,16,2048]{2,1,0:T(8,128)(2,1)}, bf16[2,16,2048]{2,1,0:T(8,128)(2,1)S(1)}, u32[]{:S(2)}) copy-start(bf16[2,16,2048]{2,1,0:T(8,128)(2,1)S(1)} %get-tuple-element.162.refs_23_) | copy-start | bytes 393220
  442.6 84.0 %copy-start.51 = (bf16[1024,256]{1,0:T(8,128)(2,1)S(1)}, bf16[1024,256]{1,0:T(8,128)(2,1)}, u32[]{:S(2)}) copy-start(bf16[1024,256]{1,0:T(8,128)(2,1)} %copy-done.50) | copy-start | bytes 1572868
  442.6 84.0 %copy-start.53 = (f32[1024,128]{1,0:T(8,128)S(1)}, f32[1024,128]{1,0:T(8,128)}, u32[]{:S(2)}) copy-start(f32[1024,128]{1,0:T(8,128)} %copy-done.52) | copy-start | bytes 1572868
  535.6 78.7 %copy-start.2 = (bf16[352,2048]{1,0:T(8,128)(2,1)S(1)}, bf16[352,2048]{1,0:T(8,128)(2,1)}, u32[]{:S(2)}) copy-start(bf16[352,2048]{1,0:T(8,128)(2,1)} %copy-done.1) | copy-start | bytes 4325380
  535.6 78.7 %copy-start.4 = (bf16[352,2048]{1,0:T(8,128)(2,1)S(1)}, bf16[352,2048]{1,0:T(8,128)(2,1)}, u32[]{:S(2)}) copy-start(bf16[352,2048]{1,0:T(8,128)(2,1)} %copy-done.3) | copy-start | bytes 4325380
  535.6 78.7 %copy-start.9 = (bf16[352,2048]{1,0:T(8,128)(2,1)S(1)}, bf16[352,2048]{1,0:T(8,128)(2,1)}, u32[]{:S(2)}) copy-start(bf16[352,2048]{1,0:T(8,128)(2,1)} %get-tuple-element.143.refs_1_) | copy-start | bytes 4325380
  535.6 78.7 %copy-start.10 = (bf16[352,2048]{1,0:T(8,128)(2,1)S(1)}, bf16[352,2048]{1,0:T(8,128)(2,1)}, u32[]{:S(2)}) copy-start(bf16[352,2048]{1,0:T(8,128)(2,1)} %get-tuple-element.134.refs_17_.refs_2_) | copy-start | bytes 4325380
  535.6 78.7 %copy-start.30 = (bf16[2,16,2048]{2,1,0:T(8,128)(2,1)S(1)}, bf16[2,16,2048]{2,1,0:T(8,128)(2,1)}, u32[]{:S(2)}) copy-start(bf16[2,16,2048]{2,1,0:T(8,128)(2,1)} %copy-done.29) | copy-start | bytes 393220
  (39 other events, 36.1 us)

commit v3 on v0

--- a/solution.py
+++ b/solution.py
@@ -1,8 +1,12 @@
+import functools
 import math
+import types
 
 import jax
 import jax.numpy as jnp
 from jax import lax
+from jax.experimental import pallas as pl
+from jax.experimental.pallas import tpu as pltpu
 from jax.sharding import PartitionSpec as P
 
 HEADS = 32
@@ -407,6 +411,1435 @@
     )
 
 
+LOW = jnp.bfloat16
+FULL = jnp.float32
+MESH = pl.DeviceIdType.MESH
+RING = 4
+CHIPS = 2 * RING
+SPLIT = 2
+PLACE = 128
+ORDER = ((2, 1), (1, 1), (3, 1), (0, 1), (2, 0), (1, 0), (3, 0), (0, 0))
+IN_VMEM = pl.BlockSpec(memory_space=pltpu.VMEM)
+IN_HBM = pl.BlockSpec(memory_space=pltpu.HBM)
+IN_SMEM = pl.BlockSpec(memory_space=pltpu.SMEM)
+
+
+class Site:
+    def __init__(self):
+        self.section = lax.axis_index("section")
+        self.z = lax.axis_index("shard")
+        member = lax.axis_index("seq")
+        self.y = lax.div(member, 2)
+        self.core = lax.rem(member, 2)
+        self.up = (self.section, lax.rem(self.z + 1, RING), member)
+        self.down = (self.section, lax.rem(self.z + RING - 1, RING), member)
+        self.across = (self.section, self.z, (1 - self.y) * 2 + self.core)
+        self.sibling = (self.section, self.z, self.y * 2 + 1 - self.core)
+        self.corner = (self.section, self.z, (1 - self.y) * 2 + 1 - self.core)
+        self.opposite = (self.section, lax.rem(self.z + 2, RING), member)
+        self.partner = (1 - self.section, self.z, member)
+        self.member = member
+
+    def chip(self, along_z, along_y):
+        return lax.rem(self.z + along_z, RING) * 2 + lax.rem(self.y + along_y, 2)
+
+
+class Links:
+    def __init__(self, send, recv, site):
+        self.send, self.recv, self.site = send, recv, site
+        self.sent = []
+
+    def copy(self, index, src, dst, device):
+        return pltpu.make_async_remote_copy(
+            src_ref=src,
+            dst_ref=dst,
+            send_sem=self.send.at[index],
+            recv_sem=self.recv.at[index],
+            device_id=device,
+            device_id_type=MESH,
+        )
+
+    def go(self, index, src, dst, device):
+        copy = self.copy(index, src, dst, device)
+        copy.start()
+        self.sent.append(copy)
+
+    def got(self, index, where):
+        self.copy(index, where, where, self.site.sibling).wait_recv()
+        return where
+
+    def close(self):
+        for copy in self.sent:
+            copy.wait_send()
+
+
+def greet(site):
+    barrier = pltpu.get_barrier_semaphore()
+    devices = (
+        site.up, site.down, site.across, site.sibling, site.corner, site.opposite, site.partner
+    )
+    for device in devices:
+        pl.semaphore_signal(barrier, inc=1, device_id=device, device_id_type=MESH)
+    pl.semaphore_wait(barrier, len(devices))
+
+
+SPREAD_SEMS = 7 * SPLIT + CHIPS
+FOLD_SEMS = 7 * SPLIT + CHIPS
+SMALL_SEMS = 11
+COPY_SEMS = 48
+CROSS_SEMS = 10
+
+
+class Spread:
+    def __init__(self, site, held, links, use):
+        self.site, self.held, self.links, self.use = site, held, links, use
+        self.size = held.shape[2] // SPLIT
+        self.up, self.down, self.over, self.relay, self.y_below, self.y_above, self.y_far = (
+            k * SPLIT for k in range(7)
+        )
+        self.along = ((0, 0), (3, 0), (1, 0), (0, 1), (2, 0), (3, 1), (1, 1), (2, 1))
+
+    def piece(self, slot, part):
+        site = self.site
+        rows = pl.ds(part * self.size, self.size)
+        return self.held.at[site.chip(*self.along[slot]), site.core, rows]
+
+    def block(self, slot, core):
+        return self.held.at[self.site.chip(*self.along[slot]), core]
+
+    def go(self, index, where, device):
+        self.links.go(index, where, where, device)
+
+    def share(self, slot):
+        self.go(7 * SPLIT + slot, self.block(slot, self.site.core), self.site.sibling)
+
+    def consume(self, *slots):
+        for slot in slots:
+            self.links.got(7 * SPLIT + slot, self.block(slot, 1 - self.site.core))
+            self.use(self.site.chip(*self.along[slot]))
+
+    def own(self, part):
+        where = self.piece(0, part)
+        self.go(self.up + part, where, self.site.up)
+        self.go(self.down + part, where, self.site.down)
+        self.go(self.over + part, where, self.site.across)
+
+    def relays(self, part):
+        came = self.links.got(self.up + part, self.piece(1, part))
+        if part % 2 == 0:
+            self.go(self.relay + part, came, self.site.up)
+        self.go(self.y_below + part, came, self.site.across)
+        came = self.links.got(self.down + part, self.piece(2, part))
+        if part % 2 == 1:
+            self.go(self.relay + part, came, self.site.down)
+        self.go(self.y_above + part, came, self.site.across)
+
+    def far(self, part):
+        came = self.links.got(self.relay + part, self.piece(4, part))
+        self.go(self.y_far + part, came, self.site.across)
+
+    def after_relays(self):
+        self.share(1)
+        self.share(2)
+        for part in range(SPLIT):
+            self.links.got(self.over + part, self.piece(3, part))
+        self.share(3)
+
+    def tail(self, consume=True):
+        def take(*slots):
+            if consume:
+                self.consume(*slots)
+
+        self.share(4)
+        take(0, 1)
+        for part in range(SPLIT):
+            self.links.got(self.y_below + part, self.piece(5, part))
+            self.links.got(self.y_above + part, self.piece(6, part))
+        self.share(5)
+        self.share(6)
+        take(2, 3, 4)
+        for part in range(SPLIT):
+            self.links.got(self.y_far + part, self.piece(7, part))
+        self.share(7)
+        take(5, 6, 7)
+        if not consume:
+            for slot in range(CHIPS):
+                self.links.got(7 * SPLIT + slot, self.block(slot, 1 - self.site.core))
+
+    def rest(self, consume=True):
+        self.after_relays()
+        for part in range(SPLIT):
+            self.far(part)
+        self.tail(consume)
+
+
+class Fold:
+    def __init__(self, site, part_of, buffers, links):
+        self.site, self.part_of, self.links = site, part_of, links
+        self.mine, self.pass_out, self.pass_in, self.stage, self.land = buffers
+        self.rows = self.mine.shape[1]
+        self.size = self.rows // SPLIT
+        self.over = CHIPS
+        self.relay, self.up, self.down = (CHIPS + (4 + k) * SPLIT for k in range(3))
+
+    def where(self, part):
+        return pl.ds(part * self.size, self.size)
+
+    def came(self, index, where):
+        return self.links.got(index, where)[...].astype(FULL)
+
+    def compute(self, step):
+        both = self.part_of(self.site.chip(*ORDER[step]))
+        self.pass_out[step] = both[: self.rows].astype(LOW)
+        self.links.go(step, self.pass_out.at[step], self.pass_in.at[step], self.site.sibling)
+        self.mine[step] = both[self.rows :]
+
+    def settle(self, step):
+        self.mine[step] += self.came(step, self.pass_in.at[step])
+
+    def send(self, index, slot, part, value, device):
+        where = self.where(part)
+        self.stage[slot, where] = value.astype(LOW)
+        self.links.go(index, self.stage.at[slot, where], self.land.at[slot, where], device)
+
+    def send_over(self, step, part):
+        value = self.mine[step, self.where(part)]
+        self.send(self.over + step * SPLIT + part, step, part, value, self.site.across)
+
+    def start(self):
+        self.compute(0)
+        self.compute(1)
+        for step in range(4):
+            self.settle(step)
+            self.send_over(step, 0)
+            self.compute(step + 2)
+        for step in range(4):
+            self.send_over(step, 1)
+        self.compute(6)
+        self.compute(7)
+        for step in range(4, CHIPS):
+            self.settle(step)
+
+    def pass_on(self, part):
+        where = self.where(part)
+        value = self.mine[4, where] + self.came(self.over + part, self.land.at[0, where])
+        device = self.site.up if part % 2 == 0 else self.site.down
+        self.send(self.relay + part, 4, part, value, device)
+
+    def up_down(self, part):
+        where = self.where(part)
+        for step, base, device in ((5, self.up, self.site.up), (6, self.down, self.site.down)):
+            from_y = self.over + (step - 4) * SPLIT + part
+            value = self.mine[step, where] + self.came(from_y, self.land.at[step - 4, where])
+            if part % 2 == step - 5:
+                value = value + self.came(self.relay + part, self.land.at[4, where])
+            self.send(base + part, step, part, value, device)
+
+    def final(self, part):
+        where = self.where(part)
+        value = self.mine[7, where] + self.came(
+            self.over + 3 * SPLIT + part, self.land.at[3, where]
+        )
+        value = value + self.came(self.up + part, self.land.at[5, where])
+        return value + self.came(self.down + part, self.land.at[6, where])
+
+
+def fold_spread(fold, spread, local, idle):
+    def finish(part):
+        rows = local(fold.final(part), fold.where(part))
+        if spread is not None:
+            site = spread.site
+            spread.held[site.chip(0, 0), site.core, fold.where(part)] = rows
+            spread.own(part)
+
+    fold.start()
+    idle(3)
+    fold.pass_on(0)
+    idle(2)
+    fold.up_down(0)
+    fold.pass_on(1)
+    idle(3)
+    finish(0)
+    fold.up_down(1)
+    idle(3)
+    if spread is not None:
+        spread.relays(0)
+    finish(1)
+    if spread is not None:
+        spread.share(0)
+        spread.far(0)
+        idle(2)
+        spread.relays(1)
+        spread.after_relays()
+        spread.far(1)
+        idle(10)
+        spread.tail()
+        spread.links.close()
+    else:
+        idle(10)
+    fold.links.close()
+
+
+class Cross:
+    def __init__(self, n):
+        self.site = n.site
+        self.links = Links(n.cross_send, n.cross_recv, n.site)
+        self.begun = []
+
+    def where(self, layer, receives, action):
+        if layer is None:
+            action()
+        else:
+            pl.when((self.site.section == layer) == receives)(action)
+
+    def send(self, src, dst, layer=None):
+        copy = self.links.copy(len(self.begun), src, dst, self.site.partner)
+        self.begun.append([copy, layer, False])
+        self.where(layer, False, copy.start)
+        return len(self.begun) - 1
+
+    def wait(self, index):
+        copy, layer, landed = self.begun[index]
+        if not landed:
+            self.begun[index][2] = True
+            self.where(layer, True, copy.wait_recv)
+
+    def close(self):
+        for index in range(len(self.begun)):
+            self.wait(index)
+        for copy, layer, _ in self.begun:
+            self.where(layer, False, copy.wait_send)
+
+
+class Copies:
+    def __init__(self, n):
+        self.n, self.count, self.open = n, 0, []
+
+    def sem(self):
+        self.count += 1
+        return self.n.copy_sem.at[self.count - 1]
+
+    def start(self, src, dst):
+        copy = pltpu.make_async_copy(src, dst, self.sem())
+        copy.start()
+        self.open.append(copy)
+        return copy
+
+    def pick(self, own, other, dst, layer):
+        sem = self.sem()
+        from_own = pltpu.make_async_copy(own, dst, sem)
+        from_other = pltpu.make_async_copy(other, dst, sem)
+        pl.when(self.n.site.section == layer)(from_own.start)
+        pl.when(self.n.site.section != layer)(from_other.start)
+        self.open.append(from_own)
+        return from_own
+
+    def wait(self, *copies):
+        for copy in copies:
+            if any(copy is other for other in self.open):
+                self.open = [other for other in self.open if other is not copy]
+                copy.wait()
+
+    def close(self):
+        self.wait(*list(self.open))
+
+
+def kernel_of(body, names, *refs):
+    n = types.SimpleNamespace(**dict(zip(names, refs)))
+    n.site = Site()
+    n.copies = Copies(n)
+    n.cross = Cross(n)
+    body(n)
+    n.cross.close()
+    n.copies.close()
+
+
+def launch(name, ident, body, scalars, inputs, outputs, scratch):
+    scratch = dict(
+        scratch,
+        copy_sem=pltpu.SemaphoreType.DMA((COPY_SEMS,)),
+        cross_send=pltpu.SemaphoreType.DMA((CROSS_SEMS,)),
+        cross_recv=pltpu.SemaphoreType.DMA((CROSS_SEMS,)),
+    )
+    names = [*scalars, *inputs, *outputs, *scratch]
+    results = pl.pallas_call(
+        functools.partial(kernel_of, body, names),
+        out_shape=[jax.ShapeDtypeStruct(*value) for value in outputs.values()],
+        in_specs=[IN_SMEM] * len(scalars) + [IN_HBM] * len(inputs),
+        out_specs=[IN_HBM] * len(outputs),
+        scratch_shapes=list(scratch.values()),
+        compiler_params=pltpu.CompilerParams(
+            collective_id=ident, has_side_effects=True, vmem_limit_bytes=60 * 2**20
+        ),
+        cost_estimate=pl.CostEstimate(flops=2**37, bytes_accessed=2**23, transcendentals=0),
+        name=name,
+    )(*scalars.values(), *inputs.values())
+    return types.SimpleNamespace(**dict(zip(outputs, results)))
+
+
+def fold_buffers(full):
+    return dict(
+        mine=pltpu.VMEM((CHIPS, *full), FULL),
+        pass_out=pltpu.VMEM((CHIPS, *full), LOW),
+        pass_in=pltpu.VMEM((CHIPS, *full), LOW),
+        stage=pltpu.VMEM((CHIPS - 1, *full), LOW),
+        land=pltpu.VMEM((CHIPS - 1, *full), LOW),
+        fold_send=pltpu.SemaphoreType.DMA((FOLD_SEMS,)),
+        fold_recv=pltpu.SemaphoreType.DMA((FOLD_SEMS,)),
+    )
+
+
+def fold_of(n, part_of):
+    buffers = (n.mine, n.pass_out, n.pass_in, n.stage, n.land)
+    return Fold(n.site, part_of, buffers, Links(n.fold_send, n.fold_recv, n.site))
+
+
+def spread_of(n, held, send, recv, use, kept=None):
+    def take(chip):
+        block = held[chip]
+        use(chip, block.reshape(block.shape[0] * block.shape[1], block.shape[2]))
+        if kept is not None:
+            n.copies.start(held.at[chip], kept.at[chip])
+
+    return Spread(n.site, held, Links(send, recv, n.site), take)
+
+
+def spread_sems(*names):
+    return {name: pltpu.SemaphoreType.DMA((SPREAD_SEMS,)) for name in names}
+
+
+def no_idle(count):
+    pass
+
+
+def rows_of(ref, chip, site):
+    return jnp.concatenate([ref[chip, 1 - site.core], ref[chip, site.core]], 0)
+
+
+def put(ref, chip, value):
+    ref[chip] = value.astype(LOW).reshape(ref.shape[1:])
+
+
+def gate_chunk(n, chip, rows):
+    gate_pre = times_trans(rows, n.w_g[...])
+    up_pre = times_trans(rows, n.w_u[...])
+    sig = jax.nn.sigmoid(gate_pre)
+    silu_val = gate_pre * sig
+    put(n.act, chip, silu_val * up_pre)
+    return up_pre * sig * (1.0 + gate_pre * (1.0 - sig)), silu_val
+
+
+def norm_back_rows(values, gain_vec, grad_in):
+    factor = lax.rsqrt(jnp.mean(values * values, -1, keepdims=True) + EPSILON)
+    gain_grad = jnp.sum(grad_in * values * factor, 0, keepdims=True)
+    mean_term = jnp.mean(grad_in * gain_vec * values, -1, keepdims=True)
+    return (
+        gain_grad,
+        factor * gain_vec * grad_in - values * (factor * factor * factor) * mean_term,
+    )
+
+
+def swap_halves(value):
+    width = value.shape[1]
+    half = HEAD_DIM // 2
+    lane = lax.broadcasted_iota(jnp.int32, value.shape, 1)
+    return jnp.where(
+        lax.rem(lane, HEAD_DIM) < half,
+        pltpu.roll(value, width - half, 1),
+        pltpu.roll(value, half, 1),
+    )
+
+
+def stacked(pair):
+    return jnp.concatenate([pair[:, :HEAD_DIM], pair[:, HEAD_DIM:]], 0)
+
+
+def side_by_side(turned):
+    return jnp.concatenate([turned[:, :PLACE], turned[:, PLACE:]], 0).T
+
+
+def hide_later(scores, fill):
+    last = scores[-PLACE:]
+    key = lax.broadcasted_iota(jnp.int32, last.shape, 0)
+    query = lax.rem(lax.broadcasted_iota(jnp.int32, last.shape, 1), PLACE)
+    last = jnp.where(key <= query, last, fill)
+    if scores.shape[0] == PLACE:
+        return last
+    return jnp.concatenate([scores[:-PLACE], last], 0)
+
+
+def turn_of(turns, place):
+    near, far = pl.ds(0, PLACE), pl.ds(PLACE + place, 1)
+    cos_near, sin_near = turns[0, near], turns[1, near]
+    cos_far, sin_far = turns[0, far], turns[1, far]
+    cosine = cos_near * cos_far - sin_near * sin_far
+    sine = sin_near * cos_far + cos_near * sin_far
+    lane = lax.broadcasted_iota(jnp.int32, cosine.shape, 1)
+    sine = jnp.where(lax.rem(lane, HEAD_DIM) < HEAD_DIM // 2, -sine, sine)
+    keyed = lane < HEAD_DIM
+    return (
+        jnp.concatenate([cosine, jnp.where(keyed, cosine, 1.0)], 1),
+        jnp.concatenate([sine, jnp.where(keyed, sine, 0.0)], 1),
+    )
+
+
+def attend(n):
+    q_width = 2 * HEAD_DIM
+    scale = jnp.asarray(1.0 / math.sqrt(HEAD_DIM), LOW)
+    for place in range(CHIPS):
+        at = pl.ds(place * PLACE, PLACE)
+        value = n.qkv[n.block_at[place]]
+        cosine, sine = turn_of(n.turns_v, place)
+        value = (value * cosine + swap_halves(value) * sine).astype(LOW)
+        n.turned_v[at, :q_width] = value[:, :q_width] * scale
+        n.turned_v[at, q_width:] = value[:, q_width:]
+        n.values_t[:, at] = value[:, q_width:].astype(FULL).T[HEAD_DIM:].astype(LOW)
+    for place in range(CHIPS):
+        at = pl.ds(place * PLACE, PLACE)
+        keys = pl.ds(0, (place + 1) * PLACE)
+        query = stacked(n.turned_v[at, :q_width])
+        scores = times_trans(n.turned_v[keys, q_width : q_width + HEAD_DIM], query)
+        scores = hide_later(scores, NEG_LARGE)
+        top = jnp.max(scores, 0, keepdims=True)
+        weight = jnp.exp(scores - top)
+        total = jnp.sum(weight, 0, keepdims=True)
+        out = plain_dot(n.values_t[:, keys], weight.astype(LOW)) / total
+        n.attended_v[place] = side_by_side(out)
+        n.spread_v[pl.ds(place, 1)] = top + jnp.log(total)
+    for block in range(CHIPS):
+        put(n.mixed_v, block, n.attended_v[n.order[block]])
+    n.copies.start(n.turned_v, n.turned)
+    n.copies.start(n.attended_v, n.attended)
+    n.copies.start(n.spread_v, n.spread)
+    n.copies.start(n.mixed_v, n.mixed)
+
+
+def attend_back(n):
+    q_width = 2 * HEAD_DIM
+    n.d_key[...] = jnp.zeros_like(n.d_key)
+    n.d_value[...] = jnp.zeros_like(n.d_value)
+    for place in range(CHIPS):
+        at = pl.ds(place * PLACE, PLACE)
+        n.keys_t[:, at] = n.turned_v[at, q_width:].astype(FULL).T[:HEAD_DIM].astype(LOW)
+    for place in range(CHIPS):
+        at = pl.ds(place * PLACE, PLACE)
+        keys = pl.ds(0, (place + 1) * PLACE)
+        d_out = n.d_mixed[n.block_at[place]]
+        product = (d_out.astype(FULL) * n.attended_v[place]).T
+        offset = jnp.concatenate(
+            [
+                jnp.sum(product[:HEAD_DIM], 0, keepdims=True),
+                jnp.sum(product[HEAD_DIM:], 0, keepdims=True),
+            ],
+            1,
+        )
+        d_out = stacked(d_out)
+        query = stacked(n.turned_v[at, :q_width])
+        scores = times_trans(n.turned_v[keys, q_width : q_width + HEAD_DIM], query)
+        scores = hide_later(scores, NEG_LARGE)
+        probs = jnp.exp(scores - n.spread_v[pl.ds(place, 1)])
+        d_probs = times_trans(n.turned_v[keys, q_width + HEAD_DIM :], d_out)
+        d_scores = (probs * (d_probs - offset)).astype(LOW)
+        n.d_key[keys] += plain_dot(d_scores, query)
+        n.d_value[keys] += plain_dot(probs.astype(LOW), d_out)
+        n.d_query[at] = side_by_side(plain_dot(n.keys_t[:, keys], d_scores)) * (
+            1.0 / math.sqrt(HEAD_DIM)
+        )
+    for place in range(CHIPS):
+        at = pl.ds(place * PLACE, PLACE)
+        value = jnp.concatenate([n.d_query[at], n.d_key[at], n.d_value[at]], 1)
+        cosine, sine = turn_of(n.turns_v, place)
+        value = value * cosine - swap_halves(value) * sine
+        n.d_turned[place] = value.astype(LOW)
+    for block in range(CHIPS):
+        put(n.d_qkv, block, n.d_turned[n.order[block]])
+
+
+def gather_small(n):
+    site = n.site
+    links = n.links_small = Links(n.small_send, n.small_recv, site)
+    links.go(0, n.gains_mine, n.gains_x, site.partner)
+    links.go(1, n.kv_mine, n.kv_x, site.partner)
+    links.got(0, n.gains_x)
+    own, came = n.gains_mine[...], n.gains_x[...]
+    first = site.section == 0
+    n.gains_all[site.z, site.member] = jnp.concatenate(
+        [
+            jnp.where(first, own, came)[:2],
+            jnp.where(first, came, own)[:2],
+            jnp.zeros((4, own.shape[1]), FULL),
+        ],
+        0,
+    )
+    peers = (site.sibling, site.across, site.corner)
+    mine = n.gains_all.at[site.z, site.member]
+    for index, device in enumerate(peers):
+        links.go(2 + index, mine, mine, device)
+    for index, device in enumerate(peers):
+        links.got(2 + index, n.gains_all.at[site.z, device[2]])
+    shard = n.gains_all.at[site.z]
+    for index, device in enumerate((site.up, site.down, site.opposite)):
+        links.go(5 + index, shard, shard, device)
+
+
+def gather_small_keys(n):
+    site, links = n.site, n.links_small
+    links.got(1, n.kv_x)
+    n.kv_all[site.member, site.section] = n.kv_mine[...]
+    n.kv_all[site.member, 1 - site.section] = n.kv_x[...]
+    mine = n.kv_all.at[site.member]
+    for index, device in enumerate((site.sibling, site.across, site.corner)):
+        links.go(8 + index, mine, mine, device)
+
+
+def gather_small_end(n):
+    site, links = n.site, n.links_small
+    for index, along_z in enumerate((RING - 1, 1, 2)):
+        links.got(5 + index, n.gains_all.at[lax.rem(site.z + along_z, RING)])
+    for index, device in enumerate((site.sibling, site.across, site.corner)):
+        links.got(8 + index, n.kv_all.at[device[2]])
+    links.close()
+    n.gains_v[...] = jnp.concatenate(
+        [n.gains_all[shard, seq] for shard in range(RING) for seq in range(RING)], 1
+    )
+    for layer in range(2):
+        for index in range(2):
+            rows = n.kv_all[:, layer, index]
+            n.w_kv[layer, pl.ds(index * HEAD_DIM, HEAD_DIM)] = rows.reshape(
+                HEAD_DIM, rows.shape[-1]
+            )
+    n.copies.start(n.gains_v, n.gains)
+    n.copies.start(n.w_kv, n.kv_rows)
+
+
+def forward_first(n):
+    site, copies, cross = n.site, n.copies, n.cross
+    own = (site.chip(0, 0), site.core)
+    small = [copies.start(n.gains_own, n.gains_mine), copies.start(n.kv_own, n.kv_mine)]
+    rows_copy = copies.start(n.x_rows, n.held.at[own])
+    top_copy = copies.start(n.top_rows, n.top_all.at[own])
+    turns_copy = copies.start(n.turns, n.turns_v)
+    greet(site)
+    copies.wait(*small)
+    gather_small(n)
+    at_query = cross.send(n.w_query, n.x_query)
+    at_out = cross.send(n.w_out, n.x_out)
+    copies.wait(rows_copy)
+
+    def use_first(chip, rows):
+        normed = scaled(rows.astype(FULL), n.gains_v[:1]).astype(LOW)
+        n.normed[chip] = normed.reshape(n.normed.shape[1:])
+        n.qkv[chip] = jnp.concatenate(
+            [times_trans(normed, n.w_q[...]), times_trans(normed, n.w_kv[0])], 1
+        )
+        copies.start(n.normed.at[chip], n.rows_one.at[chip])
+
+    spread = spread_of(n, n.held, n.spread_send, n.spread_recv, use_first)
+    for part in range(SPLIT):
+        spread.own(part)
+    spread.share(0)
+    gather_small_keys(n)
+    for part in range(SPLIT):
+        spread.relays(part)
+    gather_small_end(n)
+    spread.after_relays()
+    cross.wait(at_query)
+    at_gate = cross.send(n.w_gate, n.x_gate)
+    query_copy = copies.pick(n.w_query, n.x_query, n.w_q, 0)
+    for part in range(SPLIT):
+        spread.far(part)
+    copies.wait(query_copy)
+    spread.tail()
+    spread.links.close()
+    copies.wait(top_copy, turns_copy)
+    top = spread_of(n, n.top_all, n.top_send, n.top_recv, None)
+    for part in range(SPLIT):
+        top.own(part)
+    cross.wait(at_out)
+    at_up = cross.send(n.w_up, n.x_up)
+    out_copy = copies.pick(n.w_out, n.x_out, n.w_o, 0)
+    attend(n)
+    top.share(0)
+    for part in range(SPLIT):
+        top.relays(part)
+    copies.wait(out_copy)
+
+    def part_of(chip):
+        return plain_dot(rows_of(n.mixed_v, chip, site), n.w_o[...])
+
+    def local(total, where):
+        hidden_in = n.held[(*own, where)].astype(FULL) + total
+        n.hidden_v[where] = hidden_in
+        return scaled(hidden_in, n.gains_v[1:2]).astype(LOW)
+
+    def use_gate(chip, rows):
+        gate_slope, up_slope = gate_chunk(n, chip, rows)
+        put(n.gate_slope_v, chip, gate_slope)
+        put(n.up_slope_v, chip, up_slope)
+
+    started = []
+
+    def idle(count):
+        started.append(count)
+        if len(started) == 5:
+            top.after_relays()
+            for part in range(SPLIT):
+                top.far(part)
+        if len(started) == 6:
+            cross.wait(at_gate)
+            started.append(cross.send(n.w_down, n.x_down))
+            cross.wait(at_up)
+            gate_copies = (
+                copies.pick(n.w_gate, n.x_gate, n.w_g, 0),
+                copies.pick(n.w_up, n.x_up, n.w_u, 0),
+            )
+            copies.wait(*gate_copies)
+
+    spread = spread_of(
+        n, n.held_two, n.spread_two_send, n.spread_two_recv, use_gate, n.rows_two
+    )
+    fold_spread(fold_of(n, part_of), spread, local, idle)
+    copies.start(n.hidden_v, n.hidden)
+    for source, target in (
+        (n.act, n.act_all), (n.gate_slope_v, n.gate_slope), (n.up_slope_v, n.up_slope)
+    ):
+        copies.start(source, target)
+    top.tail(consume=False)
+    top.links.close()
+
+
+def forward_second(n):
+    site, copies = n.site, n.copies
+    first = [
+        copies.start(n.act_prev, n.act_prev_v),
+        copies.pick(n.w_down, n.x_down, n.w_d_prev, 0),
+    ]
+    rows_copies = [copies.start(n.hidden_prev, n.hidden_prev_v), copies.start(n.gains, n.gains_v)]
+    qkv_copies = [
+        copies.pick(n.w_query, n.x_query, n.w_in.at[pl.ds(0, 2 * HEAD_DIM)], 1),
+        copies.start(n.kv_rows.at[1], n.w_in.at[pl.ds(2 * HEAD_DIM, 2 * HEAD_DIM)]),
+        copies.start(n.turns, n.turns_v),
+    ]
+    later = [
+        copies.pick(n.w_out, n.x_out, n.w_o, 1),
+        copies.pick(n.w_gate, n.x_gate, n.w_g, 1),
+        copies.pick(n.w_up, n.x_up, n.w_u, 1),
+        copies.pick(n.w_down, n.x_down, n.w_d, 1),
+        copies.start(n.top_all, n.top_held),
+    ]
+    greet(site)
+    copies.wait(*first, *rows_copies)
+
+    def part_of(chip):
+        return plain_dot(rows_of(n.act_prev_v, chip, site), n.w_d_prev[...])
+
+    def local(total, where):
+        result = (n.hidden_prev_v[where] + total).astype(LOW)
+        n.result_v[where] = result
+        return scaled(result.astype(FULL), n.gains_v[2:3]).astype(LOW)
+
+    def use_qkv(chip, rows):
+        n.qkv[chip] = times_trans(rows, n.w_in[...])
+
+    def settle(count):
+        copies.wait(*qkv_copies)
+
+    spread = spread_of(n, n.held, n.spread_send, n.spread_recv, use_qkv, n.rows_one)
+    fold_spread(fold_of(n, part_of), spread, local, settle)
+    copies.start(n.result_v, n.result)
+    attend(n)
+    copies.wait(*later)
+
+    def part_of_two(chip):
+        return plain_dot(rows_of(n.mixed_v, chip, site), n.w_o[...])
+
+    def local_two(total, where):
+        hidden_in = n.result_v[where].astype(FULL) + total
+        n.hidden_v[where] = hidden_in
+        return scaled(hidden_in, n.gains_v[3:4]).astype(LOW)
+
+    def use_gate(chip, rows):
+        gate_slope, up_slope = gate_chunk(n, chip, rows)
+        d_act = times_trans(n.top_held[chip].reshape(rows.shape), n.w_d[...])
+        put(n.d_gate_v, chip, d_act * gate_slope)
+        put(n.d_up_v, chip, d_act * up_slope)
+
+    spread = spread_of(
+        n, n.held_two, n.spread_two_send, n.spread_two_recv, use_gate, n.rows_two
+    )
+    fold_spread(fold_of(n, part_of_two), spread, local_two, no_idle)
+    for source, target in (
+        (n.hidden_v, n.hidden), (n.act, n.act_all), (n.d_gate_v, n.d_gate), (n.d_up_v, n.d_up)
+    ):
+        copies.start(source, target)
+
+
+def products(n, left, right, store, tile=512):
+    count = math.prod(left.shape[:-1])
+    for start in range(0, right.shape[-1], tile):
+        where = pl.ds(start, tile)
+        value = outer_sum(
+            left[...].reshape(count, left.shape[-1]), right[:, :, :, where].reshape(count, tile)
+        )
+        store(where, value.astype(LOW))
+        yield
+
+
+def ffn_products(n, loads, made):
+    n.copies.wait(*loads)
+    for left, right, out in (
+        (n.act, n.top_held, n.g_down_v),
+        (n.d_gate_v, n.normed, n.g_gate_v),
+        (n.d_up_v, n.normed, n.g_up_v),
+    ):
+
+        def store(where, value):
+            out[:, where] = value
+
+        yield from products(n, left, right, store)
+        made(out)
+
+
+def in_products(n, loads, made):
+    site = n.site
+    n.copies.wait(*loads)
+
+    def store_out(where, value):
+        n.g_out_v[:, where] = value
+
+    def store_in(where, value):
+        query = n.g_query_v.shape[0]
+        n.g_query_v[:, where] = value[:query]
+        n.kv_mine[:, :, :, where] = value[query:].reshape(
+            *n.kv_mine.shape[:3], value.shape[1]
+        )
+
+    yield from products(n, n.d_qkv, n.normed, store_in)
+    made(n.g_query_v)
+    peers = (site.sibling, site.across, site.corner)
+    links = Links(n.kv_send, n.kv_recv, site)
+    for index, device in enumerate(peers):
+        links.go(index, n.kv_mine.at[:, device[2]], n.kv_came.at[index], device)
+    yield from products(n, n.mixed_v, n.held, store_out)
+    made(n.g_out_v)
+    total = n.kv_mine[:, site.member].astype(FULL)
+    for index in range(len(peers)):
+        total = total + links.got(index, n.kv_came.at[index])[...].astype(FULL)
+    n.g_kv_v[...] = total.astype(LOW)
+    made(n.g_kv_v)
+    links.close()
+
+
+def fold_gains(n):
+    site = n.site
+    links = Links(n.gain_send, n.gain_recv, site)
+    own = jnp.concatenate(
+        [n.gain_grads[...], n.gain_later_v[...], jnp.zeros((4, n.gain_grads.shape[1]), FULL)], 0
+    )
+    width = n.gain_parts.shape[-1]
+    for shard in range(RING):
+        for seq in range(RING):
+            start = (shard * RING + seq) * width
+            n.gain_parts[seq, shard] = own[:, start : start + width]
+    peers = (site.sibling, site.across, site.corner)
+    for index, device in enumerate(peers):
+        links.go(index, n.gain_parts.at[device[2]], n.gain_came.at[index], device)
+    yield
+    total = n.gain_parts[site.member]
+    for index in range(3):
+        total = total + links.got(index, n.gain_came.at[index])[...]
+    n.gain_shards[...] = total
+    for index, device in enumerate((site.up, site.down, site.opposite)):
+        links.go(
+            3 + index, n.gain_shards.at[device[1]], n.gain_last.at[index], device
+        )
+    yield
+    total = n.gain_shards[site.z]
+    for index in range(3):
+        total = total + links.got(3 + index, n.gain_last.at[index])[...]
+    n.gain_own[...] = total
+    links.go(6, n.gain_own, n.gain_other, site.partner)
+    yield
+    total = n.gain_own[...] + links.got(6, n.gain_other)[...]
+    n.gain_sums_v[...] = jnp.where(site.section == 0, total[:2], total[2:4])
+    links.close()
+    n.copies.start(n.gain_sums_v, n.gain_sums)
+
+
+def backward(layer, n):
+    site, copies, cross = n.site, n.copies, n.cross
+    first = [
+        copies.start(n.d_gate, n.d_gate_v),
+        copies.start(n.d_up, n.d_up_v),
+        copies.pick(n.w_gate, n.x_gate, n.w_g, layer),
+        copies.pick(n.w_up, n.x_up, n.w_u, layer),
+    ]
+    rows_copies = [
+        copies.start(n.hidden, n.hidden_v),
+        copies.start(n.top_rows, n.top_v),
+        copies.start(n.gains, n.gains_v),
+        copies.pick(n.w_out, n.x_out, n.w_o, layer),
+    ]
+    loads = [
+        copies.start(n.act_all, n.act),
+        copies.start(n.top_all, n.top_held),
+        copies.start(n.rows_two, n.normed),
+    ]
+    attn_copies = [
+        copies.start(n.turns, n.turns_v),
+        copies.start(n.turned, n.turned_v),
+        copies.start(n.attended, n.attended_v),
+        copies.start(n.spread, n.spread_v),
+        copies.start(n.mixed, n.mixed_v),
+        copies.pick(n.w_query, n.x_query, n.w_in.at[pl.ds(0, 2 * HEAD_DIM)], layer),
+        copies.start(n.kv_rows.at[layer], n.w_in.at[pl.ds(2 * HEAD_DIM, 2 * HEAD_DIM)]),
+        copies.start(n.x_rows, n.x_v),
+    ]
+    if layer == 1:
+        next_copies = [
+            copies.pick(n.w_down, n.x_down, n.w_d, 0),
+            copies.start(n.gate_slope, n.gate_slope_v),
+            copies.start(n.up_slope, n.up_slope_v),
+        ]
+    else:
+        next_copies = [
+            copies.pick(n.w_down, n.x_down, n.w_d, 1),
+            copies.start(n.act_last, n.act_last_v),
+            copies.start(n.hidden_last, n.hidden_last_v),
+            copies.start(n.gain_later, n.gain_later_v),
+        ]
+    greet(site)
+    if layer == 1:
+        cross.send(n.x_rows, n.came_result_first, 0)
+    else:
+        cross.send(n.own_up_later, n.came_up_later, 1)
+        cross.send(n.top_rows, n.came_input_later, 1)
+    copies.wait(*first, *rows_copies)
+
+    def made(out):
+        target, came = {
+            id(n.g_down_v): (n.own_down, n.came_down),
+            id(n.g_gate_v): (n.own_gate, n.came_gate),
+            id(n.g_up_v): (n.own_up, None if layer == 1 else n.came_up),
+            id(n.g_out_v): (n.own_out, n.came_out),
+            id(n.g_query_v): (n.own_query, n.came_query),
+            id(n.g_kv_v): (n.own_kv, n.came_kv),
+        }[id(out)]
+        copies.start(out, target)
+        if came is not None:
+            cross.send(out, came, layer)
+
+    def step_on(working):
+        def idle(count):
+            for _ in range(count):
+                next(working, None)
+
+        return idle
+
+    def part_of(chip):
+        return plain_dot(rows_of(n.d_gate_v, chip, site), n.w_g[...]) + plain_dot(
+            rows_of(n.d_up_v, chip, site), n.w_u[...]
+        )
+
+    def add_gain(row, value, where):
+        row = pl.ds(row, 1)
+        n.gain_grads[row] = value if where.start == 0 else n.gain_grads[row] + value
+
+    def local(total, where):
+        gain_grad, d_hidden = norm_back_rows(
+            n.hidden_v[where], n.gains_v[2 * layer + 1 : 2 * layer + 2], total
+        )
+        d_hidden = d_hidden + n.top_v[where].astype(FULL)
+        add_gain(1, gain_grad, where)
+        n.d_hidden[where] = d_hidden
+        return d_hidden.astype(LOW)
+
+    def use_d_mixed(chip, rows):
+        n.d_mixed[chip] = times_trans(rows, n.w_o[...]).astype(LOW)
+
+    working = ffn_products(n, loads, made)
+    spread = spread_of(n, n.held, n.spread_send, n.spread_recv, use_d_mixed)
+    fold_spread(fold_of(n, part_of), spread, local, step_on(working))
+    for _ in working:
+        pass
+    normed_copy = copies.start(n.rows_one, n.normed)
+    copies.wait(*attn_copies)
+    attend_back(n)
+    copies.wait(*next_copies)
+
+    def part_of_two(chip):
+        return plain_dot(rows_of(n.d_qkv, chip, site), n.w_in[...])
+
+    def local_two(total, where):
+        gain_grad, d_input = norm_back_rows(
+            n.x_v[where].astype(FULL), n.gains_v[2 * layer : 2 * layer + 1], total
+        )
+        d_input = (d_input + n.d_hidden[where]).astype(LOW)
+        add_gain(0, gain_grad, where)
+        n.d_input_v[where] = d_input
+        return d_input
+
+    working = in_products(n, [normed_copy], made)
+    if layer == 1:
+
+        def use_d_act(chip, rows):
+            d_act = times_trans(rows, n.w_d[...])
+            for out, slope in ((n.d_gate_v, n.gate_slope_v), (n.d_up_v, n.up_slope_v)):
+                put(out, chip, d_act * slope[chip].astype(FULL).reshape(d_act.shape))
+
+        spread = spread_of(
+            n, n.held_two, n.spread_two_send, n.spread_two_recv, use_d_act, n.top_next
+        )
+        fold_spread(fold_of(n, part_of_two), spread, local_two, step_on(working))
+        for _ in working:
+            pass
+        for source, target in (
+            (n.d_gate_v, n.d_gate_next), (n.d_up_v, n.d_up_next), (n.d_input_v, n.d_input),
+            (n.gain_grads, n.gain_out),
+        ):
+            copies.start(source, target)
+        return
+    fold_spread(fold_of(n, part_of_two), None, local_two, step_on(working))
+    for _ in working:
+        pass
+    copies.start(n.d_input_v, n.d_input)
+    cross.send(n.d_input_v, n.came_input, 0)
+
+    def part_of_last(chip):
+        return plain_dot(rows_of(n.act_last_v, chip, site), n.w_d[...])
+
+    def local_last(total, where):
+        n.result_v[where] = (n.hidden_last_v[where] + total).astype(LOW)
+
+    buffers = (n.mine, n.pass_out, n.pass_in_two, n.stage, n.land_two)
+    links = Links(n.last_send, n.last_recv, site)
+    gains_on = fold_gains(n)
+    next(gains_on)
+    fold_spread(
+        Fold(site, part_of_last, buffers, links), None, local_last,
+        lambda count: next(gains_on, None),
+    )
+    for _ in gains_on:
+        pass
+    copies.start(n.result_v, n.result)
+    cross.send(n.result_v, n.came_result, 1)
+
+
+def join_kernel(count, *refs):
+    own, came = (refs[:count], refs[count : 2 * count]), (
+        refs[2 * count : 3 * count],
+        refs[3 * count : 4 * count],
+    )
+    outs, refs = refs[4 * count : 5 * count], refs[5 * count :]
+    own_at, came_at, sums = refs[:count], refs[count : 2 * count], refs[2 * count : 3 * count]
+    sems, out_sem = refs[3 * count :]
+    section = lax.axis_index("section")
+    waits = []
+    for index in range(count):
+        for slot, (pair, target) in enumerate(((own, own_at), (came, came_at))):
+            copies = [
+                pltpu.make_async_copy(
+                    pair[layer][index], target[index], sems.at[2 * index + slot]
+                )
+                for layer in range(2)
+            ]
+            pl.when(section == 0)(copies[0].start)
+            pl.when(section != 0)(copies[1].start)
+            waits.append(copies[0])
+    done = []
+    for index in range(count):
+        waits[2 * index].wait()
+        waits[2 * index + 1].wait()
+        sums[index][...] = own_at[index][...].astype(FULL) + came_at[index][...].astype(FULL)
+        copy = pltpu.make_async_copy(sums[index], outs[index], out_sem.at[index])
+        copy.start()
+        done.append(copy)
+    for copy in done:
+        copy.wait()
+
+
+def join_sums(own_a, own_b, came_a, came_b):
+    count = len(own_a)
+    kept = [pltpu.VMEM(value.shape, LOW) for value in own_a]
+    return pl.pallas_call(
+        functools.partial(join_kernel, count),
+        out_shape=[jax.ShapeDtypeStruct(value.shape, FULL) for value in own_a],
+        in_specs=[IN_HBM] * (4 * count),
+        out_specs=[IN_HBM] * count,
+        scratch_shapes=kept
+        + kept
+        + [pltpu.VMEM(value.shape, FULL) for value in own_a]
+        + [pltpu.SemaphoreType.DMA((2 * count,)), pltpu.SemaphoreType.DMA((count,))],
+        compiler_params=pltpu.CompilerParams(vmem_limit_bytes=40 * 2**20),
+        cost_estimate=pl.CostEstimate(flops=2**32, bytes_accessed=2**24, transcendentals=0),
+        name="join_sums",
+    )(*own_a, *own_b, *came_a, *came_b)
+
+
+def relay_body(
+    inputs,
+    cotangent,
+    positions,
+    gain_attn,
+    w_query,
+    w_key,
+    w_value,
+    w_out,
+    gain_ffn,
+    w_gate,
+    w_up,
+    w_down,
+):
+    n_micro, per_device, model_width = inputs.shape
+    n_seq = lax.axis_size("seq")
+    n_shard = lax.axis_size("shard")
+    members = n_seq * n_shard
+    total_len = members * per_device
+    section_idx = lax.axis_index("section")
+    q_width = HEADS // members * HEAD_DIM
+    in_width = q_width + 2 * HEAD_DIM
+    hidden = w_down.shape[1]
+    vmem = pltpu.VMEM
+
+    def pick(first, second):
+        return jnp.where(section_idx == 0, first, second)
+
+    x_rows = pick(inputs[0], inputs[1])
+    top_rows = pick(cotangent[0], cotangent[1])
+    places = pick(positions[0], positions[1])
+    gains_own = jnp.concatenate(
+        [gain_attn, gain_ffn, jnp.zeros((6, gain_attn.shape[1]), gain_attn.dtype)], 0
+    ).astype(FULL)
+    kv_own = jnp.stack([w_key[0], w_value[0]])
+    own = dict(
+        w_query=w_query[0], w_out=w_out[0], w_gate=w_gate[0], w_up=w_up[0], w_down=w_down[0]
+    )
+
+    order = (places.reshape(CHIPS, PLACE)[:, 0] // PLACE).astype(jnp.int32)
+    numbers = jnp.arange(CHIPS, dtype=jnp.int32)
+    block_at = jnp.sum(
+        jnp.where(order[None, :] == numbers[:, None], numbers[None, :], 0), 1
+    ).astype(jnp.int32)
+    scalars = dict(block_at=block_at, order=order)
+    half_dim = HEAD_DIM // 2
+    inv_freq = THETA_BASE ** (-jnp.arange(half_dim, dtype=FULL) * (2.0 / HEAD_DIM))
+    steps = jnp.concatenate([jnp.arange(PLACE), PLACE * jnp.arange(CHIPS)]).astype(FULL)
+    angles = steps[:, None] * jnp.tile(inv_freq, 2 * q_width // HEAD_DIM)[None, :]
+    turns = jnp.stack([jnp.cos(angles), jnp.sin(angles)])
+
+    rows = (per_device, model_width)
+    row_low, row_full = (rows, LOW), (rows, FULL)
+    all_rows = ((CHIPS, 2, *rows), LOW)
+    narrow = ((CHIPS, 2, per_device, hidden), LOW)
+    wide = ((hidden, model_width), LOW)
+    quarter = ((q_width, model_width), LOW)
+    gain_row = ((8, model_width), FULL)
+    kv_shape = (2, w_key.shape[1], model_width)
+    small = gains_own.shape
+    saved = dict(
+        turned=((total_len, in_width), LOW),
+        attended=((CHIPS, PLACE, q_width), FULL),
+        spread=((CHIPS, 2 * PLACE), FULL),
+        mixed=((CHIPS, 2, per_device, q_width), LOW),
+    )
+    saved_v = dict(
+        turned_v=vmem(*saved["turned"]),
+        attended_v=vmem(*saved["attended"]),
+        spread_v=vmem(*saved["spread"]),
+        mixed_v=vmem(*saved["mixed"]),
+        turns_v=vmem(turns.shape, FULL),
+    )
+    attend_v = dict(
+        **saved_v,
+        qkv=vmem((CHIPS, PLACE, in_width), FULL),
+        values_t=vmem((HEAD_DIM, total_len), LOW),
+    )
+    gates_v = dict(w_g=vmem(*wide), w_u=vmem(*wide))
+
+    first = launch(
+        "forward_first",
+        0,
+        forward_first,
+        scalars,
+        dict(
+            x_rows=x_rows, top_rows=top_rows, gains_own=gains_own, kv_own=kv_own, turns=turns,
+            **own,
+        ),
+        dict(
+            x_query=quarter,
+            x_out=quarter,
+            x_gate=wide,
+            x_up=wide,
+            x_down=wide,
+            gains=gain_row,
+            kv_rows=((2, 2 * HEAD_DIM, model_width), LOW),
+            top_all=all_rows,
+            rows_one=all_rows,
+            rows_two=all_rows,
+            hidden=row_full,
+            act_all=narrow,
+            gate_slope=narrow,
+            up_slope=narrow,
+            **saved,
+        ),
+        dict(
+            gains_mine=vmem(small, FULL),
+            gains_x=vmem(small, FULL),
+            gains_all=vmem((n_shard, n_seq, *small), FULL),
+            gains_v=vmem(*gain_row),
+            kv_mine=vmem(kv_shape, LOW),
+            kv_x=vmem(kv_shape, LOW),
+            kv_all=vmem((n_seq, 2, *kv_shape), LOW),
+            w_kv=vmem((2, 2 * HEAD_DIM, model_width), LOW),
+            small_send=pltpu.SemaphoreType.DMA((SMALL_SEMS,)),
+            small_recv=pltpu.SemaphoreType.DMA((SMALL_SEMS,)),
+            held=vmem(*all_rows),
+            held_two=vmem(*all_rows),
+            normed=vmem(*all_rows),
+            w_q=vmem(*quarter),
+            w_o=vmem(*quarter),
+            hidden_v=vmem(*row_full),
+            act=vmem(*narrow),
+            gate_slope_v=vmem(*narrow),
+            up_slope_v=vmem(*narrow),
+            **gates_v,
+            **attend_v,
+            **fold_buffers(rows),
+            **spread_sems(
+                "spread_send", "spread_recv", "spread_two_send", "spread_two_recv", "top_send",
+                "top_recv",
+            ),
+        ),
+    )
+    crossed = dict(
+        **own,
+        x_query=first.x_query,
+        x_out=first.x_out,
+        x_gate=first.x_gate,
+        x_up=first.x_up,
+        x_down=first.x_down,
+        gains=first.gains,
+        kv_rows=first.kv_rows,
+        turns=turns,
+    )
+    second = launch(
+        "forward_second",
+        1,
+        forward_second,
+        scalars,
+        dict(
+            act_prev=first.act_all, hidden_prev=first.hidden, top_all=first.top_all, **crossed
+        ),
+        dict(
+            result=row_low,
+            rows_one=all_rows,
+            rows_two=all_rows,
+            hidden=row_full,
+            act_all=narrow,
+            d_gate=narrow,
+            d_up=narrow,
+            **saved,
+        ),
+        dict(
+            act_prev_v=vmem(*narrow),
+            hidden_prev_v=vmem(*row_full),
+            gains_v=vmem(*gain_row),
+            w_d_prev=vmem(*wide),
+            w_in=vmem((in_width, model_width), LOW),
+            w_o=vmem(*quarter),
+            w_d=vmem(*wide),
+            top_held=vmem(*all_rows),
+            held=vmem(*all_rows),
+            held_two=vmem(*all_rows),
+            result_v=vmem(*row_low),
+            hidden_v=vmem(*row_full),
+            act=vmem(*narrow),
+            d_gate_v=vmem(*narrow),
+            d_up_v=vmem(*narrow),
+            **gates_v,
+            **attend_v,
+            **fold_buffers(rows),
+            **spread_sems("spread_send", "spread_recv", "spread_two_send", "spread_two_recv"),
+        ),
+    )
+
+    kv_pair = ((2, *kv_shape[1:]), LOW)
+    own_sums = dict(
+        own_down=wide, own_gate=wide, own_up=wide, own_out=quarter, own_query=quarter,
+        own_kv=kv_pair,
+    )
+    came_sums = dict(
+        came_down=wide, came_gate=wide, came_out=quarter, came_query=quarter, came_kv=kv_pair
+    )
+    back_v = dict(
+        d_gate_v=vmem(*narrow),
+        d_up_v=vmem(*narrow),
+        act=vmem(*narrow),
+        hidden_v=vmem(*row_full),
+        top_v=vmem(*row_low),
+        x_v=vmem(*row_low),
+        d_hidden=vmem(*row_full),
+        d_input_v=vmem(*row_low),
+        gains_v=vmem(*gain_row),
+        gain_grads=vmem((2, model_width), FULL),
+        w_o=vmem(*quarter),
+        w_in=vmem((in_width, model_width), LOW),
+        w_d=vmem(*wide),
+        top_held=vmem(*all_rows),
+        normed=vmem(*all_rows),
+        held=vmem(*all_rows),
+        d_mixed=vmem((CHIPS, PLACE, q_width), LOW),
+        d_qkv=vmem((CHIPS, 2, per_device, in_width), LOW),
+        d_turned=vmem((CHIPS, PLACE, in_width), LOW),
+        d_query=vmem((total_len, q_width), FULL),
+        d_key=vmem((total_len, HEAD_DIM), FULL),
+        d_value=vmem((total_len, HEAD_DIM), FULL),
+        keys_t=vmem((HEAD_DIM, total_len), LOW),
+        g_down_v=vmem(*wide),
+        g_gate_v=vmem(*wide),
+        g_up_v=vmem(*wide),
+        g_out_v=vmem(*quarter),
+        g_query_v=vmem(*quarter),
+        g_kv_v=vmem(*kv_pair),
+        kv_mine=vmem((2, n_seq, *kv_shape[1:]), LOW),
+        kv_came=vmem((n_seq - 1, 2, *kv_shape[1:]), LOW),
+        kv_send=pltpu.SemaphoreType.DMA((n_seq - 1,)),
+        kv_recv=pltpu.SemaphoreType.DMA((n_seq - 1,)),
+        **gates_v,
+        **saved_v,
+        **fold_buffers(rows),
+    )
+
+    def back_in(done, layer_rows, top, d_gate, d_up, top_all):
+        return dict(
+            d_gate=d_gate,
+            d_up=d_up,
+            hidden=done.hidden,
+            top_rows=top,
+            x_rows=layer_rows,
+            act_all=done.act_all,
+            top_all=top_all,
+            rows_one=done.rows_one,
+            rows_two=done.rows_two,
+            **{key: getattr(done, key) for key in saved},
+            **crossed,
+        )
+
+    third = launch(
+        "backward_second",
+        2,
+        functools.partial(backward, 1),
+        scalars,
+        dict(
+            **back_in(
+                second, second.result, top_rows, second.d_gate, second.d_up, first.top_all
+            ),
+            gate_slope=first.gate_slope,
+            up_slope=first.up_slope,
+        ),
+        dict(
+            d_gate_next=narrow,
+            d_up_next=narrow,
+            top_next=all_rows,
+            d_input=row_low,
+            gain_out=((2, model_width), FULL),
+            came_result_first=row_low,
+            **own_sums,
+            **came_sums,
+        ),
+        dict(
+            gate_slope_v=vmem(*narrow),
+            up_slope_v=vmem(*narrow),
+            held_two=vmem(*all_rows),
+            **back_v,
+            **spread_sems("spread_send", "spread_recv", "spread_two_send", "spread_two_recv"),
+        ),
+    )
+    fourth = launch(
+        "backward_first",
+        3,
+        functools.partial(backward, 0),
+        scalars,
+        dict(
+            **back_in(
+                first, x_rows, third.d_input, third.d_gate_next, third.d_up_next, third.top_next
+            ),
+            own_up_later=third.own_up,
+            gain_later=third.gain_out,
+            act_last=second.act_all,
+            hidden_last=second.hidden,
+        ),
+        dict(
+            d_input=row_low,
+            result=row_low,
+            gain_sums=((2, small[1]), FULL),
+            came_up=wide,
+            came_up_later=wide,
+            came_input=row_low,
+            came_input_later=row_low,
+            came_result=row_low,
+            **own_sums,
+            **came_sums,
+        ),
+        dict(
+            act_last_v=vmem(*narrow),
+            hidden_last_v=vmem(*row_full),
+            gain_later_v=vmem((2, model_width), FULL),
+            result_v=vmem(*row_low),
+            pass_in_two=vmem((CHIPS, *rows), LOW),
+            land_two=vmem((CHIPS - 1, *rows), LOW),
+            last_send=pltpu.SemaphoreType.DMA((FOLD_SEMS,)),
+            last_recv=pltpu.SemaphoreType.DMA((FOLD_SEMS,)),
+            gain_parts=vmem((n_seq, n_shard, *small), FULL),
+            gain_came=vmem((n_seq - 1, n_shard, *small), FULL),
+            gain_shards=vmem((n_shard, *small), FULL),
+            gain_last=vmem((n_shard - 1, *small), FULL),
+            gain_own=vmem(small, FULL),
+            gain_other=vmem(small, FULL),
+            gain_sums_v=vmem((2, small[1]), FULL),
+            gain_send=pltpu.SemaphoreType.DMA((7,)),
+            gain_recv=pltpu.SemaphoreType.DMA((7,)),
+            **back_v,
+            **spread_sems("spread_send", "spread_recv"),
+        ),
+    )
+
+    def joined(kept, came):
+        return pick(jnp.stack([kept, came]), jnp.stack([came, kept]))[None]
+
+    outputs = joined(
+        pick(second.result, fourth.result),
+        pick(third.came_result_first, fourth.came_result),
+    )
+    input_grads = joined(
+        pick(fourth.d_input, third.d_input), pick(fourth.came_input, fourth.came_input_later)
+    )
+    g_down, g_gate, g_up, g_out, g_query, g_kv = join_sums(
+        [fourth.own_down, fourth.own_gate, fourth.own_up, fourth.own_out, fourth.own_query, fourth.own_kv],
+        [third.own_down, third.own_gate, third.own_up, third.own_out, third.own_query, third.own_kv],
+        [fourth.came_down, fourth.came_gate, fourth.came_up, fourth.came_out, fourth.came_query, fourth.came_kv],
+        [third.came_down, third.came_gate, fourth.came_up_later, third.came_out, third.came_query, third.came_kv],
+    )
+    return (
+        outputs,
+        input_grads,
+        fourth.gain_sums[:1],
+        g_query[None],
+        g_kv[:1],
+        g_kv[1:],
+        g_out[None],
+        fourth.gain_sums[1:],
+        g_gate[None],
+        g_up[None],
+        g_down[None],
+    )
+
+
+def fits_relay(mesh):
+    shape = mesh.shape
+    return shape["section"] == 2 and shape["shard"] == KV_HEADS == RING and shape["seq"] == 4
+
+
 def solution(mesh):
     in_specs = (
         P(None, ("shard", "seq"), None),
@@ -435,4 +1868,5 @@
         P("section", ("shard", "seq"), None),
         P("section", ("shard", "seq"), None),
     )
-    return jax.shard_map(body, mesh=mesh, in_specs=in_specs, out_specs=out_specs, check_vma=False)
+    chosen = relay_body if fits_relay(mesh) else body
+    return jax.shard_map(chosen, mesh=mesh, in_specs=in_specs, out_specs=out_specs, check_vma=False)

time: 2390 us -> 590 us (0.25)
  waiting for transfers between devices: 1420 us -> 0 us
  Pallas kernels: 0 us -> 557 us
  matrix products: 316 us -> 0 us
  blocking collectives: 293 us -> 0 us
  local copies, waits for them, and re-layouts: 153 us -> 7.4 us
  other arithmetic: 120 us -> 12.2 us
  starting transfers between devices: 63.4 us -> 0 us
    reduce_scatter x16 -> x0, waiting for transfers between devices: 962 us -> none  [the longest x6 546 us: fold_rows(): lax.psum_scatter(block_in, ('shard', 'seq'), scatter_dimension=0, tiled=T...]
    pallas_call x0 -> x5, Pallas kernels: none -> 557 us  [the longest x4 551 us: launch(): pl.pallas_call(functools.partial(kernel_of, body, names), out_shape=[jax....]
    all_gather x10 -> x0, waiting for transfers between devices: 407 us -> none  [the longest x6 282 us: spread_rows(): return lax.all_gather(block_in, ('shard', 'seq'), axis=0, tiled=True)]
    dot_general x76 -> x0, matrix products: 316 us -> none  [the longest x21 88 us: plain_dot(): return jnp.dot(left, right, preferred_element_type=jnp.float32)]
    all_gather x14 -> x0, blocking collectives: 212 us -> none  [the longest x6 84.3 us: over_keys(): lax.all_gather(head_values, 'shard', axis=0, tiled=True)]
    unnamed x329 -> x45, local copies, waits for them, and re-layouts: 84.7 us -> 5.99 us
    unnamed x1 -> x0, blocking collectives: 59.2 us -> none
    all_to_all x13 -> x0, starting transfers between devices: 51 us -> none  [the longest x6 23.8 us: to_heads(): lax.all_to_all(block_in, 'seq', split_axis=1, concat_axis=0, tiled=True)]
  transfers between devices with their start and end apart: 43 -> 0, of which waited for: 31 -> 0; matrix products, arithmetic and copies ran while one was open for 10% -> 0% of each run, Pallas kernels for 0% -> 0%
where the time goes in v3:
time: 590 us; the launch traced here: 579 us
  Pallas kernels  557 us (94%)
  other arithmetic  12.2 us (2%)
  local copies, waits for them, and re-layouts  7.4 us (1%)
    pallas_call x4, Pallas kernels, launch(): pl.pallas_call(functools.partial(kernel_of, body, names), out_shape=[jax....  551 us

profile of v3, /device:TPU:0, one launch (start us, length us, event | category | flops | bytes accessed | tf_op | source)
XLA Modules:
  0.0 578.5 jit_solution(17716128497437535310)
XLA Ops:
  0.6 0.0 copy-start.18
  0.7 0.1 pad.16.clone
  0.8 0.1 mul.45
  0.9 1.3 maximum_convert_fusion.refs_4_
  2.2 0.8 broadcast_select_fusion
  3.0 0.1 copy.25
  3.1 0.6 select_reduce_fusion.refs_0_
  3.7 1.5 pad_maximum_fusion.1.refs_5_
  5.3 0.3 multiply_cosine_fusion
  5.6 0.7 pad_maximum_fusion.refs_6_.refs_17_.refs_27_
  6.3 1.8 select_bitcast_fusion.5.refs_2_.refs_6_
  8.0 0.0 copy-done.18
  8.0 0.7 select_bitcast_fusion.4.refs_3_.refs_5_
  8.8 0.0 copy-done.21
  8.8 143.2 %forward_first.1 = (bf16[128,2048]{1,0:T(8,128)(2,1)}, bf16[128,2048]{1,0:T(8,128)(2,1)}, bf16[352,2048]{1,0:T(8,128)(2,1)}, bf16[352,2048]{1,0:T(8,128)(2,1)}, ...) custom-call(s32[8]{0:T(128)} %select_reduce_fusion.refs_0_, ...), custom_call_target="tpu_custom_call" | custom-call | flops 137438953472 | bytes 8388608 | tf_op jit(solution)/shard_map/forward_first/pallas_call | solution.py:765
  151.9 130.4 %forward_second.1 = (bf16[64,2048]{1,0:T(8,128)(2,1)}, bf16[8,2,64,2048]{3,2,1,0:T(8,128)(2,1)}, bf16[8,2,64,2048]{3,2,1,0:T(8,128)(2,1)}, f32[64,2048]{1,0:T(8,...) custom-call(s32[8]{0:T(128)} %select_reduce_fusion.refs_0_, ...), custom_call_target="tpu_custom_call" | custom-call | flops 137438953472 | bytes 8388608 | tf_op jit(solution)/shard_map/forward_second/pallas_call | solution.py:765
  282.3 124.5 %backward_second.1 = (bf16[8,2,64,352]{3,2,1,0:T(8,128)(2,1)}, bf16[8,2,64,352]{3,2,1,0:T(8,128)(2,1)}, bf16[8,2,64,2048]{3,2,1,0:T(8,128)(2,1)}, bf16[64,2048]{...) custom-call(s32[8]{0:T(128)} %select_reduce_fusion.refs_0_, ...), custom_call_target="tpu_custom_call" | custom-call | flops 137438953472 | bytes 8388608 | tf_op jit(solution)/shard_map/backward_second/pallas_call | solution.py:765
  406.8 0.0 copy-start.19
  406.8 0.0 copy-start.2
  406.8 0.0 copy-start.6
  406.8 0.0 copy-start.7
  406.8 0.0 copy-start.8
  406.9 0.0 copy-start.9
  406.9 0.0 copy-start.14
  406.9 0.0 copy-start.15
  406.9 153.3 %backward_first.1 = (bf16[64,2048]{1,0:T(8,128)(2,1)}, bf16[64,2048]{1,0:T(8,128)(2,1)}, f32[2,128]{1,0:T(2,128)}, bf16[352,2048]{1,0:T(8,128)(2,1)}, bf16[352,2...) custom-call(s32[8]{0:T(128)} %select_reduce_fusion.refs_0_, ...), custom_call_target="tpu_custom_call" | custom-call | flops 137438953472 | bytes 8388608 | tf_op jit(solution)/shard_map/backward_first/pallas_call | solution.py:765
  560.2 0.0 copy-start.20
  560.2 0.0 copy-start.10
  560.3 0.0 copy-start.17
  560.3 1.1 select_bitcast_fusion.1
  561.3 0.0 copy-done.19
  561.3 0.0 copy-start.3
  561.4 0.0 copy-start.16
  561.4 1.1 select_bitcast_fusion.2
  562.5 0.0 copy-done.20
  562.5 0.5 fusion.1
  563.0 1.1 select_bitcast_fusion
  564.2 1.1 maximum_select_fusion
  565.3 0.0 copy-done.2
  565.3 0.0 copy-done.6
  565.3 0.0 copy-done.7
  565.4 1.4 copy-done.4
  566.8 1.4 copy-done.5
  568.1 1.0 copy-done.11
  569.2 1.0 copy-done.12
  570.2 1.0 copy-done.13
  571.3 6.1 %join_sums.1 = (f32[352,2048]{1,0:T(8,128)}, f32[352,2048]{1,0:T(8,128)}, f32[352,2048]{1,0:T(8,128)}, f32[128,2048]{1,0:T(8,128)}, f32[128,2048]{1,0:T(8,128)}, /*index=5*/f32[2,16,2048]{2,1,0:T(8,128)S(1)}) custom-call(bf16[352,2048]{1,0:T(8,128)(2,1)S(1)} %copy-done.3, bf16[352,2048]{1,0:T(8,128)(2,1)S(1)} %copy-done.4, bf16[352,2048]{1,0:T(8,128)(2,1)S(1)} %copy-done.5, ...), custom_call_target="tpu_custom_call" | custom-call | flops 4294967296 | bytes 16777216 | tf_op jit(solution)/shard_map/join_sums/pallas_call | solution.py:1464
  577.4 0.7 fusion
  (26 shorter events, 0.1 us)
Async XLA Ops:
  0.6 7.4 %copy-start.18 = (bf16[2,64,2048]{2,1,0:T(8,128)(2,1)S(1)}, bf16[2,64,2048]{2,1,0:T(8,128)(2,1)}, u32[]{:S(2)}) copy-start(bf16[2,64,2048]{2,1,0:T(8,128)(2,1)} %param.13) | copy-start | bytes 1572868
  3.1 5.7 copy-start.21
  406.8 154.5 %copy-start.19 = (bf16[64,2048]{1,0:T(8,128)(2,1)S(1)}, bf16[64,2048]{1,0:T(8,128)(2,1)}, u32[]{:S(2)}) copy-start(bf16[64,2048]{1,0:T(8,128)(2,1)} %get-tuple-element.92.refs_6_) | copy-start | bytes 786436
  406.8 158.5 %copy-start.2 = (bf16[352,2048]{1,0:T(8,128)(2,1)S(1)}, bf16[352,2048]{1,0:T(8,128)(2,1)}, u32[]{:S(2)}) copy-start(bf16[352,2048]{1,0:T(8,128)(2,1)} %get-tuple-element.115.refs_28_.refs_8_) | copy-start | bytes 4325380
  406.8 158.5 %copy-start.6 = (bf16[128,2048]{1,0:T(8,128)(2,1)S(1)}, bf16[128,2048]{1,0:T(8,128)(2,1)}, u32[]{:S(2)}) copy-start(bf16[128,2048]{1,0:T(8,128)(2,1)} %get-tuple-element.132.refs_9_) | copy-start | bytes 1572868
  406.8 158.5 %copy-start.7 = (bf16[128,2048]{1,0:T(8,128)(2,1)S(1)}, bf16[128,2048]{1,0:T(8,128)(2,1)}, u32[]{:S(2)}) copy-start(bf16[128,2048]{1,0:T(8,128)(2,1)} %get-tuple-element.133.refs_10_) | copy-start | bytes 1572868
  406.8 158.5 %copy-start.8 = (bf16[128,2048]{1,0:T(8,128)(2,1)S(1)}, bf16[128,2048]{1,0:T(8,128)(2,1)}, u32[]{:S(2)}) copy-start(bf16[128,2048]{1,0:T(8,128)(2,1)} %get-tuple-element.144.refs_21_) | copy-start | bytes 1572868
  406.9 158.5 %copy-start.9 = (bf16[128,2048]{1,0:T(8,128)(2,1)S(1)}, bf16[128,2048]{1,0:T(8,128)(2,1)}, u32[]{:S(2)}) copy-start(bf16[128,2048]{1,0:T(8,128)(2,1)} %get-tuple-element.145.refs_22_) | copy-start | bytes 1572868
  406.9 158.5 %copy-start.14 = (bf16[2,16,2048]{2,1,0:T(8,128)(2,1)S(1)}, bf16[2,16,2048]{2,1,0:T(8,128)(2,1)}, u32[]{:S(2)}) copy-start(bf16[2,16,2048]{2,1,0:T(8,128)(2,1)} %get-tuple-element.134.refs_11_) | copy-start | bytes 393220
  406.9 158.5 %copy-start.15 = (bf16[2,16,2048]{2,1,0:T(8,128)(2,1)S(1)}, bf16[2,16,2048]{2,1,0:T(8,128)(2,1)}, u32[]{:S(2)}) copy-start(bf16[2,16,2048]{2,1,0:T(8,128)(2,1)} %get-tuple-element.146.refs_23_) | copy-start | bytes 393220
  560.2 2.3 copy-start.20
  560.2 5.1 copy-start.10
  560.3 5.1 copy-start.17
  561.3 4.0 copy-start.3
  561.4 4.0 copy-start.16
  563.0 2.4 copy-start
  563.0 2.4 copy-start.1
  565.4 1.4 copy-start.4
  566.8 1.4 copy-start.5
  568.1 1.0 copy-start.11
  569.2 1.0 copy-start.12
  570.2 1.0 copy-start.13

commit v4 on v3

--- a/solution.py
+++ b/solution.py
@@ -417,6 +417,7 @@
 RING = 4
 CHIPS = 2 * RING
 SPLIT = 2
+LAG = (0, 0, 1, 2, 3)
 PLACE = 128
 ORDER = ((2, 1), (1, 1), (3, 1), (0, 1), (2, 0), (1, 0), (3, 0), (0, 0))
 IN_VMEM = pl.BlockSpec(memory_space=pltpu.VMEM)
@@ -487,7 +488,8 @@
 FOLD_SEMS = 7 * SPLIT + CHIPS
 SMALL_SEMS = 11
 COPY_SEMS = 48
-CROSS_SEMS = 10
+CROSS_SEMS = 32
+PIECE = 128
 
 
 class Spread:
@@ -545,19 +547,19 @@
             self.links.got(self.over + part, self.piece(3, part))
         self.share(3)
 
-    def tail(self, consume=True):
+    def tail(self, consume=True, first=0):
         def take(*slots):
             if consume:
                 self.consume(*slots)
 
         self.share(4)
-        take(0, 1)
+        take(*range(first, 3))
         for part in range(SPLIT):
             self.links.got(self.y_below + part, self.piece(5, part))
             self.links.got(self.y_above + part, self.piece(6, part))
         self.share(5)
         self.share(6)
-        take(2, 3, 4)
+        take(3, 4)
         for part in range(SPLIT):
             self.links.got(self.y_far + part, self.piece(7, part))
         self.share(7)
@@ -613,8 +615,9 @@
             self.settle(step)
             self.send_over(step, 0)
             self.compute(step + 2)
-        for step in range(4):
-            self.send_over(step, 1)
+        for part in range(1, SPLIT):
+            for step in range(4):
+                self.send_over(step, part)
         self.compute(6)
         self.compute(7)
         for step in range(4, CHIPS):
@@ -654,26 +657,30 @@
 
     fold.start()
     idle(3)
-    fold.pass_on(0)
-    idle(2)
-    fold.up_down(0)
-    fold.pass_on(1)
-    idle(3)
-    finish(0)
-    fold.up_down(1)
-    idle(3)
+    last = SPLIT - 1
+    for tick in range(SPLIT + LAG[-1]):
+        steps = [tick - lag for lag in LAG]
+        if 0 <= steps[0] < SPLIT:
+            fold.pass_on(steps[0])
+        if 0 <= steps[1] < SPLIT:
+            fold.up_down(steps[1])
+        if 0 <= steps[2] < SPLIT:
+            finish(steps[2])
+        if spread is not None:
+            if steps[2] == last:
+                spread.share(0)
+            if 0 <= steps[3] < SPLIT:
+                spread.relays(steps[3])
+            if steps[3] == last:
+                spread.after_relays()
+            if 0 <= steps[4] < SPLIT:
+                spread.far(steps[4])
+            if steps[2] == last + 1:
+                spread.consume(0)
+        idle(3)
     if spread is not None:
-        spread.relays(0)
-    finish(1)
-    if spread is not None:
-        spread.share(0)
-        spread.far(0)
-        idle(2)
-        spread.relays(1)
-        spread.after_relays()
-        spread.far(1)
         idle(10)
-        spread.tail()
+        spread.tail(first=1)
         spread.links.close()
     else:
         idle(10)
@@ -685,6 +692,7 @@
         self.site = n.site
         self.links = Links(n.cross_send, n.cross_recv, n.site)
         self.begun = []
+        self.count = 0
 
     def where(self, layer, receives, action):
         if layer is None:
@@ -693,22 +701,47 @@
             pl.when((self.site.section == layer) == receives)(action)
 
     def send(self, src, dst, layer=None):
-        copy = self.links.copy(len(self.begun), src, dst, self.site.partner)
-        self.begun.append([copy, layer, False])
-        self.where(layer, False, copy.start)
+        rows = src.shape[0]
+        pieces = []
+        start = 0
+        while start < rows:
+            size = min(PIECE, rows - start)
+            where = pl.ds(start, size)
+            pieces.append(
+                self.links.copy(self.count, src.at[where], dst.at[where], self.site.partner)
+            )
+            self.count += 1
+            start += size
+
+        def begin():
+            for copy in pieces:
+                copy.start()
+
+        self.where(layer, False, begin)
+        self.begun.append([pieces, layer, False])
         return len(self.begun) - 1
 
     def wait(self, index):
-        copy, layer, landed = self.begun[index]
+        pieces, layer, landed = self.begun[index]
+
+        def arrive():
+            for copy in pieces:
+                copy.wait_recv()
+
         if not landed:
             self.begun[index][2] = True
-            self.where(layer, True, copy.wait_recv)
+            self.where(layer, True, arrive)
 
     def close(self):
         for index in range(len(self.begun)):
             self.wait(index)
-        for copy, layer, _ in self.begun:
-            self.where(layer, False, copy.wait_send)
+        for pieces, layer, _ in self.begun:
+
+            def leave():
+                for copy in pieces:
+                    copy.wait_send()
+
+            self.where(layer, False, leave)
 
 
 class Copies:
@@ -1015,15 +1048,27 @@
 def forward_first(n):
     site, copies, cross = n.site, n.copies, n.cross
     own = (site.chip(0, 0), site.core)
-    small = [copies.start(n.gains_own, n.gains_mine), copies.start(n.kv_own, n.kv_mine)]
-    rows_copy = copies.start(n.x_rows, n.held.at[own])
-    top_copy = copies.start(n.top_rows, n.top_all.at[own])
+    small = [
+        copies.start(n.gains_own, n.gains_mine),
+        copies.start(n.w_key, n.kv_mine.at[0]),
+        copies.start(n.w_value, n.kv_mine.at[1]),
+    ]
+    rows_copy = copies.pick(n.inputs.at[0], n.inputs.at[1], n.held.at[own], 0)
+    top_copy = copies.pick(n.cotangent.at[0], n.cotangent.at[1], n.top_v, 0)
     turns_copy = copies.start(n.turns, n.turns_v)
     greet(site)
     copies.wait(*small)
     gather_small(n)
-    at_query = cross.send(n.w_query, n.x_query)
-    at_out = cross.send(n.w_out, n.x_out)
+    at_query, at_out, at_gate, at_up, _ = (
+        cross.send(*pair)
+        for pair in (
+            (n.w_query, n.x_query),
+            (n.w_out, n.x_out),
+            (n.w_gate, n.x_gate),
+            (n.w_up, n.x_up),
+            (n.w_down, n.x_down),
+        )
+    )
     copies.wait(rows_copy)
 
     def use_first(chip, rows):
@@ -1044,24 +1089,22 @@
     gather_small_end(n)
     spread.after_relays()
     cross.wait(at_query)
-    at_gate = cross.send(n.w_gate, n.x_gate)
     query_copy = copies.pick(n.w_query, n.x_query, n.w_q, 0)
     for part in range(SPLIT):
         spread.far(part)
     copies.wait(query_copy)
+    copies.wait(top_copy, turns_copy)
+    top_copy = copies.start(n.top_v, n.top_all.at[own])
     spread.tail()
     spread.links.close()
-    copies.wait(top_copy, turns_copy)
+    copies.wait(top_copy)
     top = spread_of(n, n.top_all, n.top_send, n.top_recv, None)
     for part in range(SPLIT):
         top.own(part)
     cross.wait(at_out)
-    at_up = cross.send(n.w_up, n.x_up)
     out_copy = copies.pick(n.w_out, n.x_out, n.w_o, 0)
     attend(n)
     top.share(0)
-    for part in range(SPLIT):
-        top.relays(part)
     copies.wait(out_copy)
 
     def part_of(chip):
@@ -1072,34 +1115,37 @@
         n.hidden_v[where] = hidden_in
         return scaled(hidden_in, n.gains_v[1:2]).astype(LOW)
 
-    def use_gate(chip, rows):
+    waiting = []
+
+    def use_later(chip, rows):
+        waiting.append(chip)
+
+    def use_gate(chip):
+        rows = n.held_two[chip].reshape(-1, n.held_two.shape[-1])
         gate_slope, up_slope = gate_chunk(n, chip, rows)
         put(n.gate_slope_v, chip, gate_slope)
         put(n.up_slope_v, chip, up_slope)
 
-    started = []
-
     def idle(count):
-        started.append(count)
-        if len(started) == 5:
-            top.after_relays()
+        if count == 10:
             for part in range(SPLIT):
-                top.far(part)
-        if len(started) == 6:
-            cross.wait(at_gate)
-            started.append(cross.send(n.w_down, n.x_down))
-            cross.wait(at_up)
-            gate_copies = (
-                copies.pick(n.w_gate, n.x_gate, n.w_g, 0),
-                copies.pick(n.w_up, n.x_up, n.w_u, 0),
-            )
-            copies.wait(*gate_copies)
+                top.relays(part)
 
     spread = spread_of(
-        n, n.held_two, n.spread_two_send, n.spread_two_recv, use_gate, n.rows_two
+        n, n.held_two, n.spread_two_send, n.spread_two_recv, use_later, n.rows_two
     )
     fold_spread(fold_of(n, part_of), spread, local, idle)
     copies.start(n.hidden_v, n.hidden)
+    top.after_relays()
+    for part in range(SPLIT):
+        top.far(part)
+    cross.wait(at_gate)
+    cross.wait(at_up)
+    copies.wait(
+        copies.pick(n.w_gate, n.x_gate, n.w_g, 0), copies.pick(n.w_up, n.x_up, n.w_u, 0)
+    )
+    for chip in waiting:
+        use_gate(chip)
     for source, target in (
         (n.act, n.act_all), (n.gate_slope_v, n.gate_slope), (n.up_slope_v, n.up_slope)
     ):
@@ -1276,7 +1322,9 @@
     ]
     rows_copies = [
         copies.start(n.hidden, n.hidden_v),
-        copies.start(n.top_rows, n.top_v),
+        copies.pick(n.cotangent.at[0], n.cotangent.at[1], n.top_v, 0)
+        if layer == 1
+        else copies.start(n.top_rows, n.top_v),
         copies.start(n.gains, n.gains_v),
         copies.pick(n.w_out, n.x_out, n.w_o, layer),
     ]
@@ -1293,7 +1341,9 @@
         copies.start(n.mixed, n.mixed_v),
         copies.pick(n.w_query, n.x_query, n.w_in.at[pl.ds(0, 2 * HEAD_DIM)], layer),
         copies.start(n.kv_rows.at[layer], n.w_in.at[pl.ds(2 * HEAD_DIM, 2 * HEAD_DIM)]),
-        copies.start(n.x_rows, n.x_v),
+        copies.start(n.x_rows, n.x_v)
+        if layer == 1
+        else copies.pick(n.inputs.at[0], n.inputs.at[1], n.x_v, 0),
     ]
     if layer == 1:
         next_copies = [
@@ -1358,6 +1408,8 @@
         n.d_mixed[chip] = times_trans(rows, n.w_o[...]).astype(LOW)
 
     working = ffn_products(n, loads, made)
+    if layer == 0:
+        step_on(working)(5)
     spread = spread_of(n, n.held, n.spread_send, n.spread_recv, use_d_mixed)
     fold_spread(fold_of(n, part_of), spread, local, step_on(working))
     for _ in working:
@@ -1426,54 +1478,93 @@
 
 
 def join_kernel(count, *refs):
-    own, came = (refs[:count], refs[count : 2 * count]), (
-        refs[2 * count : 3 * count],
-        refs[3 * count : 4 * count],
-    )
-    outs, refs = refs[4 * count : 5 * count], refs[5 * count :]
-    own_at, came_at, sums = refs[:count], refs[count : 2 * count], refs[2 * count : 3 * count]
-    sems, out_sem = refs[3 * count :]
+    def take(number):
+        nonlocal refs
+        taken, refs = refs[:number], refs[number:]
+        return taken
+
+    own, came = (take(count), take(count)), (take(count), take(count))
+    rows = (take(4), take(4))
+    outs, row_outs = take(count + 1), take(2)
+    own_at, came_at, sums = take(count), take(count), take(count)
+    row_at, sems, out_sem, row_sem = refs
     section = lax.axis_index("section")
+
+    def either(first, second):
+        pl.when(section == 0)(first.start)
+        pl.when(section != 0)(second.start)
+        return first
+
     waits = []
     for index in range(count):
         for slot, (pair, target) in enumerate(((own, own_at), (came, came_at))):
-            copies = [
-                pltpu.make_async_copy(
-                    pair[layer][index], target[index], sems.at[2 * index + slot]
+            waits.append(
+                either(
+                    *(
+                        pltpu.make_async_copy(
+                            pair[layer][index], target[index], sems.at[2 * index + slot]
+                        )
+                        for layer in range(2)
+                    )
                 )
-                for layer in range(2)
-            ]
-            pl.when(section == 0)(copies[0].start)
-            pl.when(section != 0)(copies[1].start)
-            waits.append(copies[0])
+            )
     done = []
+    row_waits = []
+    for index, (own_a, own_b, came_a, came_b) in enumerate(rows):
+        for slot, (first, second) in enumerate(((own_a, came_b), (came_a, own_b))):
+            target, sem = row_at.at[index, slot], row_sem.at[2 * index + slot]
+            row_waits.append(
+                either(
+                    pltpu.make_async_copy(first, target, sem),
+                    pltpu.make_async_copy(second, target, sem),
+                )
+            )
+    for copy in row_waits:
+        copy.wait()
+    for index, out in enumerate(row_outs):
+        copy = pltpu.make_async_copy(row_at.at[index], out, row_sem.at[index])
+        copy.start()
+        done.append(copy)
     for index in range(count):
         waits[2 * index].wait()
         waits[2 * index + 1].wait()
         sums[index][...] = own_at[index][...].astype(FULL) + came_at[index][...].astype(FULL)
-        copy = pltpu.make_async_copy(sums[index], outs[index], out_sem.at[index])
-        copy.start()
-        done.append(copy)
+        if index < count - 1:
+            parts = [(sums[index], outs[index])]
+        else:
+            parts = [(sums[index].at[pl.ds(k, 1)], outs[index + k]) for k in range(2)]
+        for source, target in parts:
+            copy = pltpu.make_async_copy(source, target, out_sem.at[len(done) - 2])
+            copy.start()
+            done.append(copy)
     for copy in done:
         copy.wait()
 
 
-def join_sums(own_a, own_b, came_a, came_b):
+def join_all(own_a, own_b, came_a, came_b, results, input_grads):
     count = len(own_a)
     kept = [pltpu.VMEM(value.shape, LOW) for value in own_a]
+    shapes = [value.shape for value in own_a]
+    shapes = shapes[:-1] + [(1, *shapes[-1][1:])] * 2
+    row_shape = jax.ShapeDtypeStruct((2, *results[0].shape), LOW)
     return pl.pallas_call(
         functools.partial(join_kernel, count),
-        out_shape=[jax.ShapeDtypeStruct(value.shape, FULL) for value in own_a],
-        in_specs=[IN_HBM] * (4 * count),
-        out_specs=[IN_HBM] * count,
+        out_shape=[jax.ShapeDtypeStruct(value, FULL) for value in shapes] + [row_shape] * 2,
+        in_specs=[IN_HBM] * (4 * count + 8),
+        out_specs=[IN_HBM] * (count + 3),
         scratch_shapes=kept
         + kept
         + [pltpu.VMEM(value.shape, FULL) for value in own_a]
-        + [pltpu.SemaphoreType.DMA((2 * count,)), pltpu.SemaphoreType.DMA((count,))],
-        compiler_params=pltpu.CompilerParams(vmem_limit_bytes=40 * 2**20),
+        + [
+            pltpu.VMEM((2, *row_shape.shape), LOW),
+            pltpu.SemaphoreType.DMA((2 * count,)),
+            pltpu.SemaphoreType.DMA((count + 1,)),
+            pltpu.SemaphoreType.DMA((4,)),
+        ],
+        compiler_params=pltpu.CompilerParams(vmem_limit_bytes=58 * 2**20),
         cost_estimate=pl.CostEstimate(flops=2**32, bytes_accessed=2**24, transcendentals=0),
-        name="join_sums",
-    )(*own_a, *own_b, *came_a, *came_b)
+        name="join_all",
+    )(*own_a, *own_b, *came_a, *came_b, *results, *input_grads)
 
 
 def relay_body(
@@ -1504,13 +1595,10 @@
     def pick(first, second):
         return jnp.where(section_idx == 0, first, second)
 
-    x_rows = pick(inputs[0], inputs[1])
-    top_rows = pick(cotangent[0], cotangent[1])
     places = pick(positions[0], positions[1])
     gains_own = jnp.concatenate(
         [gain_attn, gain_ffn, jnp.zeros((6, gain_attn.shape[1]), gain_attn.dtype)], 0
     ).astype(FULL)
-    kv_own = jnp.stack([w_key[0], w_value[0]])
     own = dict(
         w_query=w_query[0], w_out=w_out[0], w_gate=w_gate[0], w_up=w_up[0], w_down=w_down[0]
     )
@@ -1562,8 +1650,8 @@
         forward_first,
         scalars,
         dict(
-            x_rows=x_rows, top_rows=top_rows, gains_own=gains_own, kv_own=kv_own, turns=turns,
-            **own,
+            inputs=inputs, cotangent=cotangent, gains_own=gains_own, w_key=w_key[0],
+            w_value=w_value[0], turns=turns, **own,
         ),
         dict(
             x_query=quarter,
@@ -1599,6 +1687,7 @@
             w_q=vmem(*quarter),
             w_o=vmem(*quarter),
             hidden_v=vmem(*row_full),
+            top_v=vmem(*row_low),
             act=vmem(*narrow),
             gate_slope_v=vmem(*narrow),
             up_slope_v=vmem(*narrow),
@@ -1710,13 +1799,11 @@
         **fold_buffers(rows),
     )
 
-    def back_in(done, layer_rows, top, d_gate, d_up, top_all):
+    def back_in(done, d_gate, d_up, top_all):
         return dict(
             d_gate=d_gate,
             d_up=d_up,
             hidden=done.hidden,
-            top_rows=top,
-            x_rows=layer_rows,
             act_all=done.act_all,
             top_all=top_all,
             rows_one=done.rows_one,
@@ -1731,9 +1818,9 @@
         functools.partial(backward, 1),
         scalars,
         dict(
-            **back_in(
-                second, second.result, top_rows, second.d_gate, second.d_up, first.top_all
-            ),
+            **back_in(second, second.d_gate, second.d_up, first.top_all),
+            x_rows=second.result,
+            cotangent=cotangent,
             gate_slope=first.gate_slope,
             up_slope=first.up_slope,
         ),
@@ -1761,9 +1848,9 @@
         functools.partial(backward, 0),
         scalars,
         dict(
-            **back_in(
-                first, x_rows, third.d_input, third.d_gate_next, third.d_up_next, third.top_next
-            ),
+            **back_in(first, third.d_gate_next, third.d_up_next, third.top_next),
+            inputs=inputs,
+            top_rows=third.d_input,
             own_up_later=third.own_up,
             gain_later=third.gain_out,
             act_last=second.act_all,
@@ -1804,29 +1891,25 @@
         ),
     )
 
-    def joined(kept, came):
-        return pick(jnp.stack([kept, came]), jnp.stack([came, kept]))[None]
-
-    outputs = joined(
-        pick(second.result, fourth.result),
-        pick(third.came_result_first, fourth.came_result),
-    )
-    input_grads = joined(
-        pick(fourth.d_input, third.d_input), pick(fourth.came_input, fourth.came_input_later)
-    )
-    g_down, g_gate, g_up, g_out, g_query, g_kv = join_sums(
-        [fourth.own_down, fourth.own_gate, fourth.own_up, fourth.own_out, fourth.own_query, fourth.own_kv],
-        [third.own_down, third.own_gate, third.own_up, third.own_out, third.own_query, third.own_kv],
-        [fourth.came_down, fourth.came_gate, fourth.came_up, fourth.came_out, fourth.came_query, fourth.came_kv],
-        [third.came_down, third.came_gate, fourth.came_up_later, third.came_out, third.came_query, third.came_kv],
+    def sums(of, done):
+        return [getattr(done, f"{of}_{key}") for key in ("down", "gate", "up", "out", "query", "kv")]
+
+    third.came_up = fourth.came_up_later
+    g_down, g_gate, g_up, g_out, g_query, g_key, g_value, outputs, input_grads = join_all(
+        sums("own", fourth),
+        sums("own", third),
+        sums("came", fourth),
+        sums("came", third),
+        (second.result, fourth.result, third.came_result_first, fourth.came_result),
+        (fourth.d_input, third.d_input, fourth.came_input, fourth.came_input_later),
     )
     return (
-        outputs,
-        input_grads,
+        outputs[None],
+        input_grads[None],
         fourth.gain_sums[:1],
         g_query[None],
-        g_kv[:1],
-        g_kv[1:],
+        g_key,
+        g_value,
         g_out[None],
         fourth.gain_sums[1:],
         g_gate[None],

time: 590 us -> 543 us (0.920)
  Pallas kernels: 557 us -> 528 us
  other arithmetic: 12.2 us -> 3.77 us
  local copies, waits for them, and re-layouts: 7.4 us -> 0.78 us
    pallas_call x4, Pallas kernels: 551 us -> 519 us  [launch(): pl.pallas_call(functools.partial(kernel_of, body, names), out_shape=[jax....]
    unnamed x45 -> x5, local copies, waits for them, and re-layouts: 5.99 us -> 0.09 us
where the time goes in v4:
time: 543 us; the launch traced here: 534 us
  Pallas kernels  528 us (97%)
    pallas_call x4, Pallas kernels, launch(): pl.pallas_call(functools.partial(kernel_of, body, names), out_shape=[jax....  519 us

profile of v4, /device:TPU:0, one launch (start us, length us, event | category | flops | bytes accessed | tf_op | source)
XLA Modules:
  0.0 534.2 jit_solution(12974015566430547845)
XLA Ops:
  0.7 0.1 pad.6.clone
  0.8 0.1 mul.45
  0.9 1.3 maximum_convert_fusion.refs_4_
  2.2 0.8 broadcast_select_fusion
  3.0 0.1 copy.25
  3.1 0.0 copy-start.1
  3.1 0.6 select_reduce_fusion.refs_0_
  3.7 0.3 multiply_cosine_fusion
  4.0 0.7 pad_maximum_fusion.refs_7_.refs_17_.refs_25_
  4.7 0.0 copy-done.1
  4.7 131.8 %forward_first.1 = (bf16[128,2048]{1,0:T(8,128)(2,1)}, bf16[128,2048]{1,0:T(8,128)(2,1)}, bf16[352,2048]{1,0:T(8,128)(2,1)}, bf16[352,2048]{1,0:T(8,128)(2,1)}, ...) custom-call(s32[8]{0:T(128)} %select_reduce_fusion.refs_0_, ...), custom_call_target="tpu_custom_call" | custom-call | flops 137438953472 | bytes 8388608 | tf_op jit(solution)/shard_map/forward_first/pallas_call | solution.py:798
  136.5 121.7 %forward_second.1 = (bf16[64,2048]{1,0:T(8,128)(2,1)}, bf16[8,2,64,2048]{3,2,1,0:T(8,128)(2,1)}, bf16[8,2,64,2048]{3,2,1,0:T(8,128)(2,1)}, f32[64,2048]{1,0:T(8,...) custom-call(s32[8]{0:T(128)} %select_reduce_fusion.refs_0_, ...), custom_call_target="tpu_custom_call" | custom-call | flops 137438953472 | bytes 8388608 | tf_op jit(solution)/shard_map/forward_second/pallas_call | solution.py:798
  258.2 123.0 %backward_second.1 = (bf16[8,2,64,352]{3,2,1,0:T(8,128)(2,1)}, bf16[8,2,64,352]{3,2,1,0:T(8,128)(2,1)}, bf16[8,2,64,2048]{3,2,1,0:T(8,128)(2,1)}, bf16[64,2048]{...) custom-call(s32[8]{0:T(128)} %select_reduce_fusion.refs_0_, ...), custom_call_target="tpu_custom_call" | custom-call | flops 137438953472 | bytes 8388608 | tf_op jit(solution)/shard_map/backward_second/pallas_call | solution.py:798
  381.2 142.9 %backward_first.1 = (bf16[64,2048]{1,0:T(8,128)(2,1)}, bf16[64,2048]{1,0:T(8,128)(2,1)}, f32[2,128]{1,0:T(2,128)}, bf16[352,2048]{1,0:T(8,128)(2,1)}, bf16[352,2...) custom-call(s32[8]{0:T(128)} %select_reduce_fusion.refs_0_, ...), custom_call_target="tpu_custom_call" | custom-call | flops 137438953472 | bytes 8388608 | tf_op jit(solution)/shard_map/backward_first/pallas_call | solution.py:798
  524.1 0.0 copy-start
  524.1 9.1 %join_all.1 = (f32[352,2048]{1,0:T(8,128)}, f32[352,2048]{1,0:T(8,128)}, f32[352,2048]{1,0:T(8,128)}, f32[128,2048]{1,0:T(8,128)}, f32[128,2048]{1,0:T(8,128)}, ...) custom-call(bf16[352,2048]{1,0:T(8,128)(2,1)} %get-tuple-element.120, ...), custom_call_target="tpu_custom_call" | custom-call | flops 4294967296 | bytes 16777216 | tf_op jit(solution)/shard_map/join_all/pallas_call | solution.py:1550
  533.2 0.0 copy-done
  533.2 0.5 fusion
  (7 shorter events, 0.0 us)
Async XLA Ops:
  3.1 1.6 copy-start.1
  524.1 9.1 %copy-start = (f32[2,128]{1,0:T(2,128)S(1)}, f32[2,128]{1,0:T(2,128)}, u32[]{:S(2)}) copy-start(f32[2,128]{1,0:T(2,128)} %get-tuple-element.151) | copy-start | bytes 3076

commit v5 on v4

--- a/solution.py
+++ b/solution.py
@@ -520,21 +520,25 @@
             self.links.got(7 * SPLIT + slot, self.block(slot, 1 - self.site.core))
             self.use(self.site.chip(*self.along[slot]))
 
+    def ways(self, part):
+        ways = (
+            (self.up + part, 1, self.site.up, self.y_below + part),
+            (self.down + part, 2, self.site.down, self.y_above + part),
+        )
+        return ways if part % 2 == 0 else ways[::-1]
+
     def own(self, part):
         where = self.piece(0, part)
-        self.go(self.up + part, where, self.site.up)
-        self.go(self.down + part, where, self.site.down)
+        for index, _, device, _ in self.ways(part):
+            self.go(index, where, device)
         self.go(self.over + part, where, self.site.across)
 
     def relays(self, part):
-        came = self.links.got(self.up + part, self.piece(1, part))
-        if part % 2 == 0:
-            self.go(self.relay + part, came, self.site.up)
-        self.go(self.y_below + part, came, self.site.across)
-        came = self.links.got(self.down + part, self.piece(2, part))
-        if part % 2 == 1:
-            self.go(self.relay + part, came, self.site.down)
-        self.go(self.y_above + part, came, self.site.across)
+        for turn, (index, slot, device, over) in enumerate(self.ways(part)):
+            came = self.links.got(index, self.piece(slot, part))
+            if turn == 0:
+                self.go(self.relay + part, came, device)
+            self.go(over, came, self.site.across)
 
     def far(self, part):
         came = self.links.got(self.relay + part, self.piece(4, part))
@@ -631,7 +635,8 @@
 
     def up_down(self, part):
         where = self.where(part)
-        for step, base, device in ((5, self.up, self.site.up), (6, self.down, self.site.down)):
+        ways = ((5, self.up, self.site.up), (6, self.down, self.site.down))
+        for step, base, device in ways if part % 2 else ways[::-1]:
             from_y = self.over + (step - 4) * SPLIT + part
             value = self.mine[step, where] + self.came(from_y, self.land.at[step - 4, where])
             if part % 2 == step - 5:
@@ -941,6 +946,9 @@
         n.spread_v[pl.ds(place, 1)] = top + jnp.log(total)
     for block in range(CHIPS):
         put(n.mixed_v, block, n.attended_v[n.order[block]])
+
+
+def keep_attention(n):
     n.copies.start(n.turned_v, n.turned)
     n.copies.start(n.attended_v, n.attended)
     n.copies.start(n.spread_v, n.spread)
@@ -1104,6 +1112,7 @@
     cross.wait(at_out)
     out_copy = copies.pick(n.w_out, n.x_out, n.w_o, 0)
     attend(n)
+    keep_attention(n)
     top.share(0)
     copies.wait(out_copy)
 
@@ -1154,7 +1163,7 @@
     top.links.close()
 
 
-def forward_second(n):
+def second_layer(n):
     site, copies = n.site, n.copies
     first = [
         copies.start(n.act_prev, n.act_prev_v),
@@ -1173,6 +1182,11 @@
         copies.pick(n.w_down, n.x_down, n.w_d, 1),
         copies.start(n.top_all, n.top_held),
     ]
+    back_copies = [copies.pick(n.cotangent.at[0], n.cotangent.at[1], n.top_v, 0)]
+    next_copies = [
+        copies.start(n.gate_slope, n.gate_slope_v),
+        copies.start(n.up_slope, n.up_slope_v),
+    ]
     greet(site)
     copies.wait(*first, *rows_copies)
 
@@ -1190,9 +1204,10 @@
     def settle(count):
         copies.wait(*qkv_copies)
 
-    spread = spread_of(n, n.held, n.spread_send, n.spread_recv, use_qkv, n.rows_one)
+    spread = spread_of(n, n.held, n.spread_send, n.spread_recv, use_qkv)
     fold_spread(fold_of(n, part_of), spread, local, settle)
     copies.start(n.result_v, n.result)
+    n.cross.send(n.result_v, n.came_result_first, 0)
     attend(n)
     copies.wait(*later)
 
@@ -1211,13 +1226,15 @@
         put(n.d_up_v, chip, d_act * up_slope)
 
     spread = spread_of(
-        n, n.held_two, n.spread_two_send, n.spread_two_recv, use_gate, n.rows_two
+        n, n.held_two, n.spread_two_send, n.spread_two_recv, use_gate
     )
     fold_spread(fold_of(n, part_of_two), spread, local_two, no_idle)
-    for source, target in (
-        (n.hidden_v, n.hidden), (n.act, n.act_all), (n.d_gate_v, n.d_gate), (n.d_up_v, n.d_up)
-    ):
-        copies.start(source, target)
+    copies.start(n.hidden_v, n.hidden)
+    copies.start(n.act, n.act_all)
+    copies.wait(*back_copies)
+    backward(
+        1, n, [], [], n.held_two, n.normed, n.held, None, next_copies, n.w_d_prev, n.result_v
+    )
 
 
 def products(n, left, right, store, tile=512):
@@ -1231,12 +1248,12 @@
         yield
 
 
-def ffn_products(n, loads, made):
+def ffn_products(n, loads, made, normed_two):
     n.copies.wait(*loads)
     for left, right, out in (
         (n.act, n.top_held, n.g_down_v),
-        (n.d_gate_v, n.normed, n.g_gate_v),
-        (n.d_up_v, n.normed, n.g_up_v),
+        (n.d_gate_v, normed_two, n.g_gate_v),
+        (n.d_up_v, normed_two, n.g_up_v),
     ):
 
         def store(where, value):
@@ -1246,7 +1263,7 @@
         made(out)
 
 
-def in_products(n, loads, made):
+def in_products(n, loads, made, normed_one, branch):
     site = n.site
     n.copies.wait(*loads)
 
@@ -1260,13 +1277,13 @@
             *n.kv_mine.shape[:3], value.shape[1]
         )
 
-    yield from products(n, n.d_qkv, n.normed, store_in)
+    yield from products(n, n.d_qkv, normed_one, store_in)
     made(n.g_query_v)
     peers = (site.sibling, site.across, site.corner)
     links = Links(n.kv_send, n.kv_recv, site)
     for index, device in enumerate(peers):
         links.go(index, n.kv_mine.at[:, device[2]], n.kv_came.at[index], device)
-    yield from products(n, n.mixed_v, n.held, store_out)
+    yield from products(n, n.mixed_v, branch, store_out)
     made(n.g_out_v)
     total = n.kv_mine[:, site.member].astype(FULL)
     for index in range(len(peers)):
@@ -1312,59 +1329,52 @@
     n.copies.start(n.gain_sums_v, n.gain_sums)
 
 
-def backward(layer, n):
+def first_layer_back(n):
     site, copies, cross = n.site, n.copies, n.cross
     first = [
         copies.start(n.d_gate, n.d_gate_v),
         copies.start(n.d_up, n.d_up_v),
-        copies.pick(n.w_gate, n.x_gate, n.w_g, layer),
-        copies.pick(n.w_up, n.x_up, n.w_u, layer),
+        copies.pick(n.w_gate, n.x_gate, n.w_g, 0),
+        copies.pick(n.w_up, n.x_up, n.w_u, 0),
     ]
+    loads = [copies.start(n.act_all, n.act), copies.start(n.top_all, n.top_held)]
     rows_copies = [
         copies.start(n.hidden, n.hidden_v),
-        copies.pick(n.cotangent.at[0], n.cotangent.at[1], n.top_v, 0)
-        if layer == 1
-        else copies.start(n.top_rows, n.top_v),
+        copies.start(n.top_rows, n.top_v),
         copies.start(n.gains, n.gains_v),
-        copies.pick(n.w_out, n.x_out, n.w_o, layer),
+        copies.pick(n.w_out, n.x_out, n.w_o, 0),
     ]
-    loads = [
-        copies.start(n.act_all, n.act),
-        copies.start(n.top_all, n.top_held),
-        copies.start(n.rows_two, n.normed),
-    ]
+    loads.append(copies.start(n.rows_two, n.normed))
     attn_copies = [
         copies.start(n.turns, n.turns_v),
         copies.start(n.turned, n.turned_v),
         copies.start(n.attended, n.attended_v),
         copies.start(n.spread, n.spread_v),
         copies.start(n.mixed, n.mixed_v),
-        copies.pick(n.w_query, n.x_query, n.w_in.at[pl.ds(0, 2 * HEAD_DIM)], layer),
-        copies.start(n.kv_rows.at[layer], n.w_in.at[pl.ds(2 * HEAD_DIM, 2 * HEAD_DIM)]),
-        copies.start(n.x_rows, n.x_v)
-        if layer == 1
-        else copies.pick(n.inputs.at[0], n.inputs.at[1], n.x_v, 0),
+        copies.pick(n.w_query, n.x_query, n.w_in.at[pl.ds(0, 2 * HEAD_DIM)], 0),
+        copies.start(n.kv_rows.at[0], n.w_in.at[pl.ds(2 * HEAD_DIM, 2 * HEAD_DIM)]),
+        copies.pick(n.inputs.at[0], n.inputs.at[1], n.x_v, 0),
     ]
-    if layer == 1:
-        next_copies = [
-            copies.pick(n.w_down, n.x_down, n.w_d, 0),
-            copies.start(n.gate_slope, n.gate_slope_v),
-            copies.start(n.up_slope, n.up_slope_v),
-        ]
-    else:
-        next_copies = [
-            copies.pick(n.w_down, n.x_down, n.w_d, 1),
-            copies.start(n.act_last, n.act_last_v),
-            copies.start(n.hidden_last, n.hidden_last_v),
-            copies.start(n.gain_later, n.gain_later_v),
-        ]
+    next_copies = [
+        copies.pick(n.w_down, n.x_down, n.w_d, 1),
+        copies.start(n.act_last, n.act_last_v),
+        copies.start(n.hidden_last, n.hidden_last_v),
+        copies.start(n.gain_later, n.gain_later_v),
+    ]
     greet(site)
-    if layer == 1:
-        cross.send(n.x_rows, n.came_result_first, 0)
-    else:
-        cross.send(n.own_up_later, n.came_up_later, 1)
-        cross.send(n.top_rows, n.came_input_later, 1)
+    cross.send(n.own_up_later, n.came_up_later, 1)
+    cross.send(n.top_rows, n.came_input_later, 1)
     copies.wait(*first, *rows_copies)
+    backward(
+        0, n, loads, attn_copies, n.normed, n.held, n.normed, n.rows_one, next_copies, n.w_d, n.x_v
+    )
+
+
+def backward(
+    layer, n, loads, attn_copies, normed_two, branch, normed_one, rows_one, next_copies, w_next,
+    x_rows,
+):
+    site, copies, cross = n.site, n.copies, n.cross
 
     def made(out):
         target, came = {
@@ -1407,14 +1417,14 @@
     def use_d_mixed(chip, rows):
         n.d_mixed[chip] = times_trans(rows, n.w_o[...]).astype(LOW)
 
-    working = ffn_products(n, loads, made)
+    working = ffn_products(n, loads, made, normed_two)
     if layer == 0:
         step_on(working)(5)
-    spread = spread_of(n, n.held, n.spread_send, n.spread_recv, use_d_mixed)
+    spread = spread_of(n, branch, n.back_send, n.back_recv, use_d_mixed)
     fold_spread(fold_of(n, part_of), spread, local, step_on(working))
     for _ in working:
         pass
-    normed_copy = copies.start(n.rows_one, n.normed)
+    one_copies = [] if rows_one is None else [copies.start(rows_one, normed_one)]
     copies.wait(*attn_copies)
     attend_back(n)
     copies.wait(*next_copies)
@@ -1424,23 +1434,23 @@
 
     def local_two(total, where):
         gain_grad, d_input = norm_back_rows(
-            n.x_v[where].astype(FULL), n.gains_v[2 * layer : 2 * layer + 1], total
+            x_rows[where].astype(FULL), n.gains_v[2 * layer : 2 * layer + 1], total
         )
         d_input = (d_input + n.d_hidden[where]).astype(LOW)
         add_gain(0, gain_grad, where)
         n.d_input_v[where] = d_input
         return d_input
 
-    working = in_products(n, [normed_copy], made)
+    working = in_products(n, one_copies, made, normed_one, branch)
     if layer == 1:
 
         def use_d_act(chip, rows):
-            d_act = times_trans(rows, n.w_d[...])
+            d_act = times_trans(rows, w_next[...])
             for out, slope in ((n.d_gate_v, n.gate_slope_v), (n.d_up_v, n.up_slope_v)):
                 put(out, chip, d_act * slope[chip].astype(FULL).reshape(d_act.shape))
 
         spread = spread_of(
-            n, n.held_two, n.spread_two_send, n.spread_two_recv, use_d_act, n.top_next
+            n, n.held_two, n.back_two_send, n.back_two_recv, use_d_act, n.top_next
         )
         fold_spread(fold_of(n, part_of_two), spread, local_two, step_on(working))
         for _ in working:
@@ -1458,7 +1468,7 @@
     cross.send(n.d_input_v, n.came_input, 0)
 
     def part_of_last(chip):
-        return plain_dot(rows_of(n.act_last_v, chip, site), n.w_d[...])
+        return plain_dot(rows_of(n.act_last_v, chip, site), w_next[...])
 
     def local_last(total, where):
         n.result_v[where] = (n.hidden_last_v[where] + total).astype(LOW)
@@ -1637,11 +1647,11 @@
         mixed_v=vmem(*saved["mixed"]),
         turns_v=vmem(turns.shape, FULL),
     )
-    attend_v = dict(
-        **saved_v,
+    attend_v_only = dict(
         qkv=vmem((CHIPS, PLACE, in_width), FULL),
         values_t=vmem((HEAD_DIM, total_len), LOW),
     )
+    attend_v = dict(**saved_v, **attend_v_only)
     gates_v = dict(w_g=vmem(*wide), w_u=vmem(*wide))
 
     first = launch(
@@ -1711,47 +1721,6 @@
         kv_rows=first.kv_rows,
         turns=turns,
     )
-    second = launch(
-        "forward_second",
-        1,
-        forward_second,
-        scalars,
-        dict(
-            act_prev=first.act_all, hidden_prev=first.hidden, top_all=first.top_all, **crossed
-        ),
-        dict(
-            result=row_low,
-            rows_one=all_rows,
-            rows_two=all_rows,
-            hidden=row_full,
-            act_all=narrow,
-            d_gate=narrow,
-            d_up=narrow,
-            **saved,
-        ),
-        dict(
-            act_prev_v=vmem(*narrow),
-            hidden_prev_v=vmem(*row_full),
-            gains_v=vmem(*gain_row),
-            w_d_prev=vmem(*wide),
-            w_in=vmem((in_width, model_width), LOW),
-            w_o=vmem(*quarter),
-            w_d=vmem(*wide),
-            top_held=vmem(*all_rows),
-            held=vmem(*all_rows),
-            held_two=vmem(*all_rows),
-            result_v=vmem(*row_low),
-            hidden_v=vmem(*row_full),
-            act=vmem(*narrow),
-            d_gate_v=vmem(*narrow),
-            d_up_v=vmem(*narrow),
-            **gates_v,
-            **attend_v,
-            **fold_buffers(rows),
-            **spread_sems("spread_send", "spread_recv", "spread_two_send", "spread_two_recv"),
-        ),
-    )
-
     kv_pair = ((2, *kv_shape[1:]), LOW)
     own_sums = dict(
         own_down=wide, own_gate=wide, own_up=wide, own_out=quarter, own_query=quarter,
@@ -1812,19 +1781,40 @@
             **crossed,
         )
 
+    merged_v = dict(
+        back_v,
+        act_prev_v=vmem(*narrow),
+        hidden_prev_v=vmem(*row_full),
+        w_d_prev=vmem(*wide),
+        held_two=vmem(*all_rows),
+        result_v=vmem(*row_low),
+        gate_slope_v=vmem(*narrow),
+        up_slope_v=vmem(*narrow),
+        **attend_v_only,
+        **spread_sems(
+            "spread_send", "spread_recv", "spread_two_send", "spread_two_recv", "back_send",
+            "back_recv", "back_two_send", "back_two_recv",
+        ),
+    )
+    del merged_v["x_v"]
     third = launch(
-        "backward_second",
-        2,
-        functools.partial(backward, 1),
+        "second_layer",
+        1,
+        second_layer,
         scalars,
         dict(
-            **back_in(second, second.d_gate, second.d_up, first.top_all),
-            x_rows=second.result,
+            act_prev=first.act_all,
+            hidden_prev=first.hidden,
+            top_all=first.top_all,
             cotangent=cotangent,
             gate_slope=first.gate_slope,
             up_slope=first.up_slope,
+            **crossed,
         ),
         dict(
+            result=row_low,
+            hidden=row_full,
+            act_all=narrow,
             d_gate_next=narrow,
             d_up_next=narrow,
             top_next=all_rows,
@@ -1834,18 +1824,12 @@
             **own_sums,
             **came_sums,
         ),
-        dict(
-            gate_slope_v=vmem(*narrow),
-            up_slope_v=vmem(*narrow),
-            held_two=vmem(*all_rows),
-            **back_v,
-            **spread_sems("spread_send", "spread_recv", "spread_two_send", "spread_two_recv"),
-        ),
+        merged_v,
     )
     fourth = launch(
-        "backward_first",
-        3,
-        functools.partial(backward, 0),
+        "first_layer_back",
+        2,
+        first_layer_back,
         scalars,
         dict(
             **back_in(first, third.d_gate_next, third.d_up_next, third.top_next),
@@ -1853,8 +1837,8 @@
             top_rows=third.d_input,
             own_up_later=third.own_up,
             gain_later=third.gain_out,
-            act_last=second.act_all,
-            hidden_last=second.hidden,
+            act_last=third.act_all,
+            hidden_last=third.hidden,
         ),
         dict(
             d_input=row_low,
@@ -1887,7 +1871,7 @@
             gain_send=pltpu.SemaphoreType.DMA((7,)),
             gain_recv=pltpu.SemaphoreType.DMA((7,)),
             **back_v,
-            **spread_sems("spread_send", "spread_recv"),
+            **spread_sems("back_send", "back_recv"),
         ),
     )
 
@@ -1900,7 +1884,7 @@
         sums("own", third),
         sums("came", fourth),
         sums("came", third),
-        (second.result, fourth.result, third.came_result_first, fourth.came_result),
+        (third.result, fourth.result, third.came_result_first, fourth.came_result),
         (fourth.d_input, third.d_input, fourth.came_input, fourth.came_input_later),
     )
     return (

time: 543 us -> 534 us (0.983)
  Pallas kernels: 528 us -> 520 us
    pallas_call x4 -> x3, Pallas kernels: 519 us -> 511 us  [launch(): pl.pallas_call(functools.partial(kernel_of, body, names), out_shape=[jax....]
where the time goes in v5:
time: 534 us; the launch traced here: 526 us
  Pallas kernels  520 us (97%)
    pallas_call x3, Pallas kernels, launch(): pl.pallas_call(functools.partial(kernel_of, body, names), out_shape=[jax....  511 us

profile of v5, /device:TPU:0, one launch (start us, length us, event | category | flops | bytes accessed | tf_op | source)
XLA Modules:
  0.0 525.5 jit_solution(4950141018847071732)
XLA Ops:
  0.7 0.1 pad.6.clone
  0.8 0.1 mul.45
  0.9 1.3 maximum_convert_fusion.refs_4_
  2.2 0.8 broadcast_select_fusion
  3.0 0.1 copy.25
  3.1 0.0 copy-start.1
  3.1 0.6 select_reduce_fusion.refs_0_
  3.7 0.3 multiply_cosine_fusion
  4.0 0.7 pad_maximum_fusion.refs_7_.refs_20_.refs_25_
  4.7 0.0 copy-done.1
  4.7 131.8 %forward_first.1 = (bf16[128,2048]{1,0:T(8,128)(2,1)}, bf16[128,2048]{1,0:T(8,128)(2,1)}, bf16[352,2048]{1,0:T(8,128)(2,1)}, bf16[352,2048]{1,0:T(8,128)(2,1)}, ...) custom-call(s32[8]{0:T(128)} %select_reduce_fusion.refs_0_, ...), custom_call_target="tpu_custom_call" | custom-call | flops 137438953472 | bytes 8388608 | tf_op jit(solution)/shard_map/forward_first/pallas_call | solution.py:803
  136.5 235.8 %second_layer.1 = (bf16[64,2048]{1,0:T(8,128)(2,1)}, f32[64,2048]{1,0:T(8,128)}, bf16[8,2,64,352]{3,2,1,0:T(8,128)(2,1)}, bf16[8,2,64,352]{3,2,1,0:T(8,128)(2,1)...) custom-call(s32[8]{0:T(128)} %select_reduce_fusion.refs_0_, ...), custom_call_target="tpu_custom_call" | custom-call | flops 137438953472 | bytes 8388608 | tf_op jit(solution)/shard_map/second_layer/pallas_call | solution.py:803
  372.3 142.9 %first_layer_back.1 = (bf16[64,2048]{1,0:T(8,128)(2,1)}, bf16[64,2048]{1,0:T(8,128)(2,1)}, f32[2,128]{1,0:T(2,128)}, bf16[352,2048]{1,0:T(8,128)(2,1)}, bf16[352...) custom-call(s32[8]{0:T(128)} %select_reduce_fusion.refs_0_, ...), custom_call_target="tpu_custom_call" | custom-call | flops 137438953472 | bytes 8388608 | tf_op jit(solution)/shard_map/first_layer_back/pallas_call | solution.py:803
  515.2 0.0 copy-start
  515.3 9.3 %join_all.1 = (f32[352,2048]{1,0:T(8,128)}, f32[352,2048]{1,0:T(8,128)}, f32[352,2048]{1,0:T(8,128)}, f32[128,2048]{1,0:T(8,128)}, f32[128,2048]{1,0:T(8,128)}, ...) custom-call(bf16[352,2048]{1,0:T(8,128)(2,1)} %get-tuple-element.103, ...), custom_call_target="tpu_custom_call" | custom-call | flops 4294967296 | bytes 16777216 | tf_op jit(solution)/shard_map/join_all/pallas_call | solution.py:1560
  524.5 0.0 copy-done
  524.5 0.5 fusion
  (7 shorter events, 0.0 us)
Async XLA Ops:
  3.1 1.6 copy-start.1
  515.2 9.3 %copy-start = (f32[2,128]{1,0:T(2,128)S(1)}, f32[2,128]{1,0:T(2,128)}, u32[]{:S(2)}) copy-start(f32[2,128]{1,0:T(2,128)} %get-tuple-element.135) | copy-start | bytes 3076

commit v6 on v5

--- a/solution.py
+++ b/solution.py
@@ -487,8 +487,8 @@
 SPREAD_SEMS = 7 * SPLIT + CHIPS
 FOLD_SEMS = 7 * SPLIT + CHIPS
 SMALL_SEMS = 11
-COPY_SEMS = 48
-CROSS_SEMS = 32
+COPY_SEMS = 64
+CROSS_SEMS = 40
 PIECE = 128
 
 
@@ -747,6 +747,7 @@
                     copy.wait_send()
 
             self.where(layer, False, leave)
+        self.begun = []
 
 
 class Copies:
@@ -1206,8 +1207,8 @@
 
     spread = spread_of(n, n.held, n.spread_send, n.spread_recv, use_qkv)
     fold_spread(fold_of(n, part_of), spread, local, settle)
-    copies.start(n.result_v, n.result)
-    n.cross.send(n.result_v, n.came_result_first, 0)
+    copies.start(n.result_v, n.result_a)
+    n.cross.send(n.result_v, n.came_result_a, 0)
     attend(n)
     copies.wait(*later)
 
@@ -1229,11 +1230,67 @@
         n, n.held_two, n.spread_two_send, n.spread_two_recv, use_gate
     )
     fold_spread(fold_of(n, part_of_two), spread, local_two, no_idle)
-    copies.start(n.hidden_v, n.hidden)
-    copies.start(n.act, n.act_all)
     copies.wait(*back_copies)
+    cross = n.cross
+    first_copies = []
+
+    def preload():
+        first_copies.append(copies.pick(n.w_gate, n.x_gate, n.w_g, 0))
+        first_copies.append(copies.pick(n.w_up, n.x_up, n.w_u, 0))
+        first_copies.append(copies.pick(n.w_out, n.x_out, n.w_o, 0))
+        first_copies.append(copies.start(n.rows_two, n.top_held))
+
     backward(
-        1, n, [], [], n.held_two, n.normed, n.held, None, next_copies, n.w_d_prev, n.result_v
+        n,
+        types.SimpleNamespace(
+            layer=1, attn_copies=[], one_copies=[], next_copies=next_copies, act=n.act,
+            top_all=n.top_held, normed_two=n.held_two, normed_one=n.held, branch=n.normed,
+            hidden=n.hidden_v, top=n.top_v, x_rows=n.result_v, d_input=n.d_input_v,
+            w_next=n.w_d_prev, after_first=preload, send=n.back_send, recv=n.back_recv,
+            sums=[
+                (n.g_down_v, n.own_down_b, n.came_down_b),
+                (n.g_gate_v, n.own_gate_b, n.came_gate_b),
+                (n.g_up_v, n.own_up_b, None),
+                (n.g_out_v, n.own_out_b, n.came_out_b),
+                (n.g_query_v, n.own_query_b, n.came_query_b),
+                (n.g_kv_v, n.own_kv_b, n.came_kv_b),
+            ],
+        ),
+    )
+    copies.start(n.d_input_v, n.d_input_b)
+    n.gain_later_v[...] = n.gain_grads[...]
+    copies.wait(*first_copies)
+    copies.close()
+    cross.close()
+    attn_copies = [
+        copies.start(n.turned, n.turned_v),
+        copies.start(n.attended, n.attended_v),
+        copies.start(n.spread, n.spread_v),
+        copies.start(n.mixed, n.mixed_v),
+        copies.pick(n.w_query, n.x_query, n.w_in.at[pl.ds(0, 2 * HEAD_DIM)], 0),
+        copies.start(n.kv_rows.at[0], n.w_in.at[pl.ds(2 * HEAD_DIM, 2 * HEAD_DIM)]),
+        copies.pick(n.inputs.at[0], n.inputs.at[1], n.x_v, 0),
+    ]
+    one_copies = [copies.start(n.rows_one, n.held)]
+    cross.send(n.own_up_b, n.came_up_b, 1)
+    cross.send(n.d_input_v, n.came_input_b, 1)
+    backward(
+        n,
+        types.SimpleNamespace(
+            layer=0, attn_copies=attn_copies, one_copies=one_copies, next_copies=[],
+            act=n.act_prev_v, top_all=n.held_two, normed_two=n.top_held, normed_one=n.held,
+            branch=n.normed, hidden=n.hidden_prev_v, top=n.d_input_v, x_rows=n.x_v,
+            d_input=n.d_input_two, w_next=n.w_d, after_first=lambda: None, send=n.last_back_send,
+            recv=n.last_back_recv,
+            sums=[
+                (n.g_down_v, n.own_down_a, n.came_down_a),
+                (n.g_gate_v, n.own_gate_a, n.came_gate_a),
+                (n.g_up_v, n.own_up_a, n.came_up_a),
+                (n.g_out_v, n.own_out_a, n.came_out_a),
+                (n.g_query_v, n.own_query_a, n.came_query_a),
+                (n.g_kv_v, n.own_kv_a, n.came_kv_a),
+            ],
+        ),
     )
 
 
@@ -1248,12 +1305,11 @@
         yield
 
 
-def ffn_products(n, loads, made, normed_two):
-    n.copies.wait(*loads)
+def ffn_products(n, k, made):
     for left, right, out in (
-        (n.act, n.top_held, n.g_down_v),
-        (n.d_gate_v, normed_two, n.g_gate_v),
-        (n.d_up_v, normed_two, n.g_up_v),
+        (k.act, k.top_all, n.g_down_v),
+        (n.d_gate_v, k.normed_two, n.g_gate_v),
+        (n.d_up_v, k.normed_two, n.g_up_v),
     ):
 
         def store(where, value):
@@ -1329,62 +1385,14 @@
     n.copies.start(n.gain_sums_v, n.gain_sums)
 
 
-def first_layer_back(n):
+def backward(n, k):
     site, copies, cross = n.site, n.copies, n.cross
-    first = [
-        copies.start(n.d_gate, n.d_gate_v),
-        copies.start(n.d_up, n.d_up_v),
-        copies.pick(n.w_gate, n.x_gate, n.w_g, 0),
-        copies.pick(n.w_up, n.x_up, n.w_u, 0),
-    ]
-    loads = [copies.start(n.act_all, n.act), copies.start(n.top_all, n.top_held)]
-    rows_copies = [
-        copies.start(n.hidden, n.hidden_v),
-        copies.start(n.top_rows, n.top_v),
-        copies.start(n.gains, n.gains_v),
-        copies.pick(n.w_out, n.x_out, n.w_o, 0),
-    ]
-    loads.append(copies.start(n.rows_two, n.normed))
-    attn_copies = [
-        copies.start(n.turns, n.turns_v),
-        copies.start(n.turned, n.turned_v),
-        copies.start(n.attended, n.attended_v),
-        copies.start(n.spread, n.spread_v),
-        copies.start(n.mixed, n.mixed_v),
-        copies.pick(n.w_query, n.x_query, n.w_in.at[pl.ds(0, 2 * HEAD_DIM)], 0),
-        copies.start(n.kv_rows.at[0], n.w_in.at[pl.ds(2 * HEAD_DIM, 2 * HEAD_DIM)]),
-        copies.pick(n.inputs.at[0], n.inputs.at[1], n.x_v, 0),
-    ]
-    next_copies = [
-        copies.pick(n.w_down, n.x_down, n.w_d, 1),
-        copies.start(n.act_last, n.act_last_v),
-        copies.start(n.hidden_last, n.hidden_last_v),
-        copies.start(n.gain_later, n.gain_later_v),
-    ]
-    greet(site)
-    cross.send(n.own_up_later, n.came_up_later, 1)
-    cross.send(n.top_rows, n.came_input_later, 1)
-    copies.wait(*first, *rows_copies)
-    backward(
-        0, n, loads, attn_copies, n.normed, n.held, n.normed, n.rows_one, next_copies, n.w_d, n.x_v
-    )
-
-
-def backward(
-    layer, n, loads, attn_copies, normed_two, branch, normed_one, rows_one, next_copies, w_next,
-    x_rows,
-):
-    site, copies, cross = n.site, n.copies, n.cross
+    layer = k.layer
 
     def made(out):
-        target, came = {
-            id(n.g_down_v): (n.own_down, n.came_down),
-            id(n.g_gate_v): (n.own_gate, n.came_gate),
-            id(n.g_up_v): (n.own_up, None if layer == 1 else n.came_up),
-            id(n.g_out_v): (n.own_out, n.came_out),
-            id(n.g_query_v): (n.own_query, n.came_query),
-            id(n.g_kv_v): (n.own_kv, n.came_kv),
-        }[id(out)]
+        for value, target, came in k.sums:
+            if value is out:
+                break
         copies.start(out, target)
         if came is not None:
             cross.send(out, came, layer)
@@ -1407,9 +1415,9 @@
 
     def local(total, where):
         gain_grad, d_hidden = norm_back_rows(
-            n.hidden_v[where], n.gains_v[2 * layer + 1 : 2 * layer + 2], total
-        )
-        d_hidden = d_hidden + n.top_v[where].astype(FULL)
+            k.hidden[where], n.gains_v[2 * layer + 1 : 2 * layer + 2], total
+        )
+        d_hidden = d_hidden + k.top[where].astype(FULL)
         add_gain(1, gain_grad, where)
         n.d_hidden[where] = d_hidden
         return d_hidden.astype(LOW)
@@ -1417,63 +1425,56 @@
     def use_d_mixed(chip, rows):
         n.d_mixed[chip] = times_trans(rows, n.w_o[...]).astype(LOW)
 
-    working = ffn_products(n, loads, made, normed_two)
+    working = ffn_products(n, k, made)
     if layer == 0:
         step_on(working)(5)
-    spread = spread_of(n, branch, n.back_send, n.back_recv, use_d_mixed)
+    spread = spread_of(n, k.branch, k.send, k.recv, use_d_mixed)
     fold_spread(fold_of(n, part_of), spread, local, step_on(working))
     for _ in working:
         pass
-    one_copies = [] if rows_one is None else [copies.start(rows_one, normed_one)]
-    copies.wait(*attn_copies)
+    k.after_first()
+    copies.wait(*k.attn_copies)
     attend_back(n)
-    copies.wait(*next_copies)
+    copies.wait(*k.next_copies)
 
     def part_of_two(chip):
         return plain_dot(rows_of(n.d_qkv, chip, site), n.w_in[...])
 
     def local_two(total, where):
         gain_grad, d_input = norm_back_rows(
-            x_rows[where].astype(FULL), n.gains_v[2 * layer : 2 * layer + 1], total
+            k.x_rows[where].astype(FULL), n.gains_v[2 * layer : 2 * layer + 1], total
         )
         d_input = (d_input + n.d_hidden[where]).astype(LOW)
         add_gain(0, gain_grad, where)
-        n.d_input_v[where] = d_input
+        k.d_input[where] = d_input
         return d_input
 
-    working = in_products(n, one_copies, made, normed_one, branch)
+    working = in_products(n, k.one_copies, made, k.normed_one, k.branch)
     if layer == 1:
 
         def use_d_act(chip, rows):
-            d_act = times_trans(rows, w_next[...])
+            d_act = times_trans(rows, k.w_next[...])
             for out, slope in ((n.d_gate_v, n.gate_slope_v), (n.d_up_v, n.up_slope_v)):
                 put(out, chip, d_act * slope[chip].astype(FULL).reshape(d_act.shape))
 
-        spread = spread_of(
-            n, n.held_two, n.back_two_send, n.back_two_recv, use_d_act, n.top_next
-        )
+        spread = spread_of(n, n.held_two, n.back_two_send, n.back_two_recv, use_d_act)
         fold_spread(fold_of(n, part_of_two), spread, local_two, step_on(working))
         for _ in working:
             pass
-        for source, target in (
-            (n.d_gate_v, n.d_gate_next), (n.d_up_v, n.d_up_next), (n.d_input_v, n.d_input),
-            (n.gain_grads, n.gain_out),
-        ):
-            copies.start(source, target)
         return
     fold_spread(fold_of(n, part_of_two), None, local_two, step_on(working))
     for _ in working:
         pass
-    copies.start(n.d_input_v, n.d_input)
-    cross.send(n.d_input_v, n.came_input, 0)
+    copies.start(k.d_input, n.d_input_a)
+    cross.send(k.d_input, n.came_input_a, 0)
 
     def part_of_last(chip):
-        return plain_dot(rows_of(n.act_last_v, chip, site), w_next[...])
+        return plain_dot(rows_of(n.act, chip, site), k.w_next[...])
 
     def local_last(total, where):
-        n.result_v[where] = (n.hidden_last_v[where] + total).astype(LOW)
-
-    buffers = (n.mine, n.pass_out, n.pass_in_two, n.stage, n.land_two)
+        n.result_two[where] = (n.hidden_v[where] + total).astype(LOW)
+
+    buffers = (n.mine, n.pass_out, n.held_two.at[:, 0], n.stage, n.held_two.at[:, 1])
     links = Links(n.last_send, n.last_recv, site)
     gains_on = fold_gains(n)
     next(gains_on)
@@ -1483,8 +1484,8 @@
     )
     for _ in gains_on:
         pass
-    copies.start(n.result_v, n.result)
-    cross.send(n.result_v, n.came_result, 1)
+    copies.start(n.result_two, n.result_b)
+    cross.send(n.result_two, n.came_result_b, 1)
 
 
 def join_kernel(count, *refs):
@@ -1722,143 +1723,84 @@
         turns=turns,
     )
     kv_pair = ((2, *kv_shape[1:]), LOW)
-    own_sums = dict(
-        own_down=wide, own_gate=wide, own_up=wide, own_out=quarter, own_query=quarter,
-        own_kv=kv_pair,
-    )
-    came_sums = dict(
-        came_down=wide, came_gate=wide, came_out=quarter, came_query=quarter, came_kv=kv_pair
-    )
-    back_v = dict(
-        d_gate_v=vmem(*narrow),
-        d_up_v=vmem(*narrow),
-        act=vmem(*narrow),
-        hidden_v=vmem(*row_full),
-        top_v=vmem(*row_low),
-        x_v=vmem(*row_low),
-        d_hidden=vmem(*row_full),
-        d_input_v=vmem(*row_low),
-        gains_v=vmem(*gain_row),
-        gain_grads=vmem((2, model_width), FULL),
-        w_o=vmem(*quarter),
-        w_in=vmem((in_width, model_width), LOW),
-        w_d=vmem(*wide),
-        top_held=vmem(*all_rows),
-        normed=vmem(*all_rows),
-        held=vmem(*all_rows),
-        d_mixed=vmem((CHIPS, PLACE, q_width), LOW),
-        d_qkv=vmem((CHIPS, 2, per_device, in_width), LOW),
-        d_turned=vmem((CHIPS, PLACE, in_width), LOW),
-        d_query=vmem((total_len, q_width), FULL),
-        d_key=vmem((total_len, HEAD_DIM), FULL),
-        d_value=vmem((total_len, HEAD_DIM), FULL),
-        keys_t=vmem((HEAD_DIM, total_len), LOW),
-        g_down_v=vmem(*wide),
-        g_gate_v=vmem(*wide),
-        g_up_v=vmem(*wide),
-        g_out_v=vmem(*quarter),
-        g_query_v=vmem(*quarter),
-        g_kv_v=vmem(*kv_pair),
-        kv_mine=vmem((2, n_seq, *kv_shape[1:]), LOW),
-        kv_came=vmem((n_seq - 1, 2, *kv_shape[1:]), LOW),
-        kv_send=pltpu.SemaphoreType.DMA((n_seq - 1,)),
-        kv_recv=pltpu.SemaphoreType.DMA((n_seq - 1,)),
-        **gates_v,
-        **saved_v,
-        **fold_buffers(rows),
-    )
-
-    def back_in(done, d_gate, d_up, top_all):
-        return dict(
-            d_gate=d_gate,
-            d_up=d_up,
-            hidden=done.hidden,
-            act_all=done.act_all,
-            top_all=top_all,
-            rows_one=done.rows_one,
-            rows_two=done.rows_two,
-            **{key: getattr(done, key) for key in saved},
-            **crossed,
-        )
-
-    merged_v = dict(
-        back_v,
-        act_prev_v=vmem(*narrow),
-        hidden_prev_v=vmem(*row_full),
-        w_d_prev=vmem(*wide),
-        held_two=vmem(*all_rows),
-        result_v=vmem(*row_low),
-        gate_slope_v=vmem(*narrow),
-        up_slope_v=vmem(*narrow),
-        **attend_v_only,
-        **spread_sems(
-            "spread_send", "spread_recv", "spread_two_send", "spread_two_recv", "back_send",
-            "back_recv", "back_two_send", "back_two_recv",
-        ),
-    )
-    del merged_v["x_v"]
-    third = launch(
-        "second_layer",
+    sums_out = dict(down=wide, gate=wide, up=wide, out=quarter, query=quarter, kv=kv_pair)
+    layers = dict(a=0, b=1)
+    second = launch(
+        "second_layer_and_back",
         1,
         second_layer,
         scalars,
         dict(
             act_prev=first.act_all,
             hidden_prev=first.hidden,
+            inputs=inputs,
+            cotangent=cotangent,
             top_all=first.top_all,
-            cotangent=cotangent,
+            rows_one=first.rows_one,
+            rows_two=first.rows_two,
             gate_slope=first.gate_slope,
             up_slope=first.up_slope,
+            **{key: getattr(first, key) for key in saved},
             **crossed,
         ),
         dict(
-            result=row_low,
-            hidden=row_full,
-            act_all=narrow,
-            d_gate_next=narrow,
-            d_up_next=narrow,
-            top_next=all_rows,
-            d_input=row_low,
-            gain_out=((2, model_width), FULL),
-            came_result_first=row_low,
-            **own_sums,
-            **came_sums,
-        ),
-        merged_v,
-    )
-    fourth = launch(
-        "first_layer_back",
-        2,
-        first_layer_back,
-        scalars,
-        dict(
-            **back_in(first, third.d_gate_next, third.d_up_next, third.top_next),
-            inputs=inputs,
-            top_rows=third.d_input,
-            own_up_later=third.own_up,
-            gain_later=third.gain_out,
-            act_last=third.act_all,
-            hidden_last=third.hidden,
+            gain_sums=((2, small[1]), FULL),
+            **{
+                f"{of}_{key}_{layer}": value
+                for layer in layers
+                for of in ("own", "came")
+                for key, value in sums_out.items()
+            },
+            **{
+                f"{of}_{layer}": row_low
+                for layer in layers
+                for of in ("result", "d_input", "came_result", "came_input")
+            },
         ),
         dict(
-            d_input=row_low,
-            result=row_low,
-            gain_sums=((2, small[1]), FULL),
-            came_up=wide,
-            came_up_later=wide,
-            came_input=row_low,
-            came_input_later=row_low,
-            came_result=row_low,
-            **own_sums,
-            **came_sums,
-        ),
-        dict(
-            act_last_v=vmem(*narrow),
-            hidden_last_v=vmem(*row_full),
+            act_prev_v=vmem(*narrow),
+            act=vmem(*narrow),
+            d_gate_v=vmem(*narrow),
+            d_up_v=vmem(*narrow),
+            gate_slope_v=vmem(*narrow),
+            up_slope_v=vmem(*narrow),
+            hidden_prev_v=vmem(*row_full),
+            hidden_v=vmem(*row_full),
+            d_hidden=vmem(*row_full),
+            result_v=vmem(*row_low),
+            result_two=vmem(*row_low),
+            top_v=vmem(*row_low),
+            x_v=vmem(*row_low),
+            d_input_v=vmem(*row_low),
+            d_input_two=vmem(*row_low),
+            gains_v=vmem(*gain_row),
+            gain_grads=vmem((2, model_width), FULL),
             gain_later_v=vmem((2, model_width), FULL),
-            result_v=vmem(*row_low),
-            pass_in_two=vmem((CHIPS, *rows), LOW),
-            land_two=vmem((CHIPS - 1, *rows), LOW),
+            w_d_prev=vmem(*wide),
+            w_d=vmem(*wide),
+            w_o=vmem(*quarter),
+            w_in=vmem((in_width, model_width), LOW),
+            top_held=vmem(*all_rows),
+            normed=vmem(*all_rows),
+            held=vmem(*all_rows),
+            held_two=vmem(*all_rows),
+            d_mixed=vmem((CHIPS, PLACE, q_width), LOW),
+            d_qkv=vmem((CHIPS, 2, per_device, in_width), LOW),
+            d_turned=vmem((CHIPS, PLACE, in_width), LOW),
+            d_query=vmem((total_len, q_width), FULL),
+            d_key=vmem((total_len, HEAD_DIM), FULL),
+            d_value=vmem((total_len, HEAD_DIM), FULL),
+            keys_t=vmem((HEAD_DIM, total_len), LOW),
+            g_down_v=vmem(*wide),
+            g_gate_v=vmem(*wide),
+            g_up_v=vmem(*wide),
+            g_out_v=vmem(*quarter),
+            g_query_v=vmem(*quarter),
+            g_kv_v=vmem(*kv_pair),
+            kv_mine=vmem((2, n_seq, *kv_shape[1:]), LOW),
+            kv_came=vmem((n_seq - 1, 2, *kv_shape[1:]), LOW),
+            kv_send=pltpu.SemaphoreType.DMA((n_seq - 1,)),
+            kv_recv=pltpu.SemaphoreType.DMA((n_seq - 1,)),
             last_send=pltpu.SemaphoreType.DMA((FOLD_SEMS,)),
             last_recv=pltpu.SemaphoreType.DMA((FOLD_SEMS,)),
             gain_parts=vmem((n_seq, n_shard, *small), FULL),
@@ -1870,32 +1812,34 @@
             gain_sums_v=vmem((2, small[1]), FULL),
             gain_send=pltpu.SemaphoreType.DMA((7,)),
             gain_recv=pltpu.SemaphoreType.DMA((7,)),
-            **back_v,
-            **spread_sems("back_send", "back_recv"),
+            **gates_v,
+            **attend_v,
+            **fold_buffers(rows),
+            **spread_sems(
+                "spread_send", "spread_recv", "spread_two_send", "spread_two_recv", "back_send",
+                "back_recv", "back_two_send", "back_two_recv", "last_back_send",
+                "last_back_recv",
+            ),
         ),
     )
 
-    def sums(of, done):
-        return [getattr(done, f"{of}_{key}") for key in ("down", "gate", "up", "out", "query", "kv")]
-
-    third.came_up = fourth.came_up_later
+    def sums(of, layer):
+        return [getattr(second, f"{of}_{key}_{layer}") for key in sums_out]
+
     g_down, g_gate, g_up, g_out, g_query, g_key, g_value, outputs, input_grads = join_all(
-        sums("own", fourth),
-        sums("own", third),
-        sums("came", fourth),
-        sums("came", third),
-        (third.result, fourth.result, third.came_result_first, fourth.came_result),
-        (fourth.d_input, third.d_input, fourth.came_input, fourth.came_input_later),
+        *(sums(of, layer) for of in ("own", "came") for layer in layers),
+        (second.result_a, second.result_b, second.came_result_a, second.came_result_b),
+        (second.d_input_a, second.d_input_b, second.came_input_a, second.came_input_b),
     )
     return (
         outputs[None],
         input_grads[None],
-        fourth.gain_sums[:1],
+        second.gain_sums[:1],
         g_query[None],
         g_key,
         g_value,
         g_out[None],
-        fourth.gain_sums[1:],
+        second.gain_sums[1:],
         g_gate[None],
         g_up[None],
         g_down[None],

time: 534 us -> 527 us (0.987)
  Pallas kernels: 520 us -> 512 us
    pallas_call x3 -> x2, Pallas kernels: 511 us -> 503 us  [launch(): pl.pallas_call(functools.partial(kernel_of, body, names), out_shape=[jax....]
where the time goes in v6:
time: 527 us; the launch traced here: 518 us
  Pallas kernels  512 us (97%)
    pallas_call x2, Pallas kernels, launch(): pl.pallas_call(functools.partial(kernel_of, body, names), out_shape=[jax....  503 us

profile of v6, /device:TPU:0, one launch (start us, length us, event | category | flops | bytes accessed | tf_op | source)
XLA Modules:
  0.0 517.8 jit_solution(3723568299074249931)
XLA Ops:
  0.7 0.1 pad.6.clone
  0.8 0.1 mul.45
  0.9 1.3 maximum_convert_fusion.refs_4_
  2.2 0.8 broadcast_select_fusion
  3.0 0.1 copy.25
  3.1 0.0 copy-start.1
  3.1 0.6 select_reduce_fusion.refs_0_
  3.7 0.3 multiply_cosine_fusion
  4.0 0.7 pad_maximum_fusion.refs_7_.refs_27_
  4.7 0.0 copy-done.1
  4.7 132.1 %forward_first.1 = (bf16[128,2048]{1,0:T(8,128)(2,1)}, bf16[128,2048]{1,0:T(8,128)(2,1)}, bf16[352,2048]{1,0:T(8,128)(2,1)}, bf16[352,2048]{1,0:T(8,128)(2,1)}, ...) custom-call(s32[8]{0:T(128)} %select_reduce_fusion.refs_0_, ...), custom_call_target="tpu_custom_call" | custom-call | flops 137438953472 | bytes 8388608 | tf_op jit(solution)/shard_map/forward_first/pallas_call | solution.py:804
  136.8 370.9 %second_layer_and_back.1 = (f32[2,128]{1,0:T(2,128)}, bf16[352,2048]{1,0:T(8,128)(2,1)}, bf16[352,2048]{1,0:T(8,128)(2,1)}, bf16[352,2048]{1,0:T(8,128)(2,1)}, b...) custom-call(s32[8]{0:T(128)} %select_reduce_fusion.refs_0_, ...), custom_call_target="tpu_custom_call" | custom-call | flops 137438953472 | bytes 8388608 | tf_op jit(solution)/shard_map/second_layer_and_back/pallas_call | solution.py:804
  507.8 0.0 copy-start
  507.8 9.1 %join_all.1 = (f32[352,2048]{1,0:T(8,128)}, f32[352,2048]{1,0:T(8,128)}, f32[352,2048]{1,0:T(8,128)}, f32[128,2048]{1,0:T(8,128)}, f32[128,2048]{1,0:T(8,128)}, ...) custom-call(bf16[352,2048]{1,0:T(8,128)(2,1)} %get-tuple-element.89., ...), custom_call_target="tpu_custom_call" | custom-call | flops 4294967296 | bytes 16777216 | tf_op jit(solution)/shard_map/join_all/pallas_call | solution.py:1561
  516.8 0.0 copy-done
  516.9 0.5 fusion
  (7 shorter events, 0.0 us)
Async XLA Ops:
  3.1 1.6 copy-start.1
  507.8 9.1 %copy-start = (f32[2,128]{1,0:T(2,128)S(1)}, f32[2,128]{1,0:T(2,128)}, u32[]{:S(2)}) copy-start(f32[2,128]{1,0:T(2,128)} %get-tuple-element.123) | copy-start | bytes 3076

commit v7 on v6

--- a/solution.py
+++ b/solution.py
@@ -997,11 +997,14 @@
         put(n.d_qkv, block, n.d_turned[n.order[block]])
 
 
+def gather_small_start(n):
+    links = n.links_small = Links(n.small_send, n.small_recv, n.site)
+    links.go(0, n.gains_mine, n.gains_x, n.site.partner)
+    links.go(1, n.kv_mine, n.kv_x, n.site.partner)
+
+
 def gather_small(n):
-    site = n.site
-    links = n.links_small = Links(n.small_send, n.small_recv, site)
-    links.go(0, n.gains_mine, n.gains_x, site.partner)
-    links.go(1, n.kv_mine, n.kv_x, site.partner)
+    site, links = n.site, n.links_small
     links.got(0, n.gains_x)
     own, came = n.gains_mine[...], n.gains_x[...]
     first = site.section == 0
@@ -1065,9 +1068,17 @@
     rows_copy = copies.pick(n.inputs.at[0], n.inputs.at[1], n.held.at[own], 0)
     top_copy = copies.pick(n.cotangent.at[0], n.cotangent.at[1], n.top_v, 0)
     turns_copy = copies.start(n.turns, n.turns_v)
+    def use_first(chip, rows):
+        normed = scaled(rows.astype(FULL), n.gains_v[:1]).astype(LOW)
+        n.normed[chip] = normed.reshape(n.normed.shape[1:])
+        n.qkv[chip] = jnp.concatenate(
+            [times_trans(normed, n.w_q[...]), times_trans(normed, n.w_kv[0])], 1
+        )
+        copies.start(n.normed.at[chip], n.rows_one.at[chip])
+
     greet(site)
     copies.wait(*small)
-    gather_small(n)
+    gather_small_start(n)
     at_query, at_out, at_gate, at_up, _ = (
         cross.send(*pair)
         for pair in (
@@ -1079,17 +1090,10 @@
         )
     )
     copies.wait(rows_copy)
-
-    def use_first(chip, rows):
-        normed = scaled(rows.astype(FULL), n.gains_v[:1]).astype(LOW)
-        n.normed[chip] = normed.reshape(n.normed.shape[1:])
-        n.qkv[chip] = jnp.concatenate(
-            [times_trans(normed, n.w_q[...]), times_trans(normed, n.w_kv[0])], 1
-        )
-        copies.start(n.normed.at[chip], n.rows_one.at[chip])
-
     spread = spread_of(n, n.held, n.spread_send, n.spread_recv, use_first)
-    for part in range(SPLIT):
+    spread.own(0)
+    gather_small(n)
+    for part in range(1, SPLIT):
         spread.own(part)
     spread.share(0)
     gather_small_keys(n)

time: 527 us -> 523 us (level)
  no operation moved by 1% of the time
where the time goes in v7:
time: 523 us; the launch traced here: 514 us
  Pallas kernels  508 us (97%)
    pallas_call x2, Pallas kernels, launch(): pl.pallas_call(functools.partial(kernel_of, body, names), out_shape=[jax....  499 us

profile of v7, /device:TPU:0, one launch (start us, length us, event | category | flops | bytes accessed | tf_op | source)
XLA Modules:
  0.0 514.2 jit_solution(4531895136954268199)
XLA Ops:
  0.7 0.1 pad.6.clone
  0.8 0.1 mul.45
  0.9 1.3 maximum_convert_fusion.refs_4_
  2.2 0.8 broadcast_select_fusion
  3.0 0.1 copy.25
  3.1 0.0 copy-start.1
  3.1 0.6 select_reduce_fusion.refs_0_
  3.7 0.3 multiply_cosine_fusion
  4.0 0.7 pad_maximum_fusion.refs_7_.refs_27_
  4.7 0.0 copy-done.1
  4.7 128.9 %forward_first.1 = (bf16[128,2048]{1,0:T(8,128)(2,1)}, bf16[128,2048]{1,0:T(8,128)(2,1)}, bf16[352,2048]{1,0:T(8,128)(2,1)}, bf16[352,2048]{1,0:T(8,128)(2,1)}, ...) custom-call(s32[8]{0:T(128)} %select_reduce_fusion.refs_0_, ...), custom_call_target="tpu_custom_call" | custom-call | flops 137438953472 | bytes 8388608 | tf_op jit(solution)/shard_map/forward_first/pallas_call | solution.py:804
  133.7 370.5 %second_layer_and_back.1 = (f32[2,128]{1,0:T(2,128)}, bf16[352,2048]{1,0:T(8,128)(2,1)}, bf16[352,2048]{1,0:T(8,128)(2,1)}, bf16[352,2048]{1,0:T(8,128)(2,1)}, b...) custom-call(s32[8]{0:T(128)} %select_reduce_fusion.refs_0_, ...), custom_call_target="tpu_custom_call" | custom-call | flops 137438953472 | bytes 8388608 | tf_op jit(solution)/shard_map/second_layer_and_back/pallas_call | solution.py:804
  504.1 0.0 copy-start
  504.1 9.1 %join_all.1 = (f32[352,2048]{1,0:T(8,128)}, f32[352,2048]{1,0:T(8,128)}, f32[352,2048]{1,0:T(8,128)}, f32[128,2048]{1,0:T(8,128)}, f32[128,2048]{1,0:T(8,128)}, ...) custom-call(bf16[352,2048]{1,0:T(8,128)(2,1)} %get-tuple-element.89., ...), custom_call_target="tpu_custom_call" | custom-call | flops 4294967296 | bytes 16777216 | tf_op jit(solution)/shard_map/join_all/pallas_call | solution.py:1565
  513.2 0.0 copy-done
  513.2 0.5 fusion
  (7 shorter events, 0.0 us)
Async XLA Ops:
  3.1 1.6 copy-start.1
  504.1 9.1 %copy-start = (f32[2,128]{1,0:T(2,128)S(1)}, f32[2,128]{1,0:T(2,128)}, u32[]{:S(2)}) copy-start(f32[2,128]{1,0:T(2,128)} %get-tuple-element.123) | copy-start | bytes 3076

commit v8 on v7

--- a/solution.py
+++ b/solution.py
@@ -1534,12 +1534,6 @@
                     pltpu.make_async_copy(second, target, sem),
                 )
             )
-    for copy in row_waits:
-        copy.wait()
-    for index, out in enumerate(row_outs):
-        copy = pltpu.make_async_copy(row_at.at[index], out, row_sem.at[index])
-        copy.start()
-        done.append(copy)
     for index in range(count):
         waits[2 * index].wait()
         waits[2 * index + 1].wait()
@@ -1549,9 +1543,15 @@
         else:
             parts = [(sums[index].at[pl.ds(k, 1)], outs[index + k]) for k in range(2)]
         for source, target in parts:
-            copy = pltpu.make_async_copy(source, target, out_sem.at[len(done) - 2])
+            copy = pltpu.make_async_copy(source, target, out_sem.at[len(done)])
             copy.start()
             done.append(copy)
+    for copy in row_waits:
+        copy.wait()
+    for index, out in enumerate(row_outs):
+        copy = pltpu.make_async_copy(row_at.at[index], out, row_sem.at[index])
+        copy.start()
+        done.append(copy)
     for copy in done:
         copy.wait()
 

time: 523 us -> 523 us (level)
  no operation moved by 1% of the time
where the time goes in v8:
time: 523 us; the launch traced here: 514 us
  Pallas kernels  508 us (97%)
    pallas_call x2, Pallas kernels, launch(): pl.pallas_call(functools.partial(kernel_of, body, names), out_shape=[jax....  499 us

profile of v8, /device:TPU:0, one launch (start us, length us, event | category | flops | bytes accessed | tf_op | source)
XLA Modules:
  0.0 514.1 jit_solution(15908406966630508507)
XLA Ops:
  0.7 0.1 pad.6.clone
  0.8 0.1 mul.45
  0.9 1.3 maximum_convert_fusion.refs_4_
  2.2 0.8 broadcast_select_fusion
  3.0 0.1 copy.25
  3.1 0.0 copy-start.1
  3.1 0.6 select_reduce_fusion.refs_0_
  3.7 0.3 multiply_cosine_fusion
  4.0 0.7 pad_maximum_fusion.refs_7_.refs_27_
  4.7 0.0 copy-done.1
  4.7 128.9 %forward_first.1 = (bf16[128,2048]{1,0:T(8,128)(2,1)}, bf16[128,2048]{1,0:T(8,128)(2,1)}, bf16[352,2048]{1,0:T(8,128)(2,1)}, bf16[352,2048]{1,0:T(8,128)(2,1)}, ...) custom-call(s32[8]{0:T(128)} %select_reduce_fusion.refs_0_, ...), custom_call_target="tpu_custom_call" | custom-call | flops 137438953472 | bytes 8388608 | tf_op jit(solution)/shard_map/forward_first/pallas_call | solution.py:804
  133.7 370.5 %second_layer_and_back.1 = (f32[2,128]{1,0:T(2,128)}, bf16[352,2048]{1,0:T(8,128)(2,1)}, bf16[352,2048]{1,0:T(8,128)(2,1)}, bf16[352,2048]{1,0:T(8,128)(2,1)}, b...) custom-call(s32[8]{0:T(128)} %select_reduce_fusion.refs_0_, ...), custom_call_target="tpu_custom_call" | custom-call | flops 137438953472 | bytes 8388608 | tf_op jit(solution)/shard_map/second_layer_and_back/pallas_call | solution.py:804
  504.1 0.0 copy-start
  504.1 9.0 %join_all.1 = (f32[352,2048]{1,0:T(8,128)}, f32[352,2048]{1,0:T(8,128)}, f32[352,2048]{1,0:T(8,128)}, f32[128,2048]{1,0:T(8,128)}, f32[128,2048]{1,0:T(8,128)}, ...) custom-call(bf16[352,2048]{1,0:T(8,128)(2,1)} %get-tuple-element.89., ...), custom_call_target="tpu_custom_call" | custom-call | flops 4294967296 | bytes 16777216 | tf_op jit(solution)/shard_map/join_all/pallas_call | solution.py:1565
  513.1 0.0 copy-done
  513.1 0.5 fusion
  (7 shorter events, 0.0 us)
Async XLA Ops:
  3.1 1.6 copy-start.1
  504.1 9.0 %copy-start = (f32[2,128]{1,0:T(2,128)S(1)}, f32[2,128]{1,0:T(2,128)}, u32[]{:S(2)}) copy-start(f32[2,128]{1,0:T(2,128)} %get-tuple-element.123) | copy-start | bytes 3076
